TPU v7x, 256 devices: a whole 4x4x8 slice. The times are simulated.
256 devices in a mesh: row: 16 (over y, z_lo), col: 16 (over x, z_hi, core).
Axes of the slice: x: 4, y: 4, z: 8 (z_hi: 2, z_lo: 4; z = z_hi * 4 + z_lo), core: 2. Of those that a mesh axis runs over, the one named last changes fastest.
Arguments:
- right_side: float32 [64, 32768], P(None, ('row', 'col')), may hold values from -40 to 40
- points: float32 [2, 32768], P(None, ('row', 'col')), may hold values from 0 to 1
- star_noise: float32 [32768], P(('row', 'col')), may hold values from 0.5 to 2
Outputs:
- solution_field: float32 [64, 32768], P(None, ('row', 'col'))
- residual: float32 [64, 32768], P(None, ('row', 'col'))
All inputs are finite; a program needn't handle non-finite values.
Results may differ from a plain program's by a relative error of at most 0.0003.
Values sent between devices are 32-bit elements; how exact they have to be, the bound alone decides.
No kernel may reach another device: no remote copies, remote signals or barrier semaphores. Data moves between devices by JAX's collectives and lax.ppermute only.
A program may use at most 64 MiB of HBM per device.

v0:
```python
import jax
import jax.numpy as jnp
from jax import lax
from jax.sharding import PartitionSpec as P

ITERS = 3


QUAD_XX = 1.6
QUAD_XY = 0.5
QUAD_YY = 0.7
INVERSE_SQUARE = 25.0
KERNEL_WEIGHT = 2048.0


def kernel_block(row_points, column_points, amplitude):
    delta_x = row_points[0][:, None] - column_points[0][None, :]
    delta_y = row_points[1][:, None] - column_points[1][None, :]
    quadratic = (
        QUAD_XX * delta_x * delta_x
        + 2.0 * QUAD_XY * delta_x * delta_y
        + QUAD_YY * delta_y * delta_y
    ) * INVERSE_SQUARE
    return amplitude * jnp.exp(-jnp.sqrt(quadratic))


def contract(vectors, kernel_tile):
    return lax.dot_general(
        vectors,
        kernel_tile,
        (((1,), (1,)), ((), ())),
        precision=lax.Precision.HIGHEST,
        preferred_element_type=jnp.float32,
    )


def squares(vectors):
    return lax.psum(jnp.sum(vectors * vectors, axis=1, keepdims=True), ("row", "col"))


def on_device(right_side, points, star_noise):
    star_count = points.shape[1]
    amplitude = KERNEL_WEIGHT / (lax.axis_size("row") * lax.axis_size("col") * star_count)
    row_points = lax.all_gather(points, "col", axis=1, tiled=True)
    column_points = lax.all_gather(points, "row", axis=1, tiled=True)
    solution_field = jnp.zeros_like(right_side)
    residual = right_side
    direction = right_side
    norm_now = squares(residual)
    for iteration in range(ITERS):
        partial_rows = contract(
            lax.all_gather(direction, "row", axis=1, tiled=True),
            kernel_block(row_points, column_points, amplitude),
        )
        total = lax.psum_scatter(partial_rows, "col", scatter_dimension=1, tiled=True)
        applied = total + star_noise[None, :] * direction
        curve = lax.psum(jnp.sum(direction * applied, axis=1, keepdims=True), ("row", "col"))
        step_size = norm_now / curve
        solution_field = solution_field + step_size * direction
        residual = residual - step_size * applied
        norm_next = squares(residual)
        direction = residual + norm_next / norm_now * direction
        norm_now = norm_next
    return (solution_field, residual)


def solution(mesh):
    placed = (P(None, ("row", "col")), P(None, ("row", "col")), P(("row", "col")))
    return jax.shard_map(
        on_device,
        mesh=mesh,
        in_specs=placed,
        out_specs=(P(None, ("row", "col")), P(None, ("row", "col"))),
        check_vma=False,
    )
```

profile of v0, /device:TPU:1, one launch (start us, length us, event | category | flops | bytes accessed | tf_op | source)
XLA Modules:
  0.0 893.9 jit_solution(10237760668716771405)
XLA Ops:
  7.2 37.7 %all_gather.16 = f32[2,2048]{1,0:T(2,128)S(1)} all-gather(f32[2,128]{1,0:T(2,128)} %param.4), channel_id=1, replica_groups=mesh['row'=16,'col'=16] {'row'}, dimensions={1}, use_global_device_ids=true | all-gather | bytes 17408 | tf_op jit(solution)/shard_map/all_gather | solution.py:45
  44.9 38.4 %all_gather.15 = f32[2,2048]{1,0:T(2,128)S(1)} all-gather(f32[2,128]{1,0:T(2,128)} %param.4), channel_id=1, replica_groups=mesh['row'=16,'col'=16] {'col'}, dimensions={1}, use_global_device_ids=true | all-gather | bytes 17408 | tf_op jit(solution)/shard_map/all_gather | solution.py:44
  83.3 35.7 %all_gather.17 = f32[64,2048]{1,0:T(8,128)S(1)} all-gather(f32[64,128]{1,0:T(8,128)} %param.3), channel_id=1, replica_groups=mesh['row'=16,'col'=16] {'row'}, dimensions={1}, use_global_device_ids=true | all-gather | bytes 557056 | tf_op jit(solution)/shard_map/all_gather | solution.py:52
  119.0 29.5 %fusion.12 = f32[64,2048]{1,0:T(8,128)} fusion(f32[64,2048]{1,0:T(8,128)S(1)} %all_gather.17, f32[2048]{0:T(1024)S(1)} %bitcast.28, f32[2048]{0:T(1024)S(1)} %bitcast.34, f32[2048]{0:T(1024)S(1)} %bitcast.25, f32[2048]{0:T(1024)S(1)} %bitcast.31), kind=kOutput, calls=%fused_computation.14 | convolution fusion | flops 3267362816 | bytes 1081344 | tf_op jit(solution)/shard_map/dot_general | solution.py:28
  148.6 73.1 %reduce-scatter.4.cloned.1.call-done = f32[64,128]{1,0:T(8,128)} async-done(((f32[64,2048]{1,0:T(8,128)}), f32[64,128]{1,0:T(8,128)}) %reduce-scatter.4.cloned.1.call-update) | async-done | bytes 32784 | tf_op jit(solution)/shard_map/reduce_scatter | solution.py:55
  221.7 0.9 multiply_reduce_fusion.4
  222.5 75.8 %all-reduce = (f32[64,1]{0,1:T(1,128)S(1)}, f32[64,1]{0,1:T(1,128)S(1)}) all-reduce(f32[64,1]{0,1:T(1,128)S(1)} %bitcast.38, f32[64,1]{0,1:T(1,128)S(1)} %bitcast.37), channel_id=1, replica_groups=mesh['row'=16,'col'=16] {'row','col'}, use_global_device_ids=true, to_apply=%region_1.0 | all-reduce | flops 128 | bytes 1024 | tf_op jit(solution)/shard_map/psum | solution.py:38
  298.3 0.9 multiply_reduce_fusion.3
  299.3 73.8 %psum.44 = f32[64,1]{0,1:T(1,128)S(1)} all-reduce(f32[64,1]{0,1:T(1,128)S(1)} %bitcast.39), channel_id=1, replica_groups=mesh['row'=16,'col'=16] {'row','col'}, use_global_device_ids=true, to_apply=%region_6.0 | all-reduce | flops 64 | bytes 512 | tf_op jit(solution)/shard_map/psum | solution.py:38
  373.0 0.8 multiply_add_fusion.4
  373.9 37.4 %all_gather.18 = f32[64,2048]{1,0:T(8,128)S(1)} all-gather(f32[64,128]{1,0:T(8,128)S(1)} %multiply_add_fusion.4), channel_id=1, replica_groups=mesh['row'=16,'col'=16] {'row'}, dimensions={1}, use_global_device_ids=true | all-gather | bytes 557056 | tf_op jit(solution)/shard_map/all_gather | solution.py:52
  411.3 27.8 %fusion.8 = f32[64,2048]{1,0:T(8,128)} fusion(f32[64,2048]{1,0:T(8,128)S(1)} %all_gather.18, f32[2048]{0:T(1024)S(1)} %bitcast.29, f32[2048]{0:T(1024)S(1)} %bitcast.35, f32[2048]{0:T(1024)S(1)} %bitcast.26, f32[2048]{0:T(1024)S(1)} %bitcast.32), kind=kOutput, calls=%fused_computation.12 | convolution fusion | flops 3267362816 | bytes 1081344 | tf_op jit(solution)/shard_map/dot_general | solution.py:28
  439.2 76.6 %reduce-scatter.6.cloned.1.call-done = f32[64,128]{1,0:T(8,128)} async-done(((f32[64,2048]{1,0:T(8,128)}), f32[64,128]{1,0:T(8,128)}) %reduce-scatter.6.cloned.1.call-update) | async-done | bytes 32784 | tf_op jit(solution)/shard_map/reduce_scatter | solution.py:55
  515.8 0.9 multiply_reduce_fusion.2
  516.6 75.8 %psum.45 = f32[64,1]{0,1:T(1,128)S(1)} all-reduce(f32[64,1]{0,1:T(1,128)S(1)} %bitcast.40), channel_id=1, replica_groups=mesh['row'=16,'col'=16] {'row','col'}, use_global_device_ids=true, to_apply=%region_9.0 | all-reduce | flops 64 | bytes 512 | tf_op jit(solution)/shard_map/psum | solution.py:57
  592.5 0.9 multiply_reduce_fusion.1
  593.4 73.8 %psum.46 = f32[64,1]{0,1:T(1,128)S(1)} all-reduce(f32[64,1]{0,1:T(1,128)S(1)} %bitcast.42), channel_id=1, replica_groups=mesh['row'=16,'col'=16] {'row','col'}, use_global_device_ids=true, to_apply=%region_11.0 | all-reduce | flops 64 | bytes 512 | tf_op jit(solution)/shard_map/psum | solution.py:38
  667.2 0.1 multiply_add_fusion.2
  667.3 37.4 %all_gather.19 = f32[64,2048]{1,0:T(8,128)S(1)} all-gather(f32[64,128]{1,0:T(8,128)S(1)} %multiply_add_fusion.2), channel_id=1, replica_groups=mesh['row'=16,'col'=16] {'row'}, dimensions={1}, use_global_device_ids=true | all-gather | bytes 557056 | tf_op jit(solution)/shard_map/all_gather | solution.py:52
  704.7 27.8 %fusion.6 = f32[64,2048]{1,0:T(8,128)} fusion(f32[64,2048]{1,0:T(8,128)S(1)} %all_gather.19, f32[2048]{0:T(1024)S(1)} %bitcast.30, f32[2048]{0:T(1024)S(1)} %bitcast.36, f32[2048]{0:T(1024)S(1)} %bitcast.27, f32[2048]{0:T(1024)S(1)} %bitcast.33), kind=kOutput, calls=%fused_computation.11 | convolution fusion | flops 3267362816 | bytes 1081344 | tf_op jit(solution)/shard_map/dot_general | solution.py:28
  732.5 76.7 %reduce-scatter.8.cloned.1.call-done = f32[64,128]{1,0:T(8,128)} async-done(((f32[64,2048]{1,0:T(8,128)}), f32[64,128]{1,0:T(8,128)}) %reduce-scatter.8.cloned.1.call-update) | async-done | bytes 32784 | tf_op jit(solution)/shard_map/reduce_scatter | solution.py:55
  809.2 0.9 multiply_reduce_fusion
  810.0 75.8 %psum.47 = f32[64,1]{0,1:T(1,128)S(1)} all-reduce(f32[64,1]{0,1:T(1,128)S(1)} %bitcast.41), channel_id=1, replica_groups=mesh['row'=16,'col'=16] {'row','col'}, use_global_device_ids=true, to_apply=%region_14.0 | all-reduce | flops 64 | bytes 512 | tf_op jit(solution)/shard_map/psum | solution.py:57
  885.8 1.5 multiply_subtract_fusion
  (19 shorter events, 0.2 us)
Async XLA Ops:
  7.2 214.5 %reduce-scatter.4.cloned.1.call-start = ((), (), s32[]{:S(2)}) async-start(), calls=%async_computation.3 | async-start | bytes 557056 | tf_op jit(solution)/shard_map/reduce_scatter | solution.py:55
  148.5 73.2 %copy-start = (f32[64,128]{1,0:T(8,128)S(1)}, f32[64,128]{1,0:T(8,128)}, u32[]{:S(2)}) copy-start(f32[64,128]{1,0:T(8,128)} %param.3) | copy-start | bytes 98308
  148.5 73.2 %copy-start.2 = (f32[128]{0:T(128)S(1)}, f32[128]{0:T(128)}, u32[]{:S(2)}) copy-start(f32[128]{0:T(128)} %param.5) | copy-start | bytes 1540
  148.5 367.3 %reduce-scatter.6.cloned.1.call-start = ((), (), s32[]{:S(2)}) async-start(), calls=%async_computation.4 | async-start | bytes 557056 | tf_op jit(solution)/shard_map/reduce_scatter | solution.py:55
  439.1 153.4 %copy-start.1 = (f32[64,128]{1,0:T(8,128)S(1)}, f32[64,128]{1,0:T(8,128)}, u32[]{:S(2)}) copy-start(f32[64,128]{1,0:T(8,128)} %reduce-scatter.4.cloned.1.call-done) | copy-start | bytes 98308
  439.1 370.1 %reduce-scatter.8.cloned.1.call-start = ((), (), s32[]{:S(2)}) async-start(), calls=%async_computation.5 | async-start | bytes 557056 | tf_op jit(solution)/shard_map/reduce_scatter | solution.py:55
Sparse Core Ops, SparseCore 0:
  148.6 72.9 reduce-scatter.3
  439.2 76.4 reduce-scatter.5
  732.6 76.5 reduce-scatter.7
where the time goes:
time: 895 us; the launch traced here: 894 us
  blocking collectives  561 us (63%)
  waiting for transfers between devices  226 us (25%)
  matrix products  85.1 us (10%)
  between operations  13.8 us (2%)
    reduce_scatter x3, waiting for transfers between devices, on_device(): lax.psum_scatter(partial_rows, 'col', scatter_dimension=1, tiled=True)  226 us
    psum x3, blocking collectives, squares(): lax.psum(jnp.sum(vectors * vectors, axis=1, keepdims=True), ('row', 'col'))  223 us
    psum x2, blocking collectives, on_device(): lax.psum(jnp.sum(direction * applied, axis=1, keepdims=True), ('row', 'co...  152 us
    all_gather x3, blocking collectives, on_device(): lax.all_gather(direction, 'row', axis=1, tiled=True)  110 us
    dot_general x3, matrix products, contract(): lax.dot_general(vectors, kernel_tile, (((1,), (1,)), ((), ())), precision...  85.1 us
    all_gather x1, blocking collectives, on_device(): row_points = lax.all_gather(points, 'col', axis=1, tiled=True)  38.4 us
    all_gather x1, blocking collectives, on_device(): column_points = lax.all_gather(points, 'row', axis=1, tiled=True)  37.7 us
  transfers between devices with their start and end apart: 3, of which 3 were waited for; matrix products, arithmetic and copies ran while one was open for 0% of the time, Pallas kernels for 0%

commit v1 on v0

v1 whole, which is shorter than its diff:
```python
import functools
import math

import jax
import jax.numpy as jnp
from jax import lax
from jax.experimental import pallas as pl
from jax.experimental.pallas import tpu as pltpu
from jax.sharding import PartitionSpec as P

QUAD_XX = 1.6
QUAD_XY = 0.5
QUAD_YY = 0.7
INVERSE_SQUARE = 25.0
KERNEL_WEIGHT = 2048.0

PX = math.sqrt(QUAD_XX * INVERSE_SQUARE)
PY = QUAD_XY * INVERSE_SQUARE / PX
QY = math.sqrt(QUAD_YY * INVERSE_SQUARE - PY * PY)

AXES = ("row", "col")
LANES = 128
SPARE = 8
TILE = 256
VMEM_LIMIT = 24 * 1024 * 1024

ROUNDS_A = (("z", (3, 2, 1)), ("y", (2, 1, 3)))
ROUNDS_B = (("z", (7,)), ("x", (2, 1, 3)), ("core", (1,)))


def place(index):
    row, col = divmod(index, 16)
    y, z_lo = divmod(row, 4)
    x, rest = divmod(col, 4)
    z_hi, core = divmod(rest, 2)
    return {"x": x, "y": y, "z": z_hi * 4 + z_lo, "core": core}


def number(at):
    row = at["y"] * 4 + at["z"] % 4
    return row * 16 + at["x"] * 4 + (at["z"] // 4) * 2 + at["core"]


def exchange(value, axis, mask):
    pairs = []
    for index in range(256):
        at = place(index)
        at[axis] ^= mask
        pairs.append((index, number(at)))
    return lax.ppermute(value, AXES, pairs)


def gather(block, rounds):
    for axis, masks in rounds:
        block = jnp.concatenate([block] + [exchange(block, axis, m) for m in masks], axis=0)
    return block


def scatter_sum(blocks, rounds):
    for axis, masks in reversed(rounds):
        rows = blocks.shape[0] // (len(masks) + 1)
        total = blocks[:rows]
        for i, m in enumerate(masks):
            total = total + exchange(blocks[(i + 1) * rows : (i + 2) * rows], axis, m)
        blocks = total
    return blocks


def all_sum(block):
    for axis, masks in ROUNDS_B + ROUNDS_A:
        block = block + sum(exchange(block, axis, m) for m in masks)
    return block


def split(vectors):
    high = vectors.astype(jnp.bfloat16)
    low = (vectors - high.astype(jnp.float32)).astype(jnp.bfloat16)
    return high, low


def unpack(v_ref, pair_ref, dots_ref, rhs):
    total = jnp.zeros((SPARE, LANES), jnp.float32)
    step = rhs + SPARE
    for b in range(v_ref.shape[0] // step):
        high, low = split(v_ref[b * step : b * step + rhs, :])
        pair_ref[:rhs, b * LANES : (b + 1) * LANES] = high
        pair_ref[rhs:, b * LANES : (b + 1) * LANES] = low
        total = total + v_ref[b * step + rhs : (b + 1) * step, :]
    dots_ref[...] = total


def emit(out_ref, product, dots, rhs, amplitude):
    step = rhs + SPARE
    for piece in range(product.shape[1] // LANES):
        out_ref[piece * step : piece * step + rhs, :] = (
            product[:, piece * LANES : (piece + 1) * LANES] * amplitude
        )
        out_ref[piece * step + rhs : (piece + 1) * step, :] = dots


def first_kernel(rhs, amplitude, v_ref, rows_ref, out_ref, high_ref, low_ref, pair_ref, dots_ref, points_ref):
    step = rhs + SPARE
    stars = high_ref.shape[1]

    @pl.when(pl.program_id(0) == 0)
    def _():
        unpack(v_ref, pair_ref, dots_ref, rhs)
        for b in range(stars // LANES):
            tile = v_ref[b * step + rhs : (b + 1) * step, :]
            square = jnp.concatenate([tile, jnp.zeros((LANES - SPARE, LANES), jnp.float32)], axis=0)
            points_ref[b * LANES : (b + 1) * LANES, :] = square.T

    row_x = jnp.concatenate([rows_ref[0:1, :], rows_ref[SPARE : SPARE + 1, :]], axis=1)
    row_y = jnp.concatenate([rows_ref[1:2, :], rows_ref[SPARE + 1 : SPARE + 2, :]], axis=1)
    row_p = PX * row_x + PY * row_y
    row_q = QY * row_y
    product = jnp.zeros((rhs, TILE), jnp.float32)
    for j in range(0, stars, TILE):
        x = points_ref[j : j + TILE, 0:1]
        y = points_ref[j : j + TILE, 1:2]
        delta_p = (PX * x + PY * y) - row_p
        delta_q = QY * y - row_q
        square = delta_p * delta_p + delta_q * delta_q
        distance = square * lax.rsqrt(jnp.maximum(square, 1e-30))
        high, low = split(jnp.exp(-distance))
        high_ref[0, j : j + TILE, :] = high
        low_ref[0, j : j + TILE, :] = low
        both = jnp.dot(pair_ref[:, j : j + TILE], high, preferred_element_type=jnp.float32)
        rest = jnp.dot(pair_ref[:rhs, j : j + TILE], low, preferred_element_type=jnp.float32)
        product = product + (both[:rhs] + (both[rhs:] + rest))
    emit(out_ref, product, dots_ref[...], rhs, amplitude)


def next_kernel(rhs, amplitude, v_ref, high_ref, low_ref, out_ref, pair_ref, dots_ref):
    @pl.when(pl.program_id(0) == 0)
    def _():
        unpack(v_ref, pair_ref, dots_ref, rhs)

    both = jnp.dot(pair_ref[...], high_ref[0], preferred_element_type=jnp.float32)
    rest = jnp.dot(pair_ref[:rhs, :], low_ref[0], preferred_element_type=jnp.float32)
    emit(out_ref, both[:rhs] + (both[rhs:] + rest), dots_ref[...], rhs, amplitude)


def first_product(gathered, row_points, rhs, amplitude):
    blocks = gathered.shape[0] // (rhs + SPARE)
    stars = blocks * LANES
    tiles = row_points.shape[0] // SPARE * LANES // TILE
    per = TILE // LANES
    return pl.pallas_call(
        functools.partial(first_kernel, rhs, amplitude),
        grid=(tiles,),
        in_specs=[
            pl.BlockSpec(gathered.shape, lambda i: (0, 0)),
            pl.BlockSpec((per * SPARE, LANES), lambda i: (i, 0)),
        ],
        out_specs=[
            pl.BlockSpec((per * (rhs + SPARE), LANES), lambda i: (i, 0)),
            pl.BlockSpec((1, stars, TILE), lambda i: (i, 0, 0)),
            pl.BlockSpec((1, stars, TILE), lambda i: (i, 0, 0)),
        ],
        out_shape=[
            jax.ShapeDtypeStruct((tiles * per * (rhs + SPARE), LANES), jnp.float32),
            jax.ShapeDtypeStruct((tiles, stars, TILE), jnp.bfloat16),
            jax.ShapeDtypeStruct((tiles, stars, TILE), jnp.bfloat16),
        ],
        scratch_shapes=[
            pltpu.VMEM((2 * rhs, stars), jnp.bfloat16),
            pltpu.VMEM((SPARE, LANES), jnp.float32),
            pltpu.VMEM((stars, LANES), jnp.float32),
        ],
        compiler_params=pltpu.CompilerParams(vmem_limit_bytes=VMEM_LIMIT),
    )(gathered, row_points)


def next_product(gathered, high, low, rhs, amplitude):
    tiles, stars, _ = high.shape
    per = TILE // LANES
    return pl.pallas_call(
        functools.partial(next_kernel, rhs, amplitude),
        grid=(tiles,),
        in_specs=[
            pl.BlockSpec(gathered.shape, lambda i: (0, 0)),
            pl.BlockSpec((1, stars, TILE), lambda i: (i, 0, 0)),
            pl.BlockSpec((1, stars, TILE), lambda i: (i, 0, 0)),
        ],
        out_specs=pl.BlockSpec((per * (rhs + SPARE), LANES), lambda i: (i, 0)),
        out_shape=jax.ShapeDtypeStruct((tiles * per * (rhs + SPARE), LANES), jnp.float32),
        scratch_shapes=[
            pltpu.VMEM((2 * rhs, stars), jnp.bfloat16),
            pltpu.VMEM((SPARE, LANES), jnp.float32),
        ],
        compiler_params=pltpu.CompilerParams(vmem_limit_bytes=VMEM_LIMIT),
    )(gathered, high, low)


def dot(a, b):
    return jnp.sum(a * b, axis=1, keepdims=True)


def to_rows(columns, rhs):
    lane = lax.broadcasted_iota(jnp.int32, (rhs, LANES), 1)
    tile = jnp.zeros((rhs, LANES), jnp.float32)
    for i, column in enumerate(columns):
        tile = jnp.where(lane == i, column, tile)
    square = jnp.concatenate([tile, jnp.zeros((LANES - rhs, LANES), jnp.float32)], axis=0)
    return square.T[:SPARE, :]


def to_columns(tile, count, rhs):
    square = jnp.concatenate([tile, jnp.zeros((LANES - SPARE, LANES), jnp.float32)], axis=0).T
    return [square[:rhs, i : i + 1] for i in range(count)]


def update_one(rhs, sums_ref, right_ref, noise_ref, out_ref):
    right = right_ref[...]
    image = sums_ref[:rhs, :] + noise_ref[...] * right
    out_ref[:rhs, :] = image
    out_ref[rhs:, :] = to_rows([dot(right, right), dot(right, image)], rhs)


def update_two(rhs, sums_ref, right_ref, first_ref, noise_ref, out_ref, second_ref, scalars_ref):
    right = right_ref[...]
    w0 = first_ref[:rhs, :]
    n0 = sums_ref[:rhs, :] + noise_ref[...] * w0
    norm, curve = to_columns(sums_ref[rhs:, :], 2, rhs)
    alpha = norm / curve
    r1 = right - alpha * w0
    w1 = w0 - alpha * n0
    out_ref[:rhs, :] = w1
    out_ref[rhs:, :] = to_rows([dot(r1, r1), dot(r1, w1)], rhs)
    second_ref[...] = n0
    scalars_ref[...] = sums_ref[rhs:, :]


def update_three(rhs, sums_ref, right_ref, first_ref, second_ref, third_ref, scalars_ref, noise_ref, dots_ref, carry_ref):
    right = right_ref[...]
    w0 = first_ref[:rhs, :]
    n0 = second_ref[...]
    w1 = third_ref[:rhs, :]
    n1 = sums_ref[:rhs, :] + noise_ref[...] * w1
    norm0, curve0 = to_columns(scalars_ref[...], 2, rhs)
    norm1, curve1 = to_columns(sums_ref[rhs:, :], 2, rhs)
    alpha0 = norm0 / curve0
    beta1 = norm1 / norm0
    alpha1 = norm1 / (curve1 - beta1 * norm1 / alpha0)
    r1 = right - alpha0 * w0
    s1 = w1 + beta1 * w0
    p1 = r1 + beta1 * right
    z1 = n1 + beta1 * n0
    r2 = r1 - alpha1 * s1
    w2 = w1 - alpha1 * z1
    dots_ref[...] = to_rows([dot(r2, r2), dot(r2, w2)], rhs)
    lane = lax.broadcasted_iota(jnp.int32, (rhs, LANES), 1)
    carry_ref[0] = alpha0 * right + alpha1 * p1
    carry_ref[1] = r2
    carry_ref[2] = p1
    carry_ref[3] = s1
    carry_ref[4] = w2
    carry_ref[5] = jnp.where(lane == 0, alpha1, norm1)


def update_four(rhs, dots_ref, carry_ref, solution_ref, residual_ref):
    norm2, curve2 = to_columns(dots_ref[...], 2, rhs)
    alpha1 = carry_ref[5, :, 0:1]
    norm1 = carry_ref[5, :, 1:2]
    r2 = carry_ref[1]
    beta2 = norm2 / norm1
    alpha2 = norm2 / (curve2 - beta2 * norm2 / alpha1)
    solution_ref[...] = carry_ref[0] + alpha2 * (r2 + beta2 * carry_ref[2])
    residual_ref[...] = r2 - alpha2 * (carry_ref[4] + beta2 * carry_ref[3])


def small(body, rhs, shapes, *operands):
    outs = [jax.ShapeDtypeStruct(s, jnp.float32) for s in shapes]
    return pl.pallas_call(
        functools.partial(body, rhs),
        out_shape=outs,
        compiler_params=pltpu.CompilerParams(vmem_limit_bytes=VMEM_LIMIT),
    )(*operands)


def on_device(total_stars, right_side, points, star_noise):
    rhs, own = right_side.shape
    amplitude = KERNEL_WEIGHT / total_stars
    noise = star_noise[None, :]
    vector, augmented, spare = (rhs, own), (rhs + SPARE, own), (SPARE, own)
    places = jnp.concatenate([points, jnp.zeros((SPARE - 2, own), jnp.float32)], axis=0)

    row_points = gather(places, ROUNDS_B)
    gathered = gather(jnp.concatenate([right_side, places], axis=0), ROUNDS_A)
    pieces, high, low = first_product(gathered, row_points, rhs, amplitude)
    sums = scatter_sum(pieces, ROUNDS_B)
    (first,) = small(update_one, rhs, [augmented], sums, right_side, noise)

    pieces = next_product(gather(first, ROUNDS_A), high, low, rhs, amplitude)
    sums = scatter_sum(pieces, ROUNDS_B)
    third, second, scalars = small(
        update_two, rhs, [augmented, vector, spare], sums, right_side, first, noise
    )

    pieces = next_product(gather(third, ROUNDS_A), high, low, rhs, amplitude)
    sums = scatter_sum(pieces, ROUNDS_B)
    dots, carry = small(
        update_three,
        rhs,
        [spare, (6, rhs, own)],
        sums,
        right_side,
        first,
        second,
        third,
        scalars,
        noise,
    )
    return tuple(small(update_four, rhs, [vector, vector], all_sum(dots), carry))


def solution(mesh):
    placed = (P(None, AXES), P(None, AXES), P(AXES))

    def whole(right_side, points, star_noise):
        return jax.shard_map(
            functools.partial(on_device, right_side.shape[1]),
            mesh=mesh,
            in_specs=placed,
            out_specs=(P(None, AXES), P(None, AXES)),
            check_vma=False,
        )(right_side, points, star_noise)

    return whole
```

time: 895 us -> 171 us (0.19)
  blocking collectives: 561 us -> 0 us
  waiting for transfers between devices: 226 us -> 49.4 us
  matrix products: 85.1 us -> 0 us
  starting transfers between devices: 0.12 us -> 85.2 us
  Pallas kernels: 0 us -> 25.2 us
  between operations: 13.8 us -> 0.91 us
    psum x5 -> x0, blocking collectives: 375 us -> none  [the longest x3 223 us: squares(): lax.psum(jnp.sum(vectors * vectors, axis=1, keepdims=True), ('row', 'col'))]
    reduce_scatter x3 -> x0, waiting for transfers between devices: 226 us -> none  [on_device(): lax.psum_scatter(partial_rows, 'col', scatter_dimension=1, tiled=True)]
    all_gather x5 -> x0, blocking collectives: 186 us -> none  [the longest x3 110 us: on_device(): lax.all_gather(direction, 'row', axis=1, tiled=True)]
    ppermute x0 -> x49, starting transfers between devices: none -> 85.2 us  [exchange(): return lax.ppermute(value, AXES, pairs)]
    dot_general x3 -> x0, matrix products: 85.1 us -> none  [contract(): lax.dot_general(vectors, kernel_tile, (((1,), (1,)), ((), ())), precision...]
    ppermute x0 -> x49, waiting for transfers between devices: none -> 49.4 us  [exchange(): return lax.ppermute(value, AXES, pairs)]
    pallas_call x0 -> x7, Pallas kernels: none -> 25.2 us  [the longest x1 15.5 us: first_product(): pl.pallas_call(functools.partial(first_kernel, rhs, amplitude), grid=(til...]
  transfers between devices with their start and end apart: 3 -> 49, of which waited for: 3 -> 36; matrix products, arithmetic and copies ran while one was open for 0% -> 3% of each run, Pallas kernels for 0% -> 0%
where the time goes in v1:
time: 171 us; the launch traced here: 169 us
  starting transfers between devices  85.2 us (50%)
  waiting for transfers between devices  49.4 us (29%)
  Pallas kernels  25.2 us (15%)
  local copies, waits for them, and re-layouts  6.69 us (4%)
  other arithmetic  1.72 us (1%)
    ppermute x49, starting transfers between devices, exchange(): return lax.ppermute(value, AXES, pairs)  85.2 us
    ppermute x49, waiting for transfers between devices, exchange(): return lax.ppermute(value, AXES, pairs)  49.4 us
    pallas_call x1, Pallas kernels, first_product(): pl.pallas_call(functools.partial(first_kernel, rhs, amplitude), grid=(til...  15.5 us
    pallas_call x2, Pallas kernels, next_product(): pl.pallas_call(functools.partial(next_kernel, rhs, amplitude), grid=(tile...  7.7 us
    concatenate x7, local copies, waits for them, and re-layouts, gather(): jnp.concatenate([block] + [exchange(block, axis, m) for m in masks], axis=0)  4.38 us
  transfers between devices with their start and end apart: 49, of which 36 were waited for; matrix products, arithmetic and copies ran while one was open for 3% of the time, Pallas kernels for 0%

profile of v1, /device:TPU:1, one launch (start us, length us, event | category | flops | bytes accessed | tf_op | source)
XLA Modules:
  0.0 169.2 jit_solution(18250424675545035132)
XLA Ops:
  1.4 5.2 %collective-permute-start = (f32[72,128]{1,0:T(8,128)S(1)}, f32[72,128]{1,0:T(8,128)S(1)}, u32[]{:S(2)}, u32[]{:S(2)}) collective-permute-start(f32[72,128]{1,0:T(8,128)S(1)} %pad_maximum_fusion.1), channel_id=1, source_target_pairs={{0,48},{1,49},{2,50},{3,51},{4,52},{5,53},{6,54},{7,55},{8,56},{9,... | collective-permute-start | bytes 110600 | tf_op jit(solution)/shard_map/ppermute | solution.py:50
  7.7 4.4 %collective-permute-start.6 = (f32[8,128]{1,0:T(8,128)S(1)}, f32[8,128]{1,0:T(8,128)S(1)}, u32[]{:S(2)}, u32[]{:S(2)}) collective-permute-start(f32[8,128]{1,0:T(8,128)S(1)} %concatenate.44), channel_id=1, source_target_pairs={{0,50},{1,51},{2,48},{3,49},{4,54},{5,55},{6,52},{7,53},{8,58},{9,... | collective-permute-start | bytes 12296 | tf_op jit(solution)/shard_map/ppermute | solution.py:50
  13.5 3.0 %collective-permute-start.3 = (f32[288,128]{1,0:T(8,128)S(1)}, f32[288,128]{1,0:T(8,128)S(1)}, u32[]{:S(2)}, u32[]{:S(2)}) collective-permute-start(f32[288,128]{1,0:T(8,128)S(1)} %concatenate.42), channel_id=1, source_target_pairs={{0,128},{1,129},{2,130},{3,131},{4,132},{5,133},{6,134},{7,135},{8... | collective-permute-start | bytes 442376 | tf_op jit(solution)/shard_map/ppermute | solution.py:50
  18.0 2.7 %collective-permute-start.7 = (f32[16,128]{1,0:T(8,128)S(1)}, f32[16,128]{1,0:T(8,128)S(1)}, u32[]{:S(2)}, u32[]{:S(2)}) collective-permute-start(f32[16,128]{1,0:T(8,128)S(1)} %pad_maximum_fusion.2), channel_id=1, source_target_pairs={{0,8},{1,9},{2,10},{3,11},{4,12},{5,13},{6,14},{7,15},{8,0},{9,1},... | collective-permute-start | bytes 24584 | tf_op jit(solution)/shard_map/ppermute | solution.py:50
  22.3 2.5 %collective-permute-start.9 = (f32[16,128]{1,0:T(8,128)S(1)}, f32[16,128]{1,0:T(8,128)S(1)}, u32[]{:S(2)}, u32[]{:S(2)}) collective-permute-start(f32[16,128]{1,0:T(8,128)S(1)} %pad_maximum_fusion.2), channel_id=1, source_target_pairs={{0,12},{1,13},{2,14},{3,15},{4,8},{5,9},{6,10},{7,11},{8,4},{9,5},... | collective-permute-start | bytes 24584 | tf_op jit(solution)/shard_map/ppermute | solution.py:50
  26.7 4.4 %collective-permute-start.10 = (f32[64,128]{1,0:T(8,128)S(1)}, f32[64,128]{1,0:T(8,128)S(1)}, u32[]{:S(2)}, u32[]{:S(2)}) collective-permute-start(f32[64,128]{1,0:T(8,128)S(1)} %concatenate.46), channel_id=1, source_target_pairs={{0,1},{1,0},{2,3},{3,2},{4,5},{5,4},{6,7},{7,6},{8,9},{9,8},{10,11... | collective-permute-start | bytes 98312 | tf_op jit(solution)/shard_map/ppermute | solution.py:50
  34.2 15.5 %shard_map.50 = (f32[1152,128]{1,0:T(8,128)S(1)}, bf16[8,2048,256]{2,1,0:T(8,128)(2,1)S(1)}, bf16[8,2048,256]{2,1,0:T(8,128)(2,1)S(1)}) custom-call(f32[1152,128]{1,0:T(8,128)S(1)} %concatenate.43.v_ref, f32[128,128]{1,0:T(8,128)S(1)} %concatenate.47.rows_ref), custom_call_target="tpu_custom_call" | custom-call | tf_op jit(solution)/shard_map/pallas_call | solution.py:149
  60.6 2.5 %collective-permute-done.15 = f32[72,128]{1,0:T(8,128)S(1)} collective-permute-done((f32[72,128]{1,0:T(8,128)S(1)}, f32[72,128]{1,0:T(8,128)S(1)}, u32[]{:S(2)}, u32[]{:S(2)}) %collective-permute-start.15) | collective-permute-done | bytes 36896 | tf_op jit(solution)/shard_map/ppermute | solution.py:50
  66.3 2.1 %collective-permute-start.17 = (f32[72,128]{1,0:T(8,128)S(1)}, f32[72,128]{1,0:T(8,128)S(1)}, u32[]{:S(2)}, u32[]{:S(2)}) collective-permute-start(f32[72,128]{1,0:T(8,128)S(1)} %shard_map.51.first_ref), channel_id=1, source_target_pairs={{0,32},{1,33},{2,34},{3,35},{4,36},{5,37},{6,38},{7,39},{8,40},{9,... | collective-permute-start | bytes 110600 | tf_op jit(solution)/shard_map/ppermute | solution.py:50
  71.2 2.8 %collective-permute-start.19 = (f32[288,128]{1,0:T(8,128)S(1)}, f32[288,128]{1,0:T(8,128)S(1)}, u32[]{:S(2)}, u32[]{:S(2)}) collective-permute-start(f32[288,128]{1,0:T(8,128)S(1)} %pad_maximum_fusion), channel_id=1, source_target_pairs={{0,128},{1,129},{2,130},{3,131},{4,132},{5,133},{6,134},{7,135},{8... | collective-permute-start | bytes 442376 | tf_op jit(solution)/shard_map/ppermute | solution.py:50
  79.7 3.9 %shard_map.52 = f32[1152,128]{1,0:T(8,128)S(1)} custom-call(f32[1152,128]{1,0:T(8,128)S(1)} %constant_dynamic-update-slice_fusion.v_ref, bf16[8,2048,256]{2,1,0:T(8,128)(2,1)S(1)} %get-tuple-element.11.high_ref, bf16[8,2048,256]{2,1,0:T(8,128)(2,1)S(1)} %get-tuple-element.12.low_ref), custom_call_target="tpu_custom_call" | custom-call | tf_op jit(solution)/shard_map/pallas_call | solution.py:178
  83.6 6.7 %collective-permute-start.22 = (f32[576,128]{1,0:T(8,128)S(1)}, f32[576,128]{1,0:T(8,128)S(1)}, u32[]{:S(2)}, u32[]{:S(2)}) collective-permute-start(f32[576,128]{1,0:T(8,128)S(1)} %slice.103), channel_id=1, source_target_pairs={{0,1},{1,0},{2,3},{3,2},{4,5},{5,4},{6,7},{7,6},{8,9},{9,8},{10,11... | collective-permute-start | bytes 884744 | tf_op jit(solution)/shard_map/ppermute | solution.py:50
  98.5 2.0 %collective-permute-start.26 = (f32[72,128]{1,0:T(8,128)S(1)}, f32[72,128]{1,0:T(8,128)S(1)}, u32[]{:S(2)}, u32[]{:S(2)}) collective-permute-start(f32[72,128]{1,0:T(8,128)S(1)} %slice.109), channel_id=1, source_target_pairs={{0,50},{1,51},{2,48},{3,49},{4,54},{5,55},{6,52},{7,53},{8,58},{9,... | collective-permute-start | bytes 110600 | tf_op jit(solution)/shard_map/ppermute | solution.py:50
  100.5 2.1 %collective-permute-done.26 = f32[72,128]{1,0:T(8,128)S(1)} collective-permute-done((f32[72,128]{1,0:T(8,128)S(1)}, f32[72,128]{1,0:T(8,128)S(1)}, u32[]{:S(2)}, u32[]{:S(2)}) %collective-permute-start.26) | collective-permute-done | bytes 36896 | tf_op jit(solution)/shard_map/ppermute | solution.py:50
  112.2 2.3 %collective-permute-done.30 = f32[288,128]{1,0:T(8,128)S(1)} collective-permute-done((f32[288,128]{1,0:T(8,128)S(1)}, f32[288,128]{1,0:T(8,128)S(1)}, u32[]{:S(2)}, u32[]{:S(2)}) %collective-permute-start.30) | collective-permute-done | bytes 147488 | tf_op jit(solution)/shard_map/ppermute | solution.py:50
  116.0 3.8 %shard_map.54 = f32[1152,128]{1,0:T(8,128)S(1)} custom-call(f32[1152,128]{1,0:T(8,128)S(1)} %constant_dynamic-update-slice_fusion.11.v_ref, bf16[8,2048,256]{2,1,0:T(8,128)(2,1)S(1)} %get-tuple-element.11.high_ref, bf16[8,2048,256]{2,1,0:T(8,128)(2,1)S(1)} %get-tuple-element.12.low_ref), custom_call_target="tpu_custom_call" | custom-call | tf_op jit(solution)/shard_map/pallas_call | solution.py:178
  119.9 5.3 %collective-permute-start.33 = (f32[576,128]{1,0:T(8,128)S(1)}, f32[576,128]{1,0:T(8,128)S(1)}, u32[]{:S(2)}, u32[]{:S(2)}) collective-permute-start(f32[576,128]{1,0:T(8,128)S(1)} %slice.111), channel_id=1, source_target_pairs={{0,1},{1,0},{2,3},{3,2},{4,5},{5,4},{6,7},{7,6},{8,9},{9,8},{10,11... | collective-permute-start | bytes 884744 | tf_op jit(solution)/shard_map/ppermute | solution.py:50
  126.7 2.3 %collective-permute-start.35 = (f32[144,128]{1,0:T(8,128)S(1)}, f32[144,128]{1,0:T(8,128)S(1)}, u32[]{:S(2)}, u32[]{:S(2)}) collective-permute-start(f32[144,128]{1,0:T(8,128)S(1)} %get-tuple-element.20), channel_id=1, source_target_pairs={{0,4},{1,5},{2,6},{3,7},{4,0},{5,1},{6,2},{7,3},{8,12},{9,13},{10,... | collective-permute-start | bytes 221192 | tf_op jit(solution)/shard_map/ppermute | solution.py:50
  133.6 2.3 %collective-permute-start.37 = (f32[72,128]{1,0:T(8,128)S(1)}, f32[72,128]{1,0:T(8,128)S(1)}, u32[]{:S(2)}, u32[]{:S(2)}) collective-permute-start(f32[72,128]{1,0:T(8,128)S(1)} %slice.117), channel_id=1, source_target_pairs={{0,50},{1,51},{2,48},{3,49},{4,54},{5,55},{6,52},{7,53},{8,58},{9,... | collective-permute-start | bytes 110600 | tf_op jit(solution)/shard_map/ppermute | solution.py:50
  135.8 2.1 %collective-permute-done.37 = f32[72,128]{1,0:T(8,128)S(1)} collective-permute-done((f32[72,128]{1,0:T(8,128)S(1)}, f32[72,128]{1,0:T(8,128)S(1)}, u32[]{:S(2)}, u32[]{:S(2)}) %collective-permute-start.37) | collective-permute-done | bytes 36896 | tf_op jit(solution)/shard_map/ppermute | solution.py:50
  142.2 2.1 %collective-permute-start.40 = (f32[8,128]{1,0:T(8,128)S(1)}, f32[8,128]{1,0:T(8,128)S(1)}, u32[]{:S(2)}, u32[]{:S(2)}) collective-permute-start(f32[8,128]{1,0:T(8,128)S(1)} %add.95), channel_id=1, source_target_pairs={{0,4},{1,5},{2,6},{3,7},{4,0},{5,1},{6,2},{7,3},{8,12},{9,13},{10,... | collective-permute-start | bytes 12296 | tf_op jit(solution)/shard_map/ppermute | solution.py:50
  147.9 5.3 %collective-permute-start.42 = (f32[8,128]{1,0:T(8,128)S(1)}, f32[8,128]{1,0:T(8,128)S(1)}, u32[]{:S(2)}, u32[]{:S(2)}) collective-permute-start(f32[8,128]{1,0:T(8,128)S(1)} %add_add_fusion.2), channel_id=1, source_target_pairs={{0,1},{1,0},{2,3},{3,2},{4,5},{5,4},{6,7},{7,6},{8,9},{9,8},{10,11... | collective-permute-start | bytes 12296 | tf_op jit(solution)/shard_map/ppermute | solution.py:50
  155.7 3.6 %collective-permute-start.44 = (f32[8,128]{1,0:T(8,128)S(1)}, f32[8,128]{1,0:T(8,128)S(1)}, u32[]{:S(2)}, u32[]{:S(2)}) collective-permute-start(f32[8,128]{1,0:T(8,128)S(1)} %add.99), channel_id=1, source_target_pairs={{0,32},{1,33},{2,34},{3,35},{4,36},{5,37},{6,38},{7,39},{8,40},{9,... | collective-permute-start | bytes 12296 | tf_op jit(solution)/shard_map/ppermute | solution.py:50
  165.7 2.5 %collective-permute-done.48 = f32[8,128]{1,0:T(8,128)S(1)} collective-permute-done((f32[8,128]{1,0:T(8,128)S(1)}, f32[8,128]{1,0:T(8,128)S(1)}, u32[]{:S(2)}, u32[]{:S(2)}) %collective-permute-start.48) | collective-permute-done | bytes 4128 | tf_op jit(solution)/shard_map/ppermute | solution.py:50
  (135 shorter events, 76.9 us)
Async XLA Ops:
  1.4 10.6 %collective-permute-start = (f32[72,128]{1,0:T(8,128)S(1)}, f32[72,128]{1,0:T(8,128)S(1)}, u32[]{:S(2)}, u32[]{:S(2)}) collective-permute-start(f32[72,128]{1,0:T(8,128)S(1)} %pad_maximum_fusion.1), channel_id=1, source_target_pairs={{0,48},{1,49},{2,50},{3,51},{4,52},{5,53},{6,54},{7,55},{8,56},{9,... | collective-permute-start | bytes 110600 | tf_op jit(solution)/shard_map/ppermute | solution.py:50
  6.6 5.5 %collective-permute-start.1 = (f32[72,128]{1,0:T(8,128)S(1)}, f32[72,128]{1,0:T(8,128)S(1)}, u32[]{:S(2)}, u32[]{:S(2)}) collective-permute-start(f32[72,128]{1,0:T(8,128)S(1)} %pad_maximum_fusion.1), channel_id=1, source_target_pairs={{0,32},{1,33},{2,34},{3,35},{4,36},{5,37},{6,38},{7,39},{8,40},{9,... | collective-permute-start | bytes 110600 | tf_op jit(solution)/shard_map/ppermute | solution.py:50
  6.6 5.5 %collective-permute-start.2 = (f32[72,128]{1,0:T(8,128)S(1)}, f32[72,128]{1,0:T(8,128)S(1)}, u32[]{:S(2)}, u32[]{:S(2)}) collective-permute-start(f32[72,128]{1,0:T(8,128)S(1)} %pad_maximum_fusion.1), channel_id=1, source_target_pairs={{0,16},{1,17},{2,18},{3,19},{4,20},{5,21},{6,22},{7,23},{8,24},{9,... | collective-permute-start | bytes 110600 | tf_op jit(solution)/shard_map/ppermute | solution.py:50
  7.7 9.7 %collective-permute-start.6 = (f32[8,128]{1,0:T(8,128)S(1)}, f32[8,128]{1,0:T(8,128)S(1)}, u32[]{:S(2)}, u32[]{:S(2)}) collective-permute-start(f32[8,128]{1,0:T(8,128)S(1)} %concatenate.44), channel_id=1, source_target_pairs={{0,50},{1,51},{2,48},{3,49},{4,54},{5,55},{6,52},{7,53},{8,58},{9,... | collective-permute-start | bytes 12296 | tf_op jit(solution)/shard_map/ppermute | solution.py:50
  13.5 19.1 %collective-permute-start.3 = (f32[288,128]{1,0:T(8,128)S(1)}, f32[288,128]{1,0:T(8,128)S(1)}, u32[]{:S(2)}, u32[]{:S(2)}) collective-permute-start(f32[288,128]{1,0:T(8,128)S(1)} %concatenate.42), channel_id=1, source_target_pairs={{0,128},{1,129},{2,130},{3,131},{4,132},{5,133},{6,134},{7,135},{8... | collective-permute-start | bytes 442376 | tf_op jit(solution)/shard_map/ppermute | solution.py:50
  16.5 16.1 %collective-permute-start.4 = (f32[288,128]{1,0:T(8,128)S(1)}, f32[288,128]{1,0:T(8,128)S(1)}, u32[]{:S(2)}, u32[]{:S(2)}) collective-permute-start(f32[288,128]{1,0:T(8,128)S(1)} %concatenate.42), channel_id=1, source_target_pairs={{0,64},{1,65},{2,66},{3,67},{4,68},{5,69},{6,70},{7,71},{8,72},{9,... | collective-permute-start | bytes 442376 | tf_op jit(solution)/shard_map/ppermute | solution.py:50
  16.9 15.7 %collective-permute-start.5 = (f32[288,128]{1,0:T(8,128)S(1)}, f32[288,128]{1,0:T(8,128)S(1)}, u32[]{:S(2)}, u32[]{:S(2)}) collective-permute-start(f32[288,128]{1,0:T(8,128)S(1)} %concatenate.42), channel_id=1, source_target_pairs={{0,192},{1,193},{2,194},{3,195},{4,196},{5,197},{6,198},{7,199},{8... | collective-permute-start | bytes 442376 | tf_op jit(solution)/shard_map/ppermute | solution.py:50
  26.7 5.2 %collective-permute-start.10 = (f32[64,128]{1,0:T(8,128)S(1)}, f32[64,128]{1,0:T(8,128)S(1)}, u32[]{:S(2)}, u32[]{:S(2)}) collective-permute-start(f32[64,128]{1,0:T(8,128)S(1)} %concatenate.46), channel_id=1, source_target_pairs={{0,1},{1,0},{2,3},{3,2},{4,5},{5,4},{6,7},{7,6},{8,9},{9,8},{10,11... | collective-permute-start | bytes 98312 | tf_op jit(solution)/shard_map/ppermute | solution.py:50
  51.4 4.8 %collective-permute-start.12 = (f32[144,128]{1,0:T(8,128)S(1)}, f32[144,128]{1,0:T(8,128)S(1)}, u32[]{:S(2)}, u32[]{:S(2)}) collective-permute-start(f32[144,128]{1,0:T(8,128)S(1)} %get-tuple-element.24), channel_id=1, source_target_pairs={{0,8},{1,9},{2,10},{3,11},{4,12},{5,13},{6,14},{7,15},{8,0},{9,1},... | collective-permute-start | bytes 221192 | tf_op jit(solution)/shard_map/ppermute | solution.py:50
  53.1 5.1 %collective-permute-start.13 = (f32[144,128]{1,0:T(8,128)S(1)}, f32[144,128]{1,0:T(8,128)S(1)}, u32[]{:S(2)}, u32[]{:S(2)}) collective-permute-start(f32[144,128]{1,0:T(8,128)S(1)} %get-tuple-element.26), channel_id=1, source_target_pairs={{0,4},{1,5},{2,6},{3,7},{4,0},{5,1},{6,2},{7,3},{8,12},{9,13},{10,... | collective-permute-start | bytes 221192 | tf_op jit(solution)/shard_map/ppermute | solution.py:50
  71.2 5.6 %collective-permute-start.19 = (f32[288,128]{1,0:T(8,128)S(1)}, f32[288,128]{1,0:T(8,128)S(1)}, u32[]{:S(2)}, u32[]{:S(2)}) collective-permute-start(f32[288,128]{1,0:T(8,128)S(1)} %pad_maximum_fusion), channel_id=1, source_target_pairs={{0,128},{1,129},{2,130},{3,131},{4,132},{5,133},{6,134},{7,135},{8... | collective-permute-start | bytes 442376 | tf_op jit(solution)/shard_map/ppermute | solution.py:50
  74.5 5.2 %collective-permute-start.21 = (f32[288,128]{1,0:T(8,128)S(1)}, f32[288,128]{1,0:T(8,128)S(1)}, u32[]{:S(2)}, u32[]{:S(2)}) collective-permute-start(f32[288,128]{1,0:T(8,128)S(1)} %pad_maximum_fusion), channel_id=1, source_target_pairs={{0,192},{1,193},{2,194},{3,195},{4,196},{5,197},{6,198},{7,199},{8... | collective-permute-start | bytes 442376 | tf_op jit(solution)/shard_map/ppermute | solution.py:50
  83.6 7.9 %collective-permute-start.22 = (f32[576,128]{1,0:T(8,128)S(1)}, f32[576,128]{1,0:T(8,128)S(1)}, u32[]{:S(2)}, u32[]{:S(2)}) collective-permute-start(f32[576,128]{1,0:T(8,128)S(1)} %slice.103), channel_id=1, source_target_pairs={{0,1},{1,0},{2,3},{3,2},{4,5},{5,4},{6,7},{7,6},{8,9},{9,8},{10,11... | collective-permute-start | bytes 884744 | tf_op jit(solution)/shard_map/ppermute | solution.py:50
  91.6 4.8 %collective-permute-start.23 = (f32[144,128]{1,0:T(8,128)S(1)}, f32[144,128]{1,0:T(8,128)S(1)}, u32[]{:S(2)}, u32[]{:S(2)}) collective-permute-start(f32[144,128]{1,0:T(8,128)S(1)} %get-tuple-element.21), channel_id=1, source_target_pairs={{0,8},{1,9},{2,10},{3,11},{4,12},{5,13},{6,14},{7,15},{8,0},{9,1},... | collective-permute-start | bytes 221192 | tf_op jit(solution)/shard_map/ppermute | solution.py:50
  91.7 4.7 %collective-permute-start.24 = (f32[144,128]{1,0:T(8,128)S(1)}, f32[144,128]{1,0:T(8,128)S(1)}, u32[]{:S(2)}, u32[]{:S(2)}) collective-permute-start(f32[144,128]{1,0:T(8,128)S(1)} %get-tuple-element.23), channel_id=1, source_target_pairs={{0,4},{1,5},{2,6},{3,7},{4,0},{5,1},{6,2},{7,3},{8,12},{9,13},{10,... | collective-permute-start | bytes 221192 | tf_op jit(solution)/shard_map/ppermute | solution.py:50
  93.0 5.4 %collective-permute-start.25 = (f32[144,128]{1,0:T(8,128)S(1)}, f32[144,128]{1,0:T(8,128)S(1)}, u32[]{:S(2)}, u32[]{:S(2)}) collective-permute-start(f32[144,128]{1,0:T(8,128)S(1)} %get-tuple-element.22), channel_id=1, source_target_pairs={{0,12},{1,13},{2,14},{3,15},{4,8},{5,9},{6,10},{7,11},{8,4},{9,5},... | collective-permute-start | bytes 221192 | tf_op jit(solution)/shard_map/ppermute | solution.py:50
  102.9 4.8 %collective-permute-start.27 = (f32[72,128]{1,0:T(8,128)S(1)}, f32[72,128]{1,0:T(8,128)S(1)}, u32[]{:S(2)}, u32[]{:S(2)}) collective-permute-start(f32[72,128]{1,0:T(8,128)S(1)} %get-tuple-element.13.third_ref), channel_id=1, source_target_pairs={{0,48},{1,49},{2,50},{3,51},{4,52},{5,53},{6,54},{7,55},{8,56},{9,... | collective-permute-start | bytes 110600 | tf_op jit(solution)/shard_map/ppermute | solution.py:50
  108.9 5.6 %collective-permute-start.30 = (f32[288,128]{1,0:T(8,128)S(1)}, f32[288,128]{1,0:T(8,128)S(1)}, u32[]{:S(2)}, u32[]{:S(2)}) collective-permute-start(f32[288,128]{1,0:T(8,128)S(1)} %get-tuple-element.27), channel_id=1, source_target_pairs={{0,128},{1,129},{2,130},{3,131},{4,132},{5,133},{6,134},{7,135},{8... | collective-permute-start | bytes 442376 | tf_op jit(solution)/shard_map/ppermute | solution.py:50
  110.3 5.8 %collective-permute-start.32 = (f32[288,128]{1,0:T(8,128)S(1)}, f32[288,128]{1,0:T(8,128)S(1)}, u32[]{:S(2)}, u32[]{:S(2)}) collective-permute-start(f32[288,128]{1,0:T(8,128)S(1)} %get-tuple-element.27), channel_id=1, source_target_pairs={{0,192},{1,193},{2,194},{3,195},{4,196},{5,197},{6,198},{7,199},{8... | collective-permute-start | bytes 442376 | tf_op jit(solution)/shard_map/ppermute | solution.py:50
  119.9 6.5 %collective-permute-start.33 = (f32[576,128]{1,0:T(8,128)S(1)}, f32[576,128]{1,0:T(8,128)S(1)}, u32[]{:S(2)}, u32[]{:S(2)}) collective-permute-start(f32[576,128]{1,0:T(8,128)S(1)} %slice.111), channel_id=1, source_target_pairs={{0,1},{1,0},{2,3},{3,2},{4,5},{5,4},{6,7},{7,6},{8,9},{9,8},{10,11... | collective-permute-start | bytes 884744 | tf_op jit(solution)/shard_map/ppermute | solution.py:50
  126.5 4.8 %collective-permute-start.34 = (f32[144,128]{1,0:T(8,128)S(1)}, f32[144,128]{1,0:T(8,128)S(1)}, u32[]{:S(2)}, u32[]{:S(2)}) collective-permute-start(f32[144,128]{1,0:T(8,128)S(1)} %get-tuple-element.18), channel_id=1, source_target_pairs={{0,8},{1,9},{2,10},{3,11},{4,12},{5,13},{6,14},{7,15},{8,0},{9,1},... | collective-permute-start | bytes 221192 | tf_op jit(solution)/shard_map/ppermute | solution.py:50
  126.7 5.9 %collective-permute-start.35 = (f32[144,128]{1,0:T(8,128)S(1)}, f32[144,128]{1,0:T(8,128)S(1)}, u32[]{:S(2)}, u32[]{:S(2)}) collective-permute-start(f32[144,128]{1,0:T(8,128)S(1)} %get-tuple-element.20), channel_id=1, source_target_pairs={{0,4},{1,5},{2,6},{3,7},{4,0},{5,1},{6,2},{7,3},{8,12},{9,13},{10,... | collective-permute-start | bytes 221192 | tf_op jit(solution)/shard_map/ppermute | solution.py:50
  147.9 6.2 %collective-permute-start.42 = (f32[8,128]{1,0:T(8,128)S(1)}, f32[8,128]{1,0:T(8,128)S(1)}, u32[]{:S(2)}, u32[]{:S(2)}) collective-permute-start(f32[8,128]{1,0:T(8,128)S(1)} %add_add_fusion.2), channel_id=1, source_target_pairs={{0,1},{1,0},{2,3},{3,2},{4,5},{5,4},{6,7},{7,6},{8,9},{9,8},{10,11... | collective-permute-start | bytes 12296 | tf_op jit(solution)/shard_map/ppermute | solution.py:50
  154.1 5.2 %collective-permute-start.43 = (f32[8,128]{1,0:T(8,128)S(1)}, f32[8,128]{1,0:T(8,128)S(1)}, u32[]{:S(2)}, u32[]{:S(2)}) collective-permute-start(f32[8,128]{1,0:T(8,128)S(1)} %add.99), channel_id=1, source_target_pairs={{0,48},{1,49},{2,50},{3,51},{4,52},{5,53},{6,54},{7,55},{8,56},{9,... | collective-permute-start | bytes 12296 | tf_op jit(solution)/shard_map/ppermute | solution.py:50
  (29 other events, 142.6 us)

commit v2 on v1

v2 whole, which is shorter than its diff:
```python
import functools
import math

import jax
import jax.numpy as jnp
from jax import lax
from jax.experimental import pallas as pl
from jax.experimental.pallas import tpu as pltpu
from jax.sharding import PartitionSpec as P

QUAD_XX = 1.6
QUAD_XY = 0.5
QUAD_YY = 0.7
INVERSE_SQUARE = 25.0
KERNEL_WEIGHT = 2048.0

PX = math.sqrt(QUAD_XX * INVERSE_SQUARE)
PY = QUAD_XY * INVERSE_SQUARE / PX
QY = math.sqrt(QUAD_YY * INVERSE_SQUARE - PY * PY)

AXES = ("row", "col")
LANES = 128
SPARE = 8
TILE = 256
VMEM_LIMIT = 24 * 1024 * 1024

FIRST_A, LAST_A = ("z", (3, 2, 1)), ("y", (2, 1, 3))
ROUNDS_B = (("z", (7,)), ("x", (2, 1, 3)), ("core", (1,)))


def place(index):
    row, col = divmod(index, 16)
    y, z_lo = divmod(row, 4)
    x, rest = divmod(col, 4)
    z_hi, core = divmod(rest, 2)
    return {"x": x, "y": y, "z": z_hi * 4 + z_lo, "core": core}


def number(at):
    row = at["y"] * 4 + at["z"] % 4
    return row * 16 + at["x"] * 4 + (at["z"] // 4) * 2 + at["core"]


def exchange(value, axis, mask):
    pairs = []
    for index in range(256):
        at = place(index)
        at[axis] ^= mask
        pairs.append((index, number(at)))
    return lax.ppermute(value, AXES, pairs)


def gather(block, rounds):
    for axis, masks in rounds:
        block = jnp.concatenate([block] + [exchange(block, axis, m) for m in masks], axis=0)
    return block


def scatter_sum(blocks, rounds):
    for axis, masks in reversed(rounds):
        rows = blocks.shape[0] // (len(masks) + 1)
        total = blocks[:rows]
        for i, m in enumerate(masks):
            total = total + exchange(blocks[(i + 1) * rows : (i + 2) * rows], axis, m)
        blocks = total
    return blocks


def all_sum(block):
    copies = jnp.broadcast_to(block[None], (lax.axis_size("row"),) + block.shape)
    block = jnp.sum(lax.all_to_all(copies, "row", 0, 0), axis=0)
    for axis, masks in reversed(ROUNDS_B):
        block = block + sum(exchange(block, axis, m) for m in masks)
    return block


def split(vectors):
    high = vectors.astype(jnp.bfloat16)
    low = (vectors - high.astype(jnp.float32)).astype(jnp.bfloat16)
    return high, low


def unpack(v_ref, pair_ref, rhs):
    total = jnp.zeros((SPARE, LANES), jnp.float32)
    step = rhs + SPARE
    for b in range(v_ref.shape[0] // step):
        high, low = split(v_ref[b * step : b * step + rhs, :])
        pair_ref[:rhs, b * LANES : (b + 1) * LANES] = high
        pair_ref[rhs:, b * LANES : (b + 1) * LANES] = low
        total = total + v_ref[b * step + rhs : (b + 1) * step, :]
    return total


def emit(before_ref, out_ref, tile, product, dots, rhs):
    step = rhs + SPARE
    for piece in range(TILE // LANES):
        start = pl.multiple_of((tile * (TILE // LANES) + piece) * step, 8)
        part = product[:, piece * LANES : (piece + 1) * LANES]
        spare = dots
        if before_ref is not None:
            part = part + before_ref[pl.ds(start, rhs), :]
            spare = spare + before_ref[pl.ds(start + rhs, SPARE), :]
        out_ref[pl.ds(start, rhs), :] = part
        out_ref[pl.ds(start + rhs, SPARE), :] = spare


def first_body(rhs, amplitude, v_ref, rows_ref, before_ref, out_ref, high_ref, low_ref, pair_ref, p_ref, q_ref):
    step = rhs + SPARE
    tiles, stars, _ = high_ref.shape
    unpack(v_ref, pair_ref, rhs)
    for b in range(stars // LANES):
        spare = v_ref[b * step + rhs : (b + 1) * step, :]
        x, y = to_columns(spare, 2, LANES)
        rows = slice(b * LANES, (b + 1) * LANES)
        p_ref[rows, :] = jnp.broadcast_to(PX * x + PY * y, (LANES, LANES))
        q_ref[rows, :] = jnp.broadcast_to(QY * y, (LANES, LANES))

    def tile_step(tile, carry):
        product = jnp.zeros((rhs, TILE), jnp.float32)
        row_p, row_q = [], []
        for piece in range(TILE // LANES):
            at = pl.multiple_of((tile * (TILE // LANES) + piece) * SPARE, SPARE)
            places = rows_ref[pl.ds(at, SPARE), :]
            x, y = places[0:1, :], places[1:2, :]
            row_p.append(PX * x + PY * y)
            row_q.append(QY * y)
        for j in range(0, stars, TILE):
            pieces = []
            for p, q in zip(row_p, row_q):
                delta_p = p_ref[j : j + TILE, :] - p
                delta_q = q_ref[j : j + TILE, :] - q
                square = delta_p * delta_p + delta_q * delta_q
                distance = square * lax.rsqrt(jnp.maximum(square, 1e-30))
                pieces.append(split(jnp.exp(-distance)))
            high = jnp.concatenate([h for h, _ in pieces], axis=1)
            low = jnp.concatenate([l for _, l in pieces], axis=1)
            high_ref[tile, j : j + TILE, :] = high
            low_ref[tile, j : j + TILE, :] = low
            both = jnp.dot(pair_ref[:, j : j + TILE], high, preferred_element_type=jnp.float32)
            rest = jnp.dot(pair_ref[:rhs, j : j + TILE], low, preferred_element_type=jnp.float32)
            product = product + (both[:rhs] + (both[rhs:] + rest))
        emit(before_ref, out_ref, tile, product * amplitude, jnp.zeros((SPARE, LANES), jnp.float32), rhs)
        return carry

    lax.fori_loop(0, tiles, tile_step, 0)


def next_body(rhs, amplitude, v_ref, high_ref, low_ref, before_ref, out_ref, pair_ref):
    dots = unpack(v_ref, pair_ref, rhs)
    for tile in range(high_ref.shape[0]):
        both = jnp.dot(pair_ref[...], high_ref[tile], preferred_element_type=jnp.float32)
        rest = jnp.dot(pair_ref[:rhs, :], low_ref[tile], preferred_element_type=jnp.float32)
        product = (both[:rhs] + (both[rhs:] + rest)) * amplitude
        emit(before_ref, out_ref, tile, product, dots, rhs)


def no_before(body, at, *refs):
    body(*refs[:at], None, *refs[at:])


def kernel_call(body, outs, scratch, flops, operands):
    whole = pl.BlockSpec(memory_space=pltpu.VMEM)
    return pl.pallas_call(
        body,
        in_specs=[whole] * len(operands),
        out_specs=[whole] * len(outs),
        out_shape=outs,
        scratch_shapes=scratch,
        cost_estimate=pl.CostEstimate(flops=flops, bytes_accessed=0, transcendentals=0),
        compiler_params=pltpu.CompilerParams(vmem_limit_bytes=VMEM_LIMIT),
    )(*operands)


def first_product(part, row_points, before, rhs, amplitude):
    columns = part.shape[0] // (rhs + SPARE) * LANES
    pieces = row_points.shape[0] // SPARE
    tiles = pieces * LANES // TILE
    shape = (tiles, columns, TILE)
    outs = [
        jax.ShapeDtypeStruct((pieces * (rhs + SPARE), LANES), jnp.float32),
        jax.ShapeDtypeStruct(shape, jnp.bfloat16),
        jax.ShapeDtypeStruct(shape, jnp.bfloat16),
    ]
    scratch = [
        pltpu.VMEM((2 * rhs, columns), jnp.bfloat16),
        pltpu.VMEM((columns, LANES), jnp.float32),
        pltpu.VMEM((columns, LANES), jnp.float32),
    ]
    body = functools.partial(first_body, rhs, amplitude)
    operands = [part, row_points]
    if before is None:
        body = functools.partial(no_before, body, 2)
    else:
        operands.append(before)
    return kernel_call(body, outs, scratch, 3 << 30, operands)


def next_product(part, high, low, before, rhs, amplitude):
    tiles, columns, _ = high.shape
    outs = [
        jax.ShapeDtypeStruct((tiles * (TILE // LANES) * (rhs + SPARE), LANES), jnp.float32)
    ]
    scratch = [pltpu.VMEM((2 * rhs, columns), jnp.bfloat16)]
    body = functools.partial(next_body, rhs, amplitude)
    operands = [part, high, low]
    if before is None:
        body = functools.partial(no_before, body, 3)
    else:
        operands.append(before)
    return kernel_call(body, outs, scratch, 1 << 30, operands)[0]


def parts_of(block):
    axis, masks = LAST_A
    block = gather(block, (FIRST_A,))
    return [block] + [exchange(block, axis, m) for m in masks]


def dot(a, b):
    return jnp.sum(a * b, axis=1, keepdims=True)


def to_rows(columns, rhs):
    lane = lax.broadcasted_iota(jnp.int32, (rhs, LANES), 1)
    tile = jnp.zeros((rhs, LANES), jnp.float32)
    for i, column in enumerate(columns):
        tile = jnp.where(lane == i, column, tile)
    square = jnp.concatenate([tile, jnp.zeros((LANES - rhs, LANES), jnp.float32)], axis=0)
    return square.T[:SPARE, :]


def to_columns(tile, count, rhs):
    square = jnp.concatenate([tile, jnp.zeros((LANES - SPARE, LANES), jnp.float32)], axis=0).T
    return [square[:rhs, i : i + 1] for i in range(count)]


def pack(rhs, right_ref, points_ref, noise_ref, out_ref, places_ref):
    spare = jnp.concatenate(
        [points_ref[...], noise_ref[...], jnp.zeros((SPARE - 3, LANES), jnp.float32)], axis=0
    )
    out_ref[:rhs, :] = right_ref[...]
    out_ref[rhs:, :] = spare
    places_ref[...] = spare


def right_and_noise(packed_ref, rhs):
    return packed_ref[:rhs, :], packed_ref[rhs + 2 : rhs + 3, :]


def update_one(rhs, sums_ref, packed_ref, out_ref):
    right, noise = right_and_noise(packed_ref, rhs)
    image = sums_ref[:rhs, :] + noise * right
    out_ref[:rhs, :] = image
    out_ref[rhs:, :] = to_rows([dot(right, right), dot(right, image)], rhs)


def update_two(rhs, sums_ref, packed_ref, first_ref, out_ref, second_ref, scalars_ref):
    right, noise = right_and_noise(packed_ref, rhs)
    w0 = first_ref[:rhs, :]
    n0 = sums_ref[:rhs, :] + noise * w0
    norm, curve = to_columns(sums_ref[rhs:, :], 2, rhs)
    alpha = norm / curve
    r1 = right - alpha * w0
    w1 = w0 - alpha * n0
    out_ref[:rhs, :] = w1
    out_ref[rhs:, :] = to_rows([dot(r1, r1), dot(r1, w1)], rhs)
    second_ref[...] = n0
    scalars_ref[...] = sums_ref[rhs:, :]


def update_three(rhs, sums_ref, packed_ref, first_ref, second_ref, third_ref, scalars_ref, dots_ref, carry_ref):
    right, noise = right_and_noise(packed_ref, rhs)
    w0 = first_ref[:rhs, :]
    n0 = second_ref[...]
    w1 = third_ref[:rhs, :]
    n1 = sums_ref[:rhs, :] + noise * w1
    norm0, curve0 = to_columns(scalars_ref[...], 2, rhs)
    norm1, curve1 = to_columns(sums_ref[rhs:, :], 2, rhs)
    alpha0 = norm0 / curve0
    beta1 = norm1 / norm0
    alpha1 = norm1 / (curve1 - beta1 * norm1 / alpha0)
    r1 = right - alpha0 * w0
    s1 = w1 + beta1 * w0
    p1 = r1 + beta1 * right
    z1 = n1 + beta1 * n0
    r2 = r1 - alpha1 * s1
    w2 = w1 - alpha1 * z1
    dots_ref[...] = to_rows([dot(r2, r2), dot(r2, w2)], rhs)
    lane = lax.broadcasted_iota(jnp.int32, (rhs, LANES), 1)
    carry_ref[0] = alpha0 * right + alpha1 * p1
    carry_ref[1] = r2
    carry_ref[2] = p1
    carry_ref[3] = s1
    carry_ref[4] = w2
    carry_ref[5] = jnp.where(lane == 0, alpha1, norm1)


def update_four(rhs, dots_ref, carry_ref, solution_ref, residual_ref):
    norm2, curve2 = to_columns(dots_ref[...], 2, rhs)
    alpha1 = carry_ref[5, :, 0:1]
    norm1 = carry_ref[5, :, 1:2]
    r2 = carry_ref[1]
    beta2 = norm2 / norm1
    alpha2 = norm2 / (curve2 - beta2 * norm2 / alpha1)
    solution_ref[...] = carry_ref[0] + alpha2 * (r2 + beta2 * carry_ref[2])
    residual_ref[...] = r2 - alpha2 * (carry_ref[4] + beta2 * carry_ref[3])


def small(body, rhs, shapes, *operands):
    outs = [jax.ShapeDtypeStruct(s, jnp.float32) for s in shapes]
    return pl.pallas_call(
        functools.partial(body, rhs),
        out_shape=outs,
        compiler_params=pltpu.CompilerParams(vmem_limit_bytes=VMEM_LIMIT),
    )(*operands)


def on_device(total_stars, right_side, points, star_noise):
    rhs, own = right_side.shape
    amplitude = KERNEL_WEIGHT / total_stars
    vector, augmented, spare = (rhs, own), (rhs + SPARE, own), (SPARE, own)

    packed, places = small(
        pack, rhs, [augmented, spare], right_side, points, star_noise[None, :]
    )
    row_points = gather(places, ROUNDS_B)
    pieces, kernel = None, []
    for part in parts_of(packed):
        pieces, high, low = first_product(part, row_points, pieces, rhs, amplitude)
        kernel.append((high, low))
    sums = scatter_sum(pieces, ROUNDS_B)
    (first,) = small(update_one, rhs, [augmented], sums, packed)

    def product(block):
        pieces = None
        for part, (high, low) in zip(parts_of(block), kernel):
            pieces = next_product(part, high, low, pieces, rhs, amplitude)
        return scatter_sum(pieces, ROUNDS_B)

    third, second, scalars = small(
        update_two, rhs, [augmented, vector, spare], product(first), packed, first
    )
    dots, carry = small(
        update_three,
        rhs,
        [spare, (6, rhs, own)],
        product(third),
        packed,
        first,
        second,
        third,
        scalars,
    )
    return tuple(small(update_four, rhs, [vector, vector], all_sum(dots), carry))


def solution(mesh):
    placed = (P(None, AXES), P(None, AXES), P(AXES))

    def whole(right_side, points, star_noise):
        return jax.shard_map(
            functools.partial(on_device, right_side.shape[1]),
            mesh=mesh,
            in_specs=placed,
            out_specs=(P(None, AXES), P(None, AXES)),
            check_vma=False,
        )(right_side, points, star_noise)

    return whole
```

time: 171 us -> 160 us (0.936)
  blocking collectives: 0 us -> 12 us
  waiting for transfers between devices: 49.4 us -> 38 us
  starting transfers between devices: 85.2 us -> 79.5 us
  local copies, waits for them, and re-layouts: 6.69 us -> 2.27 us
    all_to_all x0 -> x1, blocking collectives: none -> 12 us  [all_sum(): block = jnp.sum(lax.all_to_all(copies, 'row', 0, 0), axis=0)]
    ppermute x49 -> x43, waiting for transfers between devices: 49.4 us -> 38 us  [exchange(): return lax.ppermute(value, AXES, pairs)]
    ppermute x49 -> x43, starting transfers between devices: 85.2 us -> 79.5 us  [exchange(): return lax.ppermute(value, AXES, pairs)]
    concatenate x7 -> x4, local copies, waits for them, and re-layouts: 4.38 us -> 0.01 us  [gather(): jnp.concatenate([block] + [exchange(block, axis, m) for m in masks], axis=0)]
    pallas_call x3 -> x12, Pallas kernels: 23.2 us -> 22.6 us  [kernel_call(): pl.pallas_call(body, in_specs=[whole] * len(operands), out_specs=[whole]...]
  transfers between devices with their start and end apart: 49 -> 43, of which waited for: 36 -> 31; matrix products, arithmetic and copies ran while one was open for 3% -> 0% of each run, Pallas kernels for 0% -> 11%
where the time goes in v2:
time: 160 us; the launch traced here: 158 us
  starting transfers between devices  79.5 us (50%)
  waiting for transfers between devices  38 us (24%)
  Pallas kernels  24.6 us (15%)
  blocking collectives  12 us (8%)
  local copies, waits for them, and re-layouts  2.27 us (1%)
    ppermute x43, starting transfers between devices, exchange(): return lax.ppermute(value, AXES, pairs)  79.5 us
    ppermute x43, waiting for transfers between devices, exchange(): return lax.ppermute(value, AXES, pairs)  38 us
    pallas_call x12, Pallas kernels, kernel_call(): pl.pallas_call(body, in_specs=[whole] * len(operands), out_specs=[whole]...  22.6 us
    all_to_all x1, blocking collectives, all_sum(): block = jnp.sum(lax.all_to_all(copies, 'row', 0, 0), axis=0)  12 us
  transfers between devices with their start and end apart: 43, of which 31 were waited for; matrix products, arithmetic and copies ran while one was open for 0% of the time, Pallas kernels for 11%

profile of v2, /device:TPU:1, one launch (start us, length us, event | category | flops | bytes accessed | tf_op | source)
XLA Modules:
  0.0 157.5 jit_solution(4603179847751175543)
XLA Ops:
  2.7 5.2 %collective-permute-start = (f32[72,128]{1,0:T(8,128)S(1)}, f32[72,128]{1,0:T(8,128)S(1)}, u32[]{:S(2)}, u32[]{:S(2)}) collective-permute-start(f32[72,128]{1,0:T(8,128)S(1)} %get-tuple-element.21.packed_ref), channel_id=1, source_target_pairs={{0,48},{1,49},{2,50},{3,51},{4,52},{5,53},{6,54},{7,55},{8,56},{9,... | collective-permute-start | bytes 110600 | tf_op jit(solution)/shard_map/ppermute | solution.py:50
  8.3 4.4 %collective-permute-start.4 = (f32[8,128]{1,0:T(8,128)S(1)}, f32[8,128]{1,0:T(8,128)S(1)}, u32[]{:S(2)}, u32[]{:S(2)}) collective-permute-start(f32[8,128]{1,0:T(8,128)S(1)} %get-tuple-element.22), channel_id=1, source_target_pairs={{0,50},{1,51},{2,48},{3,49},{4,54},{5,55},{6,52},{7,53},{8,58},{9,... | collective-permute-start | bytes 12296 | tf_op jit(solution)/shard_map/ppermute | solution.py:50
  13.7 2.7 %collective-permute-start.5 = (f32[16,128]{1,0:T(8,128)S(1)}, f32[16,128]{1,0:T(8,128)S(1)}, u32[]{:S(2)}, u32[]{:S(2)}) collective-permute-start(f32[16,128]{1,0:T(8,128)S(1)} %get-tuple-element.57), channel_id=1, source_target_pairs={{0,8},{1,9},{2,10},{3,11},{4,12},{5,13},{6,14},{7,15},{8,0},{9,1},... | collective-permute-start | bytes 24584 | tf_op jit(solution)/shard_map/ppermute | solution.py:50
  17.7 2.5 %collective-permute-start.7 = (f32[16,128]{1,0:T(8,128)S(1)}, f32[16,128]{1,0:T(8,128)S(1)}, u32[]{:S(2)}, u32[]{:S(2)}) collective-permute-start(f32[16,128]{1,0:T(8,128)S(1)} %get-tuple-element.57), channel_id=1, source_target_pairs={{0,12},{1,13},{2,14},{3,15},{4,8},{5,9},{6,10},{7,11},{8,4},{9,5},... | collective-permute-start | bytes 24584 | tf_op jit(solution)/shard_map/ppermute | solution.py:50
  21.4 4.7 %collective-permute-start.8 = (f32[64,128]{1,0:T(8,128)S(1)}, f32[64,128]{1,0:T(8,128)S(1)}, u32[]{:S(2)}, u32[]{:S(2)}) collective-permute-start(f32[64,128]{1,0:T(8,128)S(1)} %get-tuple-element.49), channel_id=1, source_target_pairs={{0,1},{1,0},{2,3},{3,2},{4,5},{5,4},{6,7},{7,6},{8,9},{9,8},{10,11... | collective-permute-start | bytes 98312 | tf_op jit(solution)/shard_map/ppermute | solution.py:50
  26.1 3.0 %collective-permute-start.10 = (f32[288,128]{1,0:T(8,128)S(1)}, f32[288,128]{1,0:T(8,128)S(1)}, u32[]{:S(2)}, u32[]{:S(2)}) collective-permute-start(f32[288,128]{1,0:T(8,128)S(1)} %constant_dynamic-update-slice_fusion.refs_0_), channel_id=1, source_target_pairs={{0,128},{1,129},{2,130},{3,131},{4,132},{5,133},{6,134},{7,135},{8... | collective-permute-start | bytes 442376 | tf_op jit(solution)/shard_map/ppermute | solution.py:50
  29.9 4.0 %shard_map.51 = (f32[1152,128]{1,0:T(8,128)S(1)}, bf16[8,512,256]{2,1,0:T(8,128)(2,1)S(1)}, bf16[8,512,256]{2,1,0:T(8,128)(2,1)S(1)}) custom-call(f32[288,128]{1,0:T(8,128)S(1)} %constant_dynamic-update-slice_fusion.refs_0_, f32[128,128]{1,0:T(8,128)S(1)} %constant_dynamic-update-slice_fusion.11.refs_1_.rows_ref), custom_call_target="tpu_custom_call" | custom-call | flops 3221225472 | tf_op jit(solution)/shard_map/pallas_call | solution.py:163
  33.9 4.0 %shard_map.52 = (f32[1152,128]{1,0:T(8,128)S(1)}, bf16[8,512,256]{2,1,0:T(8,128)(2,1)S(1)}, bf16[8,512,256]{2,1,0:T(8,128)(2,1)S(1)}) custom-call(f32[288,128]{1,0:T(8,128)S(1)} %collective-permute-done.10.v_ref, f32[128,128]{1,0:T(8,128)S(1)} %constant_dynamic-update-slice_fusion.11.refs_1_.rows_ref, f32[1152,128]{1,0:T(8,128)S(1)} %get-tuple-element.23.before_ref), custom_call_target="tpu_custom_call" | custom-call | flops 3221225472 | tf_op jit(solution)/shard_map/pallas_call | solution.py:163
  37.9 4.0 %shard_map.53 = (f32[1152,128]{1,0:T(8,128)S(1)}, bf16[8,512,256]{2,1,0:T(8,128)(2,1)S(1)}, bf16[8,512,256]{2,1,0:T(8,128)(2,1)S(1)}) custom-call(f32[288,128]{1,0:T(8,128)S(1)} %collective-permute-done.9.v_ref, f32[128,128]{1,0:T(8,128)S(1)} %constant_dynamic-update-slice_fusion.11.refs_1_.rows_ref, f32[1152,128]{1,0:T(8,128)S(1)} %get-tuple-element.24.before_ref), custom_call_target="tpu_custom_call" | custom-call | flops 3221225472 | tf_op jit(solution)/shard_map/pallas_call | solution.py:163
  41.9 4.0 %shard_map.54 = (f32[1152,128]{1,0:T(8,128)S(1)}, bf16[8,512,256]{2,1,0:T(8,128)(2,1)S(1)}, bf16[8,512,256]{2,1,0:T(8,128)(2,1)S(1)}) custom-call(f32[288,128]{1,0:T(8,128)S(1)} %collective-permute-done.3.v_ref, f32[128,128]{1,0:T(8,128)S(1)} %constant_dynamic-update-slice_fusion.11.refs_1_.rows_ref, f32[1152,128]{1,0:T(8,128)S(1)} %get-tuple-element.25.before_ref), custom_call_target="tpu_custom_call" | custom-call | flops 3221225472 | tf_op jit(solution)/shard_map/pallas_call | solution.py:163
  55.5 3.0 %collective-permute-start.15 = (f32[72,128]{1,0:T(8,128)S(1)}, f32[72,128]{1,0:T(8,128)S(1)}, u32[]{:S(2)}, u32[]{:S(2)}) collective-permute-start(f32[72,128]{1,0:T(8,128)S(1)} %slice.101), channel_id=1, source_target_pairs={{0,50},{1,51},{2,48},{3,49},{4,54},{5,55},{6,52},{7,53},{8,58},{9,... | collective-permute-start | bytes 110600 | tf_op jit(solution)/shard_map/ppermute | solution.py:50
  61.9 2.7 %collective-permute-start.17 = (f32[72,128]{1,0:T(8,128)S(1)}, f32[72,128]{1,0:T(8,128)S(1)}, u32[]{:S(2)}, u32[]{:S(2)}) collective-permute-start(f32[72,128]{1,0:T(8,128)S(1)} %shard_map.55.first_ref), channel_id=1, source_target_pairs={{0,32},{1,33},{2,34},{3,35},{4,36},{5,37},{6,38},{7,39},{8,40},{9,... | collective-permute-start | bytes 110600 | tf_op jit(solution)/shard_map/ppermute | solution.py:50
  67.4 2.9 %collective-permute-start.21 = (f32[288,128]{1,0:T(8,128)S(1)}, f32[288,128]{1,0:T(8,128)S(1)}, u32[]{:S(2)}, u32[]{:S(2)}) collective-permute-start(f32[288,128]{1,0:T(8,128)S(1)} %pad_maximum_fusion.refs_0_), channel_id=1, source_target_pairs={{0,128},{1,129},{2,130},{3,131},{4,132},{5,133},{6,134},{7,135},{8... | collective-permute-start | bytes 442376 | tf_op jit(solution)/shard_map/ppermute | solution.py:50
  76.8 6.7 %collective-permute-start.22 = (f32[576,128]{1,0:T(8,128)S(1)}, f32[576,128]{1,0:T(8,128)S(1)}, u32[]{:S(2)}, u32[]{:S(2)}) collective-permute-start(f32[576,128]{1,0:T(8,128)S(1)} %slice.103), channel_id=1, source_target_pairs={{0,1},{1,0},{2,3},{3,2},{4,5},{5,4},{6,7},{7,6},{8,9},{9,8},{10,11... | collective-permute-start | bytes 884744 | tf_op jit(solution)/shard_map/ppermute | solution.py:50
  86.2 2.0 %collective-permute-start.25 = (f32[144,128]{1,0:T(8,128)S(1)}, f32[144,128]{1,0:T(8,128)S(1)}, u32[]{:S(2)}, u32[]{:S(2)}) collective-permute-start(f32[144,128]{1,0:T(8,128)S(1)} %get-tuple-element.44), channel_id=1, source_target_pairs={{0,12},{1,13},{2,14},{3,15},{4,8},{5,9},{6,10},{7,11},{8,4},{9,5},... | collective-permute-start | bytes 221192 | tf_op jit(solution)/shard_map/ppermute | solution.py:50
  89.6 2.0 %collective-permute-done.25 = f32[144,128]{1,0:T(8,128)S(1)} collective-permute-done((f32[144,128]{1,0:T(8,128)S(1)}, f32[144,128]{1,0:T(8,128)S(1)}, u32[]{:S(2)}, u32[]{:S(2)}) %collective-permute-start.25) | collective-permute-done | bytes 73760 | tf_op jit(solution)/shard_map/ppermute | solution.py:50
  91.6 3.3 %collective-permute-start.26 = (f32[72,128]{1,0:T(8,128)S(1)}, f32[72,128]{1,0:T(8,128)S(1)}, u32[]{:S(2)}, u32[]{:S(2)}) collective-permute-start(f32[72,128]{1,0:T(8,128)S(1)} %slice.109), channel_id=1, source_target_pairs={{0,50},{1,51},{2,48},{3,49},{4,54},{5,55},{6,52},{7,53},{8,58},{9,... | collective-permute-start | bytes 110600 | tf_op jit(solution)/shard_map/ppermute | solution.py:50
  105.2 2.1 %collective-permute-start.30 = (f32[288,128]{1,0:T(8,128)S(1)}, f32[288,128]{1,0:T(8,128)S(1)}, u32[]{:S(2)}, u32[]{:S(2)}) collective-permute-start(f32[288,128]{1,0:T(8,128)S(1)} %constant_dynamic-update-slice_fusion.17.refs_0_), channel_id=1, source_target_pairs={{0,192},{1,193},{2,194},{3,195},{4,196},{5,197},{6,198},{7,199},{8... | collective-permute-start | bytes 442376 | tf_op jit(solution)/shard_map/ppermute | solution.py:50
  110.1 2.4 %collective-permute-done.30.v_ref = f32[288,128]{1,0:T(8,128)S(1)} collective-permute-done((f32[288,128]{1,0:T(8,128)S(1)}, f32[288,128]{1,0:T(8,128)S(1)}, u32[]{:S(2)}, u32[]{:S(2)}) %collective-permute-start.30) | collective-permute-done | bytes 147488 | tf_op jit(solution)/shard_map/ppermute | solution.py:50
  113.3 3.3 %collective-permute-start.33 = (f32[576,128]{1,0:T(8,128)S(1)}, f32[576,128]{1,0:T(8,128)S(1)}, u32[]{:S(2)}, u32[]{:S(2)}) collective-permute-start(f32[576,128]{1,0:T(8,128)S(1)} %slice.111), channel_id=1, source_target_pairs={{0,1},{1,0},{2,3},{3,2},{4,5},{5,4},{6,7},{7,6},{8,9},{9,8},{10,11... | collective-permute-start | bytes 884744 | tf_op jit(solution)/shard_map/ppermute | solution.py:50
  118.1 2.4 %collective-permute-start.35 = (f32[144,128]{1,0:T(8,128)S(1)}, f32[144,128]{1,0:T(8,128)S(1)}, u32[]{:S(2)}, u32[]{:S(2)}) collective-permute-start(f32[144,128]{1,0:T(8,128)S(1)} %get-tuple-element.42), channel_id=1, source_target_pairs={{0,4},{1,5},{2,6},{3,7},{4,0},{5,1},{6,2},{7,3},{8,12},{9,13},{10,... | collective-permute-start | bytes 221192 | tf_op jit(solution)/shard_map/ppermute | solution.py:50
  125.1 3.3 %collective-permute-start.37 = (f32[72,128]{1,0:T(8,128)S(1)}, f32[72,128]{1,0:T(8,128)S(1)}, u32[]{:S(2)}, u32[]{:S(2)}) collective-permute-start(f32[72,128]{1,0:T(8,128)S(1)} %slice.117), channel_id=1, source_target_pairs={{0,50},{1,51},{2,48},{3,49},{4,54},{5,55},{6,52},{7,53},{8,58},{9,... | collective-permute-start | bytes 110600 | tf_op jit(solution)/shard_map/ppermute | solution.py:50
  130.3 12.0 %all_to_all.5 = f32[16,8,128]{2,1,0:T(8,128)S(1)} all-to-all(f32[16,8,128]{2,1,0:T(8,128)S(1)} %broadcast_in_dim.10), channel_id=1, replica_groups=mesh['row'=16,'col'=16] {'row'}, dimensions={0} | all-to-all | bytes 131072 | tf_op jit(solution)/shard_map/all_to_all | solution.py:71
  142.3 4.7 %collective-permute-start.38 = (f32[8,128]{1,0:T(8,128)S(1)}, f32[8,128]{1,0:T(8,128)S(1)}, u32[]{:S(2)}, u32[]{:S(2)}) collective-permute-start(f32[8,128]{1,0:T(8,128)S(1)} %reduce_sum.9), channel_id=1, source_target_pairs={{0,1},{1,0},{2,3},{3,2},{4,5},{5,4},{6,7},{7,6},{8,9},{9,8},{10,11... | collective-permute-start | bytes 12296 | tf_op jit(solution)/shard_map/ppermute | solution.py:50
  (124 shorter events, 65.3 us)
Async XLA Ops:
  2.7 23.4 %collective-permute-start = (f32[72,128]{1,0:T(8,128)S(1)}, f32[72,128]{1,0:T(8,128)S(1)}, u32[]{:S(2)}, u32[]{:S(2)}) collective-permute-start(f32[72,128]{1,0:T(8,128)S(1)} %get-tuple-element.21.packed_ref), channel_id=1, source_target_pairs={{0,48},{1,49},{2,50},{3,51},{4,52},{5,53},{6,54},{7,55},{8,56},{9,... | collective-permute-start | bytes 110600 | tf_op jit(solution)/shard_map/ppermute | solution.py:50
  7.9 18.2 %collective-permute-start.1 = (f32[72,128]{1,0:T(8,128)S(1)}, f32[72,128]{1,0:T(8,128)S(1)}, u32[]{:S(2)}, u32[]{:S(2)}) collective-permute-start(f32[72,128]{1,0:T(8,128)S(1)} %get-tuple-element.21.packed_ref), channel_id=1, source_target_pairs={{0,32},{1,33},{2,34},{3,35},{4,36},{5,37},{6,38},{7,39},{8,40},{9,... | collective-permute-start | bytes 110600 | tf_op jit(solution)/shard_map/ppermute | solution.py:50
  7.9 18.2 %collective-permute-start.2 = (f32[72,128]{1,0:T(8,128)S(1)}, f32[72,128]{1,0:T(8,128)S(1)}, u32[]{:S(2)}, u32[]{:S(2)}) collective-permute-start(f32[72,128]{1,0:T(8,128)S(1)} %get-tuple-element.21.packed_ref), channel_id=1, source_target_pairs={{0,16},{1,17},{2,18},{3,19},{4,20},{5,21},{6,22},{7,23},{8,24},{9,... | collective-permute-start | bytes 110600 | tf_op jit(solution)/shard_map/ppermute | solution.py:50
  8.3 5.4 %collective-permute-start.4 = (f32[8,128]{1,0:T(8,128)S(1)}, f32[8,128]{1,0:T(8,128)S(1)}, u32[]{:S(2)}, u32[]{:S(2)}) collective-permute-start(f32[8,128]{1,0:T(8,128)S(1)} %get-tuple-element.22), channel_id=1, source_target_pairs={{0,50},{1,51},{2,48},{3,49},{4,54},{5,55},{6,52},{7,53},{8,58},{9,... | collective-permute-start | bytes 12296 | tf_op jit(solution)/shard_map/ppermute | solution.py:50
  21.4 8.5 %collective-permute-start.8 = (f32[64,128]{1,0:T(8,128)S(1)}, f32[64,128]{1,0:T(8,128)S(1)}, u32[]{:S(2)}, u32[]{:S(2)}) collective-permute-start(f32[64,128]{1,0:T(8,128)S(1)} %get-tuple-element.49), channel_id=1, source_target_pairs={{0,1},{1,0},{2,3},{3,2},{4,5},{5,4},{6,7},{7,6},{8,9},{9,8},{10,11... | collective-permute-start | bytes 98312 | tf_op jit(solution)/shard_map/ppermute | solution.py:50
  26.1 7.8 %collective-permute-start.10 = (f32[288,128]{1,0:T(8,128)S(1)}, f32[288,128]{1,0:T(8,128)S(1)}, u32[]{:S(2)}, u32[]{:S(2)}) collective-permute-start(f32[288,128]{1,0:T(8,128)S(1)} %constant_dynamic-update-slice_fusion.refs_0_), channel_id=1, source_target_pairs={{0,128},{1,129},{2,130},{3,131},{4,132},{5,133},{6,134},{7,135},{8... | collective-permute-start | bytes 442376 | tf_op jit(solution)/shard_map/ppermute | solution.py:50
  29.1 8.8 %collective-permute-start.9 = (f32[288,128]{1,0:T(8,128)S(1)}, f32[288,128]{1,0:T(8,128)S(1)}, u32[]{:S(2)}, u32[]{:S(2)}) collective-permute-start(f32[288,128]{1,0:T(8,128)S(1)} %constant_dynamic-update-slice_fusion.refs_0_), channel_id=1, source_target_pairs={{0,64},{1,65},{2,66},{3,67},{4,68},{5,69},{6,70},{7,71},{8,72},{9,... | collective-permute-start | bytes 442376 | tf_op jit(solution)/shard_map/ppermute | solution.py:50
  29.5 12.4 %collective-permute-start.3 = (f32[288,128]{1,0:T(8,128)S(1)}, f32[288,128]{1,0:T(8,128)S(1)}, u32[]{:S(2)}, u32[]{:S(2)}) collective-permute-start(f32[288,128]{1,0:T(8,128)S(1)} %constant_dynamic-update-slice_fusion.refs_0_), channel_id=1, source_target_pairs={{0,192},{1,193},{2,194},{3,195},{4,196},{5,197},{6,198},{7,199},{8... | collective-permute-start | bytes 442376 | tf_op jit(solution)/shard_map/ppermute | solution.py:50
  47.9 4.8 %collective-permute-start.12 = (f32[144,128]{1,0:T(8,128)S(1)}, f32[144,128]{1,0:T(8,128)S(1)}, u32[]{:S(2)}, u32[]{:S(2)}) collective-permute-start(f32[144,128]{1,0:T(8,128)S(1)} %get-tuple-element.46), channel_id=1, source_target_pairs={{0,8},{1,9},{2,10},{3,11},{4,12},{5,13},{6,14},{7,15},{8,0},{9,1},... | collective-permute-start | bytes 221192 | tf_op jit(solution)/shard_map/ppermute | solution.py:50
  49.5 5.0 %collective-permute-start.13 = (f32[144,128]{1,0:T(8,128)S(1)}, f32[144,128]{1,0:T(8,128)S(1)}, u32[]{:S(2)}, u32[]{:S(2)}) collective-permute-start(f32[144,128]{1,0:T(8,128)S(1)} %get-tuple-element.48), channel_id=1, source_target_pairs={{0,4},{1,5},{2,6},{3,7},{4,0},{5,1},{6,2},{7,3},{8,12},{9,13},{10,... | collective-permute-start | bytes 221192 | tf_op jit(solution)/shard_map/ppermute | solution.py:50
  60.0 4.9 %collective-permute-start.16 = (f32[72,128]{1,0:T(8,128)S(1)}, f32[72,128]{1,0:T(8,128)S(1)}, u32[]{:S(2)}, u32[]{:S(2)}) collective-permute-start(f32[72,128]{1,0:T(8,128)S(1)} %shard_map.55.first_ref), channel_id=1, source_target_pairs={{0,48},{1,49},{2,50},{3,51},{4,52},{5,53},{6,54},{7,55},{8,56},{9,... | collective-permute-start | bytes 110600 | tf_op jit(solution)/shard_map/ppermute | solution.py:50
  67.4 5.6 %collective-permute-start.21 = (f32[288,128]{1,0:T(8,128)S(1)}, f32[288,128]{1,0:T(8,128)S(1)}, u32[]{:S(2)}, u32[]{:S(2)}) collective-permute-start(f32[288,128]{1,0:T(8,128)S(1)} %pad_maximum_fusion.refs_0_), channel_id=1, source_target_pairs={{0,128},{1,129},{2,130},{3,131},{4,132},{5,133},{6,134},{7,135},{8... | collective-permute-start | bytes 442376 | tf_op jit(solution)/shard_map/ppermute | solution.py:50
  70.7 5.2 %collective-permute-start.19 = (f32[288,128]{1,0:T(8,128)S(1)}, f32[288,128]{1,0:T(8,128)S(1)}, u32[]{:S(2)}, u32[]{:S(2)}) collective-permute-start(f32[288,128]{1,0:T(8,128)S(1)} %pad_maximum_fusion.refs_0_), channel_id=1, source_target_pairs={{0,192},{1,193},{2,194},{3,195},{4,196},{5,197},{6,198},{7,199},{8... | collective-permute-start | bytes 442376 | tf_op jit(solution)/shard_map/ppermute | solution.py:50
  76.8 7.9 %collective-permute-start.22 = (f32[576,128]{1,0:T(8,128)S(1)}, f32[576,128]{1,0:T(8,128)S(1)}, u32[]{:S(2)}, u32[]{:S(2)}) collective-permute-start(f32[576,128]{1,0:T(8,128)S(1)} %slice.103), channel_id=1, source_target_pairs={{0,1},{1,0},{2,3},{3,2},{4,5},{5,4},{6,7},{7,6},{8,9},{9,8},{10,11... | collective-permute-start | bytes 884744 | tf_op jit(solution)/shard_map/ppermute | solution.py:50
  84.8 4.8 %collective-permute-start.23 = (f32[144,128]{1,0:T(8,128)S(1)}, f32[144,128]{1,0:T(8,128)S(1)}, u32[]{:S(2)}, u32[]{:S(2)}) collective-permute-start(f32[144,128]{1,0:T(8,128)S(1)} %get-tuple-element.43), channel_id=1, source_target_pairs={{0,8},{1,9},{2,10},{3,11},{4,12},{5,13},{6,14},{7,15},{8,0},{9,1},... | collective-permute-start | bytes 221192 | tf_op jit(solution)/shard_map/ppermute | solution.py:50
  84.9 4.7 %collective-permute-start.24 = (f32[144,128]{1,0:T(8,128)S(1)}, f32[144,128]{1,0:T(8,128)S(1)}, u32[]{:S(2)}, u32[]{:S(2)}) collective-permute-start(f32[144,128]{1,0:T(8,128)S(1)} %get-tuple-element.45), channel_id=1, source_target_pairs={{0,4},{1,5},{2,6},{3,7},{4,0},{5,1},{6,2},{7,3},{8,12},{9,13},{10,... | collective-permute-start | bytes 221192 | tf_op jit(solution)/shard_map/ppermute | solution.py:50
  86.2 5.4 %collective-permute-start.25 = (f32[144,128]{1,0:T(8,128)S(1)}, f32[144,128]{1,0:T(8,128)S(1)}, u32[]{:S(2)}, u32[]{:S(2)}) collective-permute-start(f32[144,128]{1,0:T(8,128)S(1)} %get-tuple-element.44), channel_id=1, source_target_pairs={{0,12},{1,13},{2,14},{3,15},{4,8},{5,9},{6,10},{7,11},{8,4},{9,5},... | collective-permute-start | bytes 221192 | tf_op jit(solution)/shard_map/ppermute | solution.py:50
  91.6 5.0 %collective-permute-start.26 = (f32[72,128]{1,0:T(8,128)S(1)}, f32[72,128]{1,0:T(8,128)S(1)}, u32[]{:S(2)}, u32[]{:S(2)}) collective-permute-start(f32[72,128]{1,0:T(8,128)S(1)} %slice.109), channel_id=1, source_target_pairs={{0,50},{1,51},{2,48},{3,49},{4,54},{5,55},{6,52},{7,53},{8,58},{9,... | collective-permute-start | bytes 110600 | tf_op jit(solution)/shard_map/ppermute | solution.py:50
  102.8 5.6 %collective-permute-start.32 = (f32[288,128]{1,0:T(8,128)S(1)}, f32[288,128]{1,0:T(8,128)S(1)}, u32[]{:S(2)}, u32[]{:S(2)}) collective-permute-start(f32[288,128]{1,0:T(8,128)S(1)} %constant_dynamic-update-slice_fusion.17.refs_0_), channel_id=1, source_target_pairs={{0,128},{1,129},{2,130},{3,131},{4,132},{5,133},{6,134},{7,135},{8... | collective-permute-start | bytes 442376 | tf_op jit(solution)/shard_map/ppermute | solution.py:50
  104.0 5.2 %collective-permute-start.31 = (f32[288,128]{1,0:T(8,128)S(1)}, f32[288,128]{1,0:T(8,128)S(1)}, u32[]{:S(2)}, u32[]{:S(2)}) collective-permute-start(f32[288,128]{1,0:T(8,128)S(1)} %constant_dynamic-update-slice_fusion.17.refs_0_), channel_id=1, source_target_pairs={{0,64},{1,65},{2,66},{3,67},{4,68},{5,69},{6,70},{7,71},{8,72},{9,... | collective-permute-start | bytes 442376 | tf_op jit(solution)/shard_map/ppermute | solution.py:50
  105.2 7.3 %collective-permute-start.30 = (f32[288,128]{1,0:T(8,128)S(1)}, f32[288,128]{1,0:T(8,128)S(1)}, u32[]{:S(2)}, u32[]{:S(2)}) collective-permute-start(f32[288,128]{1,0:T(8,128)S(1)} %constant_dynamic-update-slice_fusion.17.refs_0_), channel_id=1, source_target_pairs={{0,192},{1,193},{2,194},{3,195},{4,196},{5,197},{6,198},{7,199},{8... | collective-permute-start | bytes 442376 | tf_op jit(solution)/shard_map/ppermute | solution.py:50
  117.9 4.8 %collective-permute-start.34 = (f32[144,128]{1,0:T(8,128)S(1)}, f32[144,128]{1,0:T(8,128)S(1)}, u32[]{:S(2)}, u32[]{:S(2)}) collective-permute-start(f32[144,128]{1,0:T(8,128)S(1)} %get-tuple-element.40), channel_id=1, source_target_pairs={{0,8},{1,9},{2,10},{3,11},{4,12},{5,13},{6,14},{7,15},{8,0},{9,1},... | collective-permute-start | bytes 221192 | tf_op jit(solution)/shard_map/ppermute | solution.py:50
  118.1 6.0 %collective-permute-start.35 = (f32[144,128]{1,0:T(8,128)S(1)}, f32[144,128]{1,0:T(8,128)S(1)}, u32[]{:S(2)}, u32[]{:S(2)}) collective-permute-start(f32[144,128]{1,0:T(8,128)S(1)} %get-tuple-element.42), channel_id=1, source_target_pairs={{0,4},{1,5},{2,6},{3,7},{4,0},{5,1},{6,2},{7,3},{8,12},{9,13},{10,... | collective-permute-start | bytes 221192 | tf_op jit(solution)/shard_map/ppermute | solution.py:50
  142.3 5.5 %collective-permute-start.38 = (f32[8,128]{1,0:T(8,128)S(1)}, f32[8,128]{1,0:T(8,128)S(1)}, u32[]{:S(2)}, u32[]{:S(2)}) collective-permute-start(f32[8,128]{1,0:T(8,128)S(1)} %reduce_sum.9), channel_id=1, source_target_pairs={{0,1},{1,0},{2,3},{3,2},{4,5},{5,4},{6,7},{7,6},{8,9},{9,8},{10,11... | collective-permute-start | bytes 12296 | tf_op jit(solution)/shard_map/ppermute | solution.py:50
  (22 other events, 77.0 us)

commit v3 on v2

v3 whole, which is shorter than its diff:
```python
import functools
import math

import jax
import jax.numpy as jnp
from jax import lax
from jax.experimental import pallas as pl
from jax.experimental.pallas import tpu as pltpu
from jax.sharding import PartitionSpec as P

QUAD_XX = 1.6
QUAD_XY = 0.5
QUAD_YY = 0.7
INVERSE_SQUARE = 25.0
KERNEL_WEIGHT = 2048.0

LOG2E = math.log2(math.e)
PX = math.sqrt(QUAD_XX * INVERSE_SQUARE)
PY = QUAD_XY * INVERSE_SQUARE / PX
QY = math.sqrt(QUAD_YY * INVERSE_SQUARE - PY * PY)
PX, PY, QY = PX * LOG2E, PY * LOG2E, QY * LOG2E

AXES = ("row", "col")
DEVICES = 256
LANES = 128
SPARE = 8
TILE = 256
VMEM_LIMIT = 24 * 1024 * 1024


def place(index):
    row, col = divmod(index, 16)
    y, z_lo = divmod(row, 4)
    x, rest = divmod(col, 4)
    z_hi, core = divmod(rest, 2)
    return {"x": x, "y": y, "z": z_hi * 4 + z_lo, "core": core}


def number(at):
    row = at["y"] * 4 + at["z"] % 4
    return row * 16 + at["x"] * 4 + (at["z"] // 4) * 2 + at["core"]


def groups_along(*axes):
    groups = {}
    for index in range(DEVICES):
        rest = tuple(v for k, v in place(index).items() if k not in axes)
        groups.setdefault(rest, []).append(index)
    return list(groups.values())


PLANES = groups_along("x", "y")
COLUMNS = groups_along("z", "core")


def exchange(value, axis, mask):
    pairs = []
    for index in range(DEVICES):
        at = place(index)
        at[axis] ^= mask
        pairs.append((index, number(at)))
    return lax.ppermute(value, AXES, pairs)


def parts_of(block):
    near = jnp.concatenate([block] + [exchange(block, "z", m) for m in (3, 2, 1)], axis=0)
    far = exchange(near, "z", 7)
    return [near, exchange(near, "core", 1), far, exchange(far, "core", 1)]


def deal(blocks, groups):
    count = len(groups[0])
    rows = blocks.shape[0] // count
    dealt = lax.all_to_all(
        blocks.reshape(count, rows, LANES), AXES, 0, 0, axis_index_groups=groups
    )
    return dealt.reshape(count * rows, LANES)


def all_sum(block):
    for groups in (COLUMNS, PLANES):
        copies = jnp.broadcast_to(block[None], (len(groups[0]),) + block.shape)
        dealt = lax.all_to_all(copies, AXES, 0, 0, axis_index_groups=groups)
        block = jnp.sum(dealt, axis=0)
    return block


def split(vectors):
    high = vectors.astype(jnp.bfloat16)
    low = (vectors - high.astype(jnp.float32)).astype(jnp.bfloat16)
    return high, low


def as_columns(row, rhs):
    return jnp.broadcast_to(row, (LANES, LANES)).T[:rhs, :]


def unpack(v_ref, pair_ref, rhs):
    total = jnp.zeros((SPARE, LANES), jnp.float32)
    step = rhs + SPARE
    for b in range(v_ref.shape[0] // step):
        high, low = split(v_ref[b * step : b * step + rhs, :])
        pair_ref[:rhs, b * LANES : (b + 1) * LANES] = high
        pair_ref[rhs:, b * LANES : (b + 1) * LANES] = low
        total = total + v_ref[b * step + rhs : (b + 1) * step, :]
    return total


def emit(before_ref, out_ref, tile, product, dots, rhs):
    step = rhs + SPARE
    for piece in range(TILE // LANES):
        start = (tile * (TILE // LANES) + piece) * step
        part = product[:, piece * LANES : (piece + 1) * LANES]
        spare = dots
        if before_ref is not None:
            part = part + before_ref[start : start + rhs, :]
            spare = spare + before_ref[start + rhs : start + step, :]
        out_ref[start : start + rhs, :] = part
        out_ref[start + rhs : start + step, :] = spare


def first_body(rhs, amplitude, v_ref, rows_ref, before_ref, out_ref, high_ref, low_ref, pair_ref, p_ref, q_ref):
    step = rhs + SPARE
    tiles, stars, _ = high_ref.shape
    unpack(v_ref, pair_ref, rhs)
    for b in range(stars // LANES):
        x = v_ref[b * step + rhs : b * step + rhs + 1, :]
        y = v_ref[b * step + rhs + 1 : b * step + rhs + 2, :]
        rows = slice(b * LANES, (b + 1) * LANES)
        p_ref[rows, :] = as_columns(PX * x + PY * y, LANES)
        q_ref[rows, :] = as_columns(QY * y, LANES)

    for tile in range(tiles):
        product = jnp.zeros((rhs, TILE), jnp.float32)
        for j in range(0, stars, TILE):
            pieces = []
            for piece in range(TILE // LANES):
                at = (tile * (TILE // LANES) + piece) * SPARE
                x, y = rows_ref[at : at + 1, :], rows_ref[at + 1 : at + 2, :]
                delta_p = p_ref[j : j + TILE, :] - (PX * x + PY * y)
                delta_q = q_ref[j : j + TILE, :] - QY * y
                square = delta_p * delta_p + delta_q * delta_q
                distance = square * lax.rsqrt(jnp.maximum(square, 1e-30))
                pieces.append(split(jnp.exp2(-distance)))
            high = jnp.concatenate([h for h, _ in pieces], axis=1)
            low = jnp.concatenate([l for _, l in pieces], axis=1)
            high_ref[tile, j : j + TILE, :] = high
            low_ref[tile, j : j + TILE, :] = low
            both = jnp.dot(pair_ref[:, j : j + TILE], high, preferred_element_type=jnp.float32)
            rest = jnp.dot(pair_ref[:rhs, j : j + TILE], low, preferred_element_type=jnp.float32)
            product = product + (both[:rhs] + (both[rhs:] + rest))
        emit(before_ref, out_ref, tile, product * amplitude, jnp.zeros((SPARE, LANES), jnp.float32), rhs)


def next_body(rhs, amplitude, v_ref, high_ref, low_ref, before_ref, out_ref, pair_ref):
    dots = unpack(v_ref, pair_ref, rhs)
    for tile in range(high_ref.shape[0]):
        both = jnp.dot(pair_ref[...], high_ref[tile], preferred_element_type=jnp.float32)
        rest = jnp.dot(pair_ref[:rhs, :], low_ref[tile], preferred_element_type=jnp.float32)
        product = (both[:rhs] + (both[rhs:] + rest)) * amplitude
        emit(before_ref, out_ref, tile, product, dots, rhs)


def no_before(body, at, *refs):
    body(*refs[:at], None, *refs[at:])


def kernel_call(body, outs, scratch, flops, operands):
    whole = pl.BlockSpec(memory_space=pltpu.VMEM)
    return pl.pallas_call(
        body,
        in_specs=[whole] * len(operands),
        out_specs=[whole] * len(outs),
        out_shape=outs,
        scratch_shapes=scratch,
        cost_estimate=pl.CostEstimate(flops=flops, bytes_accessed=0, transcendentals=0),
        compiler_params=pltpu.CompilerParams(vmem_limit_bytes=VMEM_LIMIT),
    )(*operands)


def first_product(part, row_points, before, rhs, amplitude):
    columns = part.shape[0] // (rhs + SPARE) * LANES
    pieces = row_points.shape[0] // SPARE
    tiles = pieces * LANES // TILE
    shape = (tiles, columns, TILE)
    outs = [
        jax.ShapeDtypeStruct((pieces * (rhs + SPARE), LANES), jnp.float32),
        jax.ShapeDtypeStruct(shape, jnp.bfloat16),
        jax.ShapeDtypeStruct(shape, jnp.bfloat16),
    ]
    scratch = [
        pltpu.VMEM((2 * rhs, columns), jnp.bfloat16),
        pltpu.VMEM((columns, LANES), jnp.float32),
        pltpu.VMEM((columns, LANES), jnp.float32),
    ]
    body = functools.partial(first_body, rhs, amplitude)
    operands = [part, row_points]
    if before is None:
        body = functools.partial(no_before, body, 2)
    else:
        operands.append(before)
    return kernel_call(body, outs, scratch, 3 << 30, operands)


def next_product(part, high, low, before, rhs, amplitude):
    tiles, columns, _ = high.shape
    outs = [
        jax.ShapeDtypeStruct((tiles * (TILE // LANES) * (rhs + SPARE), LANES), jnp.float32)
    ]
    scratch = [pltpu.VMEM((2 * rhs, columns), jnp.bfloat16)]
    body = functools.partial(next_body, rhs, amplitude)
    operands = [part, high, low]
    if before is None:
        body = functools.partial(no_before, body, 3)
    else:
        operands.append(before)
    return kernel_call(body, outs, scratch, 1 << 30, operands)[0]


def dot(a, b):
    return jnp.sum(a * b, axis=1, keepdims=True)


def to_rows(columns, rhs):
    lane = lax.broadcasted_iota(jnp.int32, (rhs, LANES), 1)
    tile = jnp.zeros((rhs, LANES), jnp.float32)
    for i, column in enumerate(columns):
        tile = jnp.where(lane == i, column, tile)
    square = jnp.concatenate([tile, jnp.zeros((LANES - rhs, LANES), jnp.float32)], axis=0)
    return square.T[:SPARE, :]


def pack(rhs, right_ref, points_ref, noise_ref, out_ref, places_ref):
    spare = jnp.concatenate(
        [points_ref[...], noise_ref[...], jnp.zeros((SPARE - 3, LANES), jnp.float32)], axis=0
    )
    out_ref[:rhs, :] = right_ref[...]
    out_ref[rhs:, :] = spare
    for copy in range(places_ref.shape[0] // SPARE):
        places_ref[copy * SPARE : (copy + 1) * SPARE, :] = spare


def summed(dealt_ref, rhs):
    step = rhs + SPARE
    blocks = [dealt_ref[at : at + step, :] for at in range(0, dealt_ref.shape[0], step)]
    while len(blocks) > 1:
        blocks = [a + b for a, b in zip(blocks[::2], blocks[1::2])]
    return blocks[0][:rhs, :], blocks[0][rhs:, :]


def right_and_noise(packed_ref, rhs):
    return packed_ref[:rhs, :], packed_ref[rhs + 2 : rhs + 3, :]


def update_one(rhs, dealt_ref, packed_ref, out_ref):
    right, noise = right_and_noise(packed_ref, rhs)
    image, _ = summed(dealt_ref, rhs)
    image = image + noise * right
    out_ref[:rhs, :] = image
    out_ref[rhs:, :] = to_rows([dot(right, right), dot(right, image)], rhs)


def update_two(rhs, dealt_ref, packed_ref, first_ref, out_ref, second_ref, scalars_ref):
    right, noise = right_and_noise(packed_ref, rhs)
    w0 = first_ref[:rhs, :]
    image, dots = summed(dealt_ref, rhs)
    n0 = image + noise * w0
    alpha = as_columns(dots[0:1, :] / dots[1:2, :], rhs)
    r1 = right - alpha * w0
    w1 = w0 - alpha * n0
    out_ref[:rhs, :] = w1
    out_ref[rhs:, :] = to_rows([dot(r1, r1), dot(r1, w1)], rhs)
    second_ref[...] = n0
    scalars_ref[...] = dots


def update_three(rhs, dealt_ref, packed_ref, first_ref, second_ref, third_ref, scalars_ref, dots_ref, carry_ref, kept_ref):
    right, noise = right_and_noise(packed_ref, rhs)
    w0 = first_ref[:rhs, :]
    n0 = second_ref[...]
    w1 = third_ref[:rhs, :]
    image, dots = summed(dealt_ref, rhs)
    n1 = image + noise * w1
    norm0, curve0 = scalars_ref[0:1, :], scalars_ref[1:2, :]
    norm1, curve1 = dots[0:1, :], dots[1:2, :]
    alpha0_row = norm0 / curve0
    beta1_row = norm1 / norm0
    alpha1_row = norm1 / (curve1 - beta1_row * norm1 / alpha0_row)
    alpha0, beta1, alpha1 = (as_columns(row, rhs) for row in (alpha0_row, beta1_row, alpha1_row))
    r1 = right - alpha0 * w0
    s1 = w1 + beta1 * w0
    p1 = r1 + beta1 * right
    z1 = n1 + beta1 * n0
    r2 = r1 - alpha1 * s1
    w2 = w1 - alpha1 * z1
    dots_ref[...] = to_rows([dot(r2, r2), dot(r2, w2)], rhs)
    carry_ref[0] = alpha0 * right + alpha1 * p1
    carry_ref[1] = r2
    carry_ref[2] = p1
    carry_ref[3] = s1
    carry_ref[4] = w2
    kept_ref[...] = jnp.concatenate(
        [norm1, alpha1_row, jnp.zeros((SPARE - 2, LANES), jnp.float32)], axis=0
    )


def update_four(rhs, dots_ref, carry_ref, kept_ref, solution_ref, residual_ref):
    norm2, curve2 = dots_ref[0:1, :], dots_ref[1:2, :]
    norm1, alpha1 = kept_ref[0:1, :], kept_ref[1:2, :]
    beta2_row = norm2 / norm1
    alpha2 = as_columns(norm2 / (curve2 - beta2_row * norm2 / alpha1), rhs)
    beta2 = as_columns(beta2_row, rhs)
    r2 = carry_ref[1]
    solution_ref[...] = carry_ref[0] + alpha2 * (r2 + beta2 * carry_ref[2])
    residual_ref[...] = r2 - alpha2 * (carry_ref[4] + beta2 * carry_ref[3])


def small(body, rhs, shapes, *operands):
    outs = [jax.ShapeDtypeStruct(s, jnp.float32) for s in shapes]
    return pl.pallas_call(
        functools.partial(body, rhs),
        out_shape=outs,
        compiler_params=pltpu.CompilerParams(vmem_limit_bytes=VMEM_LIMIT),
    )(*operands)


def on_device(total_stars, right_side, points, star_noise):
    rhs, own = right_side.shape
    amplitude = KERNEL_WEIGHT / total_stars
    vector, augmented, spare = (rhs, own), (rhs + SPARE, own), (SPARE, own)

    packed, places = small(
        pack,
        rhs,
        [augmented, (SPARE * len(PLANES[0]), own)],
        right_side,
        points,
        star_noise[None, :],
    )
    row_points = deal(places, PLANES)
    pieces, kernel = None, []
    for part in parts_of(packed):
        pieces, high, low = first_product(part, row_points, pieces, rhs, amplitude)
        kernel.append((high, low))
    (first,) = small(update_one, rhs, [augmented], deal(pieces, PLANES), packed)

    def product(block):
        pieces = None
        for part, (high, low) in zip(parts_of(block), kernel):
            pieces = next_product(part, high, low, pieces, rhs, amplitude)
        return deal(pieces, PLANES)

    third, second, scalars = small(
        update_two, rhs, [augmented, vector, spare], product(first), packed, first
    )
    dots, carry, kept = small(
        update_three,
        rhs,
        [spare, (5, rhs, own), spare],
        product(third),
        packed,
        first,
        second,
        third,
        scalars,
    )
    return tuple(small(update_four, rhs, [vector, vector], all_sum(dots), carry, kept))


def solution(mesh):
    placed = (P(None, AXES), P(None, AXES), P(AXES))

    def whole(right_side, points, star_noise):
        return jax.shard_map(
            functools.partial(on_device, right_side.shape[1]),
            mesh=mesh,
            in_specs=placed,
            out_specs=(P(None, AXES), P(None, AXES)),
            check_vma=False,
        )(right_side, points, star_noise)

    return whole
```

time: 160 us -> 150 us (0.938); the launches traced: 158 us -> 150 us
  blocking collectives: 12 us -> 72.4 us
  starting transfers between devices: 79.5 us -> 41.6 us
  waiting for transfers between devices: 38 us -> 14.7 us
  Pallas kernels: 24.6 us -> 18.2 us
    all_to_all x1 -> x5, blocking collectives: 12 us -> 72.4 us  [the longest x3 48.7 us: deal(): lax.all_to_all(blocks.reshape(count, rows, LANES), AXES, 0, 0, axis_index...]
    ppermute x43 -> x18, starting transfers between devices: 79.5 us -> 34.9 us  [exchange(): return lax.ppermute(value, AXES, pairs)]
    ppermute x43 -> x18, waiting for transfers between devices: 38 us -> 14.6 us  [exchange(): return lax.ppermute(value, AXES, pairs)]
    all_to_all x0 -> x1, starting transfers between devices: none -> 6.75 us  [deal(): lax.all_to_all(blocks.reshape(count, rows, LANES), AXES, 0, 0, axis_index...]
    pallas_call x12, Pallas kernels: 22.6 us -> 16.2 us  [kernel_call(): pl.pallas_call(body, in_specs=[whole] * len(operands), out_specs=[whole]...]
  transfers between devices with their start and end apart: 43 -> 19, of which waited for: 31 -> 7; matrix products, arithmetic and copies ran while one was open for 0% -> 0% of each run, Pallas kernels for 11% -> 8%
where the time goes in v3:
time: 150 us
  blocking collectives  72.4 us (48%)
  starting transfers between devices  41.6 us (28%)
  Pallas kernels  18.2 us (12%)
  waiting for transfers between devices  14.7 us (10%)
  local copies, waits for them, and re-layouts  2.14 us (1%)
    all_to_all x3, blocking collectives, deal(): lax.all_to_all(blocks.reshape(count, rows, LANES), AXES, 0, 0, axis_index...  48.7 us
    ppermute x18, starting transfers between devices, exchange(): return lax.ppermute(value, AXES, pairs)  34.9 us
    all_to_all x2, blocking collectives, all_sum(): dealt = lax.all_to_all(copies, AXES, 0, 0, axis_index_groups=groups)  23.7 us
    pallas_call x12, Pallas kernels, kernel_call(): pl.pallas_call(body, in_specs=[whole] * len(operands), out_specs=[whole]...  16.2 us
    ppermute x18, waiting for transfers between devices, exchange(): return lax.ppermute(value, AXES, pairs)  14.6 us
    all_to_all x1, starting transfers between devices, deal(): lax.all_to_all(blocks.reshape(count, rows, LANES), AXES, 0, 0, axis_index...  6.75 us
  transfers between devices with their start and end apart: 19, of which 7 were waited for; matrix products, arithmetic and copies ran while one was open for 0% of the time, Pallas kernels for 8%

profile of v3, /device:TPU:1, one launch (start us, length us, event | category | flops | bytes accessed | tf_op | source)
XLA Modules:
  0.0 149.9 jit_solution(71429425602139081)
XLA Ops:
  3.4 5.2 %collective-permute-start = (f32[72,128]{1,0:T(8,128)S(1)}, f32[72,128]{1,0:T(8,128)S(1)}, u32[]{:S(2)}, u32[]{:S(2)}) collective-permute-start(f32[72,128]{1,0:T(8,128)S(1)} %get-tuple-element.22.packed_ref), channel_id=1, source_target_pairs={{0,48},{1,49},{2,50},{3,51},{4,52},{5,53},{6,54},{7,55},{8,56},{9,... | collective-permute-start | bytes 110600 | tf_op jit(solution)/shard_map/ppermute | solution.py:62
  8.8 6.8 %all-to-all-start = ((f32[16,8,128]{2,1,0:T(8,128)}), f32[16,8,128]{2,1,0:T(8,128)S(1)}, u32[]{:S(2)}, u32[]{:S(2)}) async-start(f32[16,8,128]{2,1,0:T(8,128)} %bitcast.1), calls=%async_computation | async-start | bytes 131072 | tf_op jit(solution)/shard_map/all_to_all | solution.py:74
  15.7 1.6 %collective-permute-start.5 = (f32[288,128]{1,0:T(8,128)S(1)}, f32[288,128]{1,0:T(8,128)S(1)}, u32[]{:S(2)}, u32[]{:S(2)}) collective-permute-start(f32[288,128]{1,0:T(8,128)S(1)} %constant_dynamic-update-slice_fusion.refs_0_), channel_id=1, source_target_pairs={{0,1},{1,0},{2,3},{3,2},{4,5},{5,4},{6,7},{7,6},{8,9},{9,8},{10,11... | collective-permute-start | bytes 442376 | tf_op jit(solution)/shard_map/ppermute | solution.py:62
  17.3 4.8 %collective-permute-start.3 = (f32[288,128]{1,0:T(8,128)S(1)}, f32[288,128]{1,0:T(8,128)S(1)}, u32[]{:S(2)}, u32[]{:S(2)}) collective-permute-start(f32[288,128]{1,0:T(8,128)S(1)} %constant_dynamic-update-slice_fusion.refs_0_), channel_id=1, source_target_pairs={{0,50},{1,51},{2,48},{3,49},{4,54},{5,55},{6,52},{7,53},{8,58},{9,... | collective-permute-start | bytes 442376 | tf_op jit(solution)/shard_map/ppermute | solution.py:62
  22.1 2.4 %shard_map.51 = (f32[1152,128]{1,0:T(8,128)S(1)}, bf16[8,512,256]{2,1,0:T(8,128)(2,1)S(1)}, bf16[8,512,256]{2,1,0:T(8,128)(2,1)S(1)}) custom-call(f32[288,128]{1,0:T(8,128)S(1)} %constant_dynamic-update-slice_fusion.refs_0_, f32[128,128]{1,0:T(8,128)S(1)} %bitcast.15), custom_call_target="tpu_custom_call" | custom-call | flops 3221225472 | tf_op jit(solution)/shard_map/pallas_call | solution.py:170
  24.5 4.8 %collective-permute-done.3.v_ref = f32[288,128]{1,0:T(8,128)S(1)} collective-permute-done((f32[288,128]{1,0:T(8,128)S(1)}, f32[288,128]{1,0:T(8,128)S(1)}, u32[]{:S(2)}, u32[]{:S(2)}) %collective-permute-start.3) | collective-permute-done | bytes 147488 | tf_op jit(solution)/shard_map/ppermute | solution.py:62
  29.7 2.4 %shard_map.52 = (f32[1152,128]{1,0:T(8,128)S(1)}, bf16[8,512,256]{2,1,0:T(8,128)(2,1)S(1)}, bf16[8,512,256]{2,1,0:T(8,128)(2,1)S(1)}) custom-call(f32[288,128]{1,0:T(8,128)S(1)} %collective-permute-done.5.v_ref, f32[128,128]{1,0:T(8,128)S(1)} %bitcast.16, f32[1152,128]{1,0:T(8,128)S(1)} %get-tuple-element.24.before_ref), custom_call_target="tpu_custom_call" | custom-call | flops 3221225472 | tf_op jit(solution)/shard_map/pallas_call | solution.py:170
  32.1 2.4 %shard_map.53 = (f32[1152,128]{1,0:T(8,128)S(1)}, bf16[8,512,256]{2,1,0:T(8,128)(2,1)S(1)}, bf16[8,512,256]{2,1,0:T(8,128)(2,1)S(1)}) custom-call(f32[288,128]{1,0:T(8,128)S(1)} %collective-permute-done.3.v_ref, f32[128,128]{1,0:T(8,128)S(1)} %bitcast.17, f32[1152,128]{1,0:T(8,128)S(1)} %get-tuple-element.25.before_ref), custom_call_target="tpu_custom_call" | custom-call | flops 3221225472 | tf_op jit(solution)/shard_map/pallas_call | solution.py:170
  34.5 2.4 %shard_map.54 = (f32[1152,128]{1,0:T(8,128)S(1)}, bf16[8,512,256]{2,1,0:T(8,128)(2,1)S(1)}, bf16[8,512,256]{2,1,0:T(8,128)(2,1)S(1)}) custom-call(f32[288,128]{1,0:T(8,128)S(1)} %collective-permute-done.4.v_ref, f32[128,128]{1,0:T(8,128)S(1)} %bitcast.18, f32[1152,128]{1,0:T(8,128)S(1)} %get-tuple-element.26.before_ref), custom_call_target="tpu_custom_call" | custom-call | flops 3221225472 | tf_op jit(solution)/shard_map/pallas_call | solution.py:170
  36.9 18.5 %all_to_all.30 = f32[16,72,128]{2,1,0:T(8,128)S(1)} all-to-all(f32[16,72,128]{2,1,0:T(8,128)S(1)} %bitcast.14), channel_id=1, replica_groups={{0,4,8,12,64,68,72,76,128,132,136,140,192,196,200,204},{1,5,9,13,65,69,..., dimensions={0} | all-to-all | bytes 1179648 | tf_op jit(solution)/shard_map/all_to_all | solution.py:74
  55.6 2.3 %collective-permute-start.6 = (f32[72,128]{1,0:T(8,128)S(1)}, f32[72,128]{1,0:T(8,128)S(1)}, u32[]{:S(2)}, u32[]{:S(2)}) collective-permute-start(f32[72,128]{1,0:T(8,128)S(1)} %shard_map.55.first_ref), channel_id=1, source_target_pairs={{0,48},{1,49},{2,50},{3,51},{4,52},{5,53},{6,54},{7,55},{8,56},{9,... | collective-permute-start | bytes 110600 | tf_op jit(solution)/shard_map/ppermute | solution.py:62
  61.6 2.8 %collective-permute-start.9 = (f32[288,128]{1,0:T(8,128)S(1)}, f32[288,128]{1,0:T(8,128)S(1)}, u32[]{:S(2)}, u32[]{:S(2)}) collective-permute-start(f32[288,128]{1,0:T(8,128)S(1)} %pad_maximum_fusion.refs_0_), channel_id=1, source_target_pairs={{0,50},{1,51},{2,48},{3,49},{4,54},{5,55},{6,52},{7,53},{8,58},{9,... | collective-permute-start | bytes 442376 | tf_op jit(solution)/shard_map/ppermute | solution.py:62
  64.4 2.9 %collective-permute-start.11 = (f32[288,128]{1,0:T(8,128)S(1)}, f32[288,128]{1,0:T(8,128)S(1)}, u32[]{:S(2)}, u32[]{:S(2)}) collective-permute-start(f32[288,128]{1,0:T(8,128)S(1)} %pad_maximum_fusion.refs_0_), channel_id=1, source_target_pairs={{0,1},{1,0},{2,3},{3,2},{4,5},{5,4},{6,7},{7,6},{8,9},{9,8},{10,11... | collective-permute-start | bytes 442376 | tf_op jit(solution)/shard_map/ppermute | solution.py:62
  68.9 3.5 %collective-permute-start.10 = (f32[288,128]{1,0:T(8,128)S(1)}, f32[288,128]{1,0:T(8,128)S(1)}, u32[]{:S(2)}, u32[]{:S(2)}) collective-permute-start(f32[288,128]{1,0:T(8,128)S(1)} %collective-permute-done.9.v_ref), channel_id=1, source_target_pairs={{0,1},{1,0},{2,3},{3,2},{4,5},{5,4},{6,7},{7,6},{8,9},{9,8},{10,11... | collective-permute-start | bytes 442376 | tf_op jit(solution)/shard_map/ppermute | solution.py:62
  74.9 15.2 %all_to_all.31 = f32[16,72,128]{2,1,0:T(8,128)S(1)} all-to-all(f32[16,72,128]{2,1,0:T(8,128)S(1)} %bitcast.13), channel_id=1, replica_groups={{0,4,8,12,64,68,72,76,128,132,136,140,192,196,200,204},{1,5,9,13,65,69,..., dimensions={0} | all-to-all | bytes 1179648 | tf_op jit(solution)/shard_map/all_to_all | solution.py:74
  90.3 2.0 %collective-permute-start.12 = (f32[72,128]{1,0:T(8,128)S(1)}, f32[72,128]{1,0:T(8,128)S(1)}, u32[]{:S(2)}, u32[]{:S(2)}) collective-permute-start(f32[72,128]{1,0:T(8,128)S(1)} %get-tuple-element.36.third_ref), channel_id=1, source_target_pairs={{0,48},{1,49},{2,50},{3,51},{4,52},{5,53},{6,54},{7,55},{8,56},{9,... | collective-permute-start | bytes 110600 | tf_op jit(solution)/shard_map/ppermute | solution.py:62
  92.4 1.4 collective-permute-start.14
  95.0 1.9 %collective-permute-done.13 = f32[72,128]{1,0:T(8,128)S(1)} collective-permute-done((f32[72,128]{1,0:T(8,128)S(1)}, f32[72,128]{1,0:T(8,128)S(1)}, u32[]{:S(2)}, u32[]{:S(2)}) %collective-permute-start.13) | collective-permute-done | bytes 36896 | tf_op jit(solution)/shard_map/ppermute | solution.py:62
  96.8 2.5 %collective-permute-start.15 = (f32[288,128]{1,0:T(8,128)S(1)}, f32[288,128]{1,0:T(8,128)S(1)}, u32[]{:S(2)}, u32[]{:S(2)}) collective-permute-start(f32[288,128]{1,0:T(8,128)S(1)} %constant_dynamic-update-slice_fusion.4.refs_0_), channel_id=1, source_target_pairs={{0,50},{1,51},{2,48},{3,49},{4,54},{5,55},{6,52},{7,53},{8,58},{9,... | collective-permute-start | bytes 442376 | tf_op jit(solution)/shard_map/ppermute | solution.py:62
  99.3 2.6 %collective-permute-start.17 = (f32[288,128]{1,0:T(8,128)S(1)}, f32[288,128]{1,0:T(8,128)S(1)}, u32[]{:S(2)}, u32[]{:S(2)}) collective-permute-start(f32[288,128]{1,0:T(8,128)S(1)} %constant_dynamic-update-slice_fusion.4.refs_0_), channel_id=1, source_target_pairs={{0,1},{1,0},{2,3},{3,2},{4,5},{5,4},{6,7},{7,6},{8,9},{9,8},{10,11... | collective-permute-start | bytes 442376 | tf_op jit(solution)/shard_map/ppermute | solution.py:62
  102.7 3.7 %collective-permute-done.15.v_ref = f32[288,128]{1,0:T(8,128)S(1)} collective-permute-done((f32[288,128]{1,0:T(8,128)S(1)}, f32[288,128]{1,0:T(8,128)S(1)}, u32[]{:S(2)}, u32[]{:S(2)}) %collective-permute-start.15) | collective-permute-done | bytes 147488 | tf_op jit(solution)/shard_map/ppermute | solution.py:62
  110.1 15.1 %all_to_all.32 = f32[16,72,128]{2,1,0:T(8,128)S(1)} all-to-all(f32[16,72,128]{2,1,0:T(8,128)S(1)} %bitcast.12), channel_id=1, replica_groups={{0,4,8,12,64,68,72,76,128,132,136,140,192,196,200,204},{1,5,9,13,65,69,..., dimensions={0} | all-to-all | bytes 1179648 | tf_op jit(solution)/shard_map/all_to_all | solution.py:74
  125.4 14.3 %all_to_all.33 = f32[16,8,128]{2,1,0:T(8,128)S(1)} all-to-all(f32[16,8,128]{2,1,0:T(8,128)S(1)} %broadcast_in_dim.7), channel_id=1, replica_groups={{0,1,2,3,16,17,18,19,32,33,34,35,48,49,50,51},{4,5,6,7,20,21,22,23,36,3..., dimensions={0} | all-to-all | bytes 131072 | tf_op jit(solution)/shard_map/all_to_all | solution.py:83
  139.8 9.4 %all_to_all.34 = f32[16,8,128]{2,1,0:T(8,128)S(1)} all-to-all(f32[16,8,128]{2,1,0:T(8,128)S(1)} %broadcast_in_dim.8), channel_id=1, replica_groups={{0,4,8,12,64,68,72,76,128,132,136,140,192,196,200,204},{1,5,9,13,65,69,..., dimensions={0} | all-to-all | bytes 131072 | tf_op jit(solution)/shard_map/all_to_all | solution.py:83
  (55 shorter events, 18.4 us)
Async XLA Ops:
  0.6 0.8 copy-start
  1.4 0.7 copy-start.1
  2.1 0.7 copy-start.2
  3.4 12.2 %collective-permute-start = (f32[72,128]{1,0:T(8,128)S(1)}, f32[72,128]{1,0:T(8,128)S(1)}, u32[]{:S(2)}, u32[]{:S(2)}) collective-permute-start(f32[72,128]{1,0:T(8,128)S(1)} %get-tuple-element.22.packed_ref), channel_id=1, source_target_pairs={{0,48},{1,49},{2,50},{3,51},{4,52},{5,53},{6,54},{7,55},{8,56},{9,... | collective-permute-start | bytes 110600 | tf_op jit(solution)/shard_map/ppermute | solution.py:62
  8.5 7.1 %collective-permute-start.1 = (f32[72,128]{1,0:T(8,128)S(1)}, f32[72,128]{1,0:T(8,128)S(1)}, u32[]{:S(2)}, u32[]{:S(2)}) collective-permute-start(f32[72,128]{1,0:T(8,128)S(1)} %get-tuple-element.22.packed_ref), channel_id=1, source_target_pairs={{0,32},{1,33},{2,34},{3,35},{4,36},{5,37},{6,38},{7,39},{8,40},{9,... | collective-permute-start | bytes 110600 | tf_op jit(solution)/shard_map/ppermute | solution.py:62
  8.5 7.1 %collective-permute-start.2 = (f32[72,128]{1,0:T(8,128)S(1)}, f32[72,128]{1,0:T(8,128)S(1)}, u32[]{:S(2)}, u32[]{:S(2)}) collective-permute-start(f32[72,128]{1,0:T(8,128)S(1)} %get-tuple-element.22.packed_ref), channel_id=1, source_target_pairs={{0,16},{1,17},{2,18},{3,19},{4,20},{5,21},{6,22},{7,23},{8,24},{9,... | collective-permute-start | bytes 110600 | tf_op jit(solution)/shard_map/ppermute | solution.py:62
  8.8 13.3 %all-to-all-start = ((f32[16,8,128]{2,1,0:T(8,128)}), f32[16,8,128]{2,1,0:T(8,128)S(1)}, u32[]{:S(2)}, u32[]{:S(2)}) async-start(f32[16,8,128]{2,1,0:T(8,128)} %bitcast.1), calls=%async_computation | async-start | bytes 131072 | tf_op jit(solution)/shard_map/all_to_all | solution.py:74
  15.7 14.1 %collective-permute-start.5 = (f32[288,128]{1,0:T(8,128)S(1)}, f32[288,128]{1,0:T(8,128)S(1)}, u32[]{:S(2)}, u32[]{:S(2)}) collective-permute-start(f32[288,128]{1,0:T(8,128)S(1)} %constant_dynamic-update-slice_fusion.refs_0_), channel_id=1, source_target_pairs={{0,1},{1,0},{2,3},{3,2},{4,5},{5,4},{6,7},{7,6},{8,9},{9,8},{10,11... | collective-permute-start | bytes 442376 | tf_op jit(solution)/shard_map/ppermute | solution.py:62
  17.3 12.0 %collective-permute-start.3 = (f32[288,128]{1,0:T(8,128)S(1)}, f32[288,128]{1,0:T(8,128)S(1)}, u32[]{:S(2)}, u32[]{:S(2)}) collective-permute-start(f32[288,128]{1,0:T(8,128)S(1)} %constant_dynamic-update-slice_fusion.refs_0_), channel_id=1, source_target_pairs={{0,50},{1,51},{2,48},{3,49},{4,54},{5,55},{6,52},{7,53},{8,58},{9,... | collective-permute-start | bytes 442376 | tf_op jit(solution)/shard_map/ppermute | solution.py:62
  29.3 5.2 %collective-permute-start.4 = (f32[288,128]{1,0:T(8,128)S(1)}, f32[288,128]{1,0:T(8,128)S(1)}, u32[]{:S(2)}, u32[]{:S(2)}) collective-permute-start(f32[288,128]{1,0:T(8,128)S(1)} %collective-permute-done.3.v_ref), channel_id=1, source_target_pairs={{0,1},{1,0},{2,3},{3,2},{4,5},{5,4},{6,7},{7,6},{8,9},{9,8},{10,11... | collective-permute-start | bytes 442376 | tf_op jit(solution)/shard_map/ppermute | solution.py:62
  55.6 4.6 %collective-permute-start.6 = (f32[72,128]{1,0:T(8,128)S(1)}, f32[72,128]{1,0:T(8,128)S(1)}, u32[]{:S(2)}, u32[]{:S(2)}) collective-permute-start(f32[72,128]{1,0:T(8,128)S(1)} %shard_map.55.first_ref), channel_id=1, source_target_pairs={{0,48},{1,49},{2,50},{3,51},{4,52},{5,53},{6,54},{7,55},{8,56},{9,... | collective-permute-start | bytes 110600 | tf_op jit(solution)/shard_map/ppermute | solution.py:62
  57.9 3.7 %collective-permute-start.7 = (f32[72,128]{1,0:T(8,128)S(1)}, f32[72,128]{1,0:T(8,128)S(1)}, u32[]{:S(2)}, u32[]{:S(2)}) collective-permute-start(f32[72,128]{1,0:T(8,128)S(1)} %shard_map.55.first_ref), channel_id=1, source_target_pairs={{0,32},{1,33},{2,34},{3,35},{4,36},{5,37},{6,38},{7,39},{8,40},{9,... | collective-permute-start | bytes 110600 | tf_op jit(solution)/shard_map/ppermute | solution.py:62
  57.9 3.7 %collective-permute-start.8 = (f32[72,128]{1,0:T(8,128)S(1)}, f32[72,128]{1,0:T(8,128)S(1)}, u32[]{:S(2)}, u32[]{:S(2)}) collective-permute-start(f32[72,128]{1,0:T(8,128)S(1)} %shard_map.55.first_ref), channel_id=1, source_target_pairs={{0,16},{1,17},{2,18},{3,19},{4,20},{5,21},{6,22},{7,23},{8,24},{9,... | collective-permute-start | bytes 110600 | tf_op jit(solution)/shard_map/ppermute | solution.py:62
  61.6 7.3 %collective-permute-start.9 = (f32[288,128]{1,0:T(8,128)S(1)}, f32[288,128]{1,0:T(8,128)S(1)}, u32[]{:S(2)}, u32[]{:S(2)}) collective-permute-start(f32[288,128]{1,0:T(8,128)S(1)} %pad_maximum_fusion.refs_0_), channel_id=1, source_target_pairs={{0,50},{1,51},{2,48},{3,49},{4,54},{5,55},{6,52},{7,53},{8,58},{9,... | collective-permute-start | bytes 442376 | tf_op jit(solution)/shard_map/ppermute | solution.py:62
  64.4 8.0 %collective-permute-start.11 = (f32[288,128]{1,0:T(8,128)S(1)}, f32[288,128]{1,0:T(8,128)S(1)}, u32[]{:S(2)}, u32[]{:S(2)}) collective-permute-start(f32[288,128]{1,0:T(8,128)S(1)} %pad_maximum_fusion.refs_0_), channel_id=1, source_target_pairs={{0,1},{1,0},{2,3},{3,2},{4,5},{5,4},{6,7},{7,6},{8,9},{9,8},{10,11... | collective-permute-start | bytes 442376 | tf_op jit(solution)/shard_map/ppermute | solution.py:62
  68.9 5.2 %collective-permute-start.10 = (f32[288,128]{1,0:T(8,128)S(1)}, f32[288,128]{1,0:T(8,128)S(1)}, u32[]{:S(2)}, u32[]{:S(2)}) collective-permute-start(f32[288,128]{1,0:T(8,128)S(1)} %collective-permute-done.9.v_ref), channel_id=1, source_target_pairs={{0,1},{1,0},{2,3},{3,2},{4,5},{5,4},{6,7},{7,6},{8,9},{9,8},{10,11... | collective-permute-start | bytes 442376 | tf_op jit(solution)/shard_map/ppermute | solution.py:62
  90.3 4.7 %collective-permute-start.12 = (f32[72,128]{1,0:T(8,128)S(1)}, f32[72,128]{1,0:T(8,128)S(1)}, u32[]{:S(2)}, u32[]{:S(2)}) collective-permute-start(f32[72,128]{1,0:T(8,128)S(1)} %get-tuple-element.36.third_ref), channel_id=1, source_target_pairs={{0,48},{1,49},{2,50},{3,51},{4,52},{5,53},{6,54},{7,55},{8,56},{9,... | collective-permute-start | bytes 110600 | tf_op jit(solution)/shard_map/ppermute | solution.py:62
  92.3 4.6 %collective-permute-start.13 = (f32[72,128]{1,0:T(8,128)S(1)}, f32[72,128]{1,0:T(8,128)S(1)}, u32[]{:S(2)}, u32[]{:S(2)}) collective-permute-start(f32[72,128]{1,0:T(8,128)S(1)} %get-tuple-element.36.third_ref), channel_id=1, source_target_pairs={{0,32},{1,33},{2,34},{3,35},{4,36},{5,37},{6,38},{7,39},{8,40},{9,... | collective-permute-start | bytes 110600 | tf_op jit(solution)/shard_map/ppermute | solution.py:62
  92.4 4.4 %collective-permute-start.14 = (f32[72,128]{1,0:T(8,128)S(1)}, f32[72,128]{1,0:T(8,128)S(1)}, u32[]{:S(2)}, u32[]{:S(2)}) collective-permute-start(f32[72,128]{1,0:T(8,128)S(1)} %get-tuple-element.36.third_ref), channel_id=1, source_target_pairs={{0,16},{1,17},{2,18},{3,19},{4,20},{5,21},{6,22},{7,23},{8,24},{9,... | collective-permute-start | bytes 110600 | tf_op jit(solution)/shard_map/ppermute | solution.py:62
  96.8 9.6 %collective-permute-start.15 = (f32[288,128]{1,0:T(8,128)S(1)}, f32[288,128]{1,0:T(8,128)S(1)}, u32[]{:S(2)}, u32[]{:S(2)}) collective-permute-start(f32[288,128]{1,0:T(8,128)S(1)} %constant_dynamic-update-slice_fusion.4.refs_0_), channel_id=1, source_target_pairs={{0,50},{1,51},{2,48},{3,49},{4,54},{5,55},{6,52},{7,53},{8,58},{9,... | collective-permute-start | bytes 442376 | tf_op jit(solution)/shard_map/ppermute | solution.py:62
  99.3 8.2 %collective-permute-start.17 = (f32[288,128]{1,0:T(8,128)S(1)}, f32[288,128]{1,0:T(8,128)S(1)}, u32[]{:S(2)}, u32[]{:S(2)}) collective-permute-start(f32[288,128]{1,0:T(8,128)S(1)} %constant_dynamic-update-slice_fusion.4.refs_0_), channel_id=1, source_target_pairs={{0,1},{1,0},{2,3},{3,2},{4,5},{5,4},{6,7},{7,6},{8,9},{9,8},{10,11... | collective-permute-start | bytes 442376 | tf_op jit(solution)/shard_map/ppermute | solution.py:62
  106.4 2.8 %collective-permute-start.16 = (f32[288,128]{1,0:T(8,128)S(1)}, f32[288,128]{1,0:T(8,128)S(1)}, u32[]{:S(2)}, u32[]{:S(2)}) collective-permute-start(f32[288,128]{1,0:T(8,128)S(1)} %collective-permute-done.15.v_ref), channel_id=1, source_target_pairs={{0,1},{1,0},{2,3},{3,2},{4,5},{5,4},{6,7},{7,6},{8,9},{9,8},{10,11... | collective-permute-start | bytes 442376 | tf_op jit(solution)/shard_map/ppermute | solution.py:62

commit v4 on v3

--- a/solution.py
+++ b/solution.py
@@ -50,7 +50,10 @@
 
 
 PLANES = groups_along("x", "y")
+LINES = groups_along("z")
 COLUMNS = groups_along("z", "core")
+NEAR = (3, 2, 1)
+BLOCKS = (0,) + NEAR + tuple(7 ^ m for m in (0,) + NEAR)
 
 
 def exchange(value, axis, mask):
@@ -63,7 +66,7 @@
 
 
 def parts_of(block):
-    near = jnp.concatenate([block] + [exchange(block, "z", m) for m in (3, 2, 1)], axis=0)
+    near = jnp.concatenate([block] + [exchange(block, "z", m) for m in NEAR], axis=0)
     far = exchange(near, "z", 7)
     return [near, exchange(near, "core", 1), far, exchange(far, "core", 1)]
 
@@ -78,7 +81,7 @@
 
 
 def all_sum(block):
-    for groups in (COLUMNS, PLANES):
+    for groups in (PLANES, COLUMNS):
         copies = jnp.broadcast_to(block[None], (len(groups[0]),) + block.shape)
         dealt = lax.all_to_all(copies, AXES, 0, 0, axis_index_groups=groups)
         block = jnp.sum(dealt, axis=0)
@@ -95,37 +98,21 @@
     return jnp.broadcast_to(row, (LANES, LANES)).T[:rhs, :]
 
 
-def unpack(v_ref, pair_ref, rhs):
-    total = jnp.zeros((SPARE, LANES), jnp.float32)
-    step = rhs + SPARE
-    for b in range(v_ref.shape[0] // step):
-        high, low = split(v_ref[b * step : b * step + rhs, :])
-        pair_ref[:rhs, b * LANES : (b + 1) * LANES] = high
-        pair_ref[rhs:, b * LANES : (b + 1) * LANES] = low
-        total = total + v_ref[b * step + rhs : (b + 1) * step, :]
-    return total
-
-
-def emit(before_ref, out_ref, tile, product, dots, rhs):
-    step = rhs + SPARE
-    for piece in range(TILE // LANES):
-        start = (tile * (TILE // LANES) + piece) * step
-        part = product[:, piece * LANES : (piece + 1) * LANES]
-        spare = dots
-        if before_ref is not None:
-            part = part + before_ref[start : start + rhs, :]
-            spare = spare + before_ref[start + rhs : start + step, :]
-        out_ref[start : start + rhs, :] = part
-        out_ref[start + rhs : start + step, :] = spare
-
-
-def first_body(rhs, amplitude, v_ref, rows_ref, before_ref, out_ref, high_ref, low_ref, pair_ref, p_ref, q_ref):
+def put_pair(pair_ref, b, block, rhs):
+    high, low = split(block)
+    pair_ref[:rhs, b * LANES : (b + 1) * LANES] = high
+    pair_ref[rhs:, b * LANES : (b + 1) * LANES] = low
+
+
+def first_body(rhs, amplitude, has_before, v_ref, rows_ref, *refs):
+    before_ref, refs = (refs[0], refs[1:]) if has_before else (None, refs)
+    out_ref, high_ref, low_ref, pair_ref, p_ref, q_ref = refs
     step = rhs + SPARE
     tiles, stars, _ = high_ref.shape
-    unpack(v_ref, pair_ref, rhs)
     for b in range(stars // LANES):
-        x = v_ref[b * step + rhs : b * step + rhs + 1, :]
-        y = v_ref[b * step + rhs + 1 : b * step + rhs + 2, :]
+        at = b * step + rhs
+        put_pair(pair_ref, b, v_ref[at - rhs : at, :], rhs)
+        x, y = v_ref[at : at + 1, :], v_ref[at + 1 : at + 2, :]
         rows = slice(b * LANES, (b + 1) * LANES)
         p_ref[rows, :] = as_columns(PX * x + PY * y, LANES)
         q_ref[rows, :] = as_columns(QY * y, LANES)
@@ -149,20 +136,58 @@
             both = jnp.dot(pair_ref[:, j : j + TILE], high, preferred_element_type=jnp.float32)
             rest = jnp.dot(pair_ref[:rhs, j : j + TILE], low, preferred_element_type=jnp.float32)
             product = product + (both[:rhs] + (both[rhs:] + rest))
-        emit(before_ref, out_ref, tile, product * amplitude, jnp.zeros((SPARE, LANES), jnp.float32), rhs)
-
-
-def next_body(rhs, amplitude, v_ref, high_ref, low_ref, before_ref, out_ref, pair_ref):
-    dots = unpack(v_ref, pair_ref, rhs)
-    for tile in range(high_ref.shape[0]):
-        both = jnp.dot(pair_ref[...], high_ref[tile], preferred_element_type=jnp.float32)
-        rest = jnp.dot(pair_ref[:rhs, :], low_ref[tile], preferred_element_type=jnp.float32)
-        product = (both[:rhs] + (both[rhs:] + rest)) * amplitude
-        emit(before_ref, out_ref, tile, product, dots, rhs)
-
-
-def no_before(body, at, *refs):
-    body(*refs[:at], None, *refs[at:])
+        for piece in range(TILE // LANES):
+            at = (tile * (TILE // LANES) + piece) * rhs
+            part = product[:, piece * LANES : (piece + 1) * LANES] * amplitude
+            if has_before:
+                part = part + before_ref[at : at + rhs, :]
+            out_ref[at : at + rhs, :] = part
+
+
+def next_body(rhs, amplitude, has_last, has_before, v_ref, right_near_ref, right_far_ref, *refs):
+    last_ref, scalars_ref, refs = (refs[0], refs[1], refs[2:]) if has_last else (None, None, refs)
+    before_ref, refs = (refs[0], refs[1:]) if has_before else (None, refs)
+    kernel, out_ref, pair_ref = refs[:4], refs[4], refs[5]
+    step = rhs + SPARE
+    z_lo = lax.rem(lax.axis_index("row"), 4)
+    z_hi = lax.rem(lax.div(lax.axis_index("col"), 2), 2)
+    if has_last:
+        alpha = as_columns(scalars_ref[0:1, :] / scalars_ref[1:2, :], rhs)
+    norm = jnp.zeros((rhs, LANES), jnp.float32)
+    curve = jnp.zeros((rhs, LANES), jnp.float32)
+    half = len(BLOCKS) // 2
+    for b, mask in enumerate(BLOCKS):
+        lo, hi = lax.bitwise_xor(z_lo, mask % 4), lax.bitwise_xor(z_hi, mask // 4)
+        at = pl.multiple_of((lo * 2 + hi) * rhs, rhs)
+        block = v_ref[pl.ds(at, rhs), :]
+        put_pair(pair_ref, b, block, rhs)
+        right_ref = right_near_ref if b < half else right_far_ref
+        residual = right_ref[b % half * step : b % half * step + rhs, :]
+        if has_last:
+            residual = residual - alpha * last_ref[pl.ds(at, rhs), :]
+        norm = norm + residual * residual
+        curve = curve + residual * block
+    ones = jnp.ones((rhs, LANES), jnp.float32)
+    dots = to_rows([dot(norm, ones), dot(curve, ones)], rhs)
+    if has_before:
+        dots = dots + before_ref[rhs:step, :]
+
+    columns = half * LANES
+    for tile in range(kernel[0].shape[0]):
+        product = jnp.zeros((rhs, TILE), jnp.float32)
+        for part in range(2):
+            cut = slice(part * columns, (part + 1) * columns)
+            high, low = kernel[2 * part][tile], kernel[2 * part + 1][tile]
+            both = jnp.dot(pair_ref[:, cut], high, preferred_element_type=jnp.float32)
+            rest = jnp.dot(pair_ref[:rhs, cut], low, preferred_element_type=jnp.float32)
+            product = product + (both[:rhs] + (both[rhs:] + rest))
+        for piece in range(TILE // LANES):
+            at = (tile * (TILE // LANES) + piece) * step
+            part = product[:, piece * LANES : (piece + 1) * LANES] * amplitude
+            if has_before:
+                part = part + before_ref[at : at + rhs, :]
+            out_ref[at : at + rhs, :] = part
+            out_ref[at + rhs : at + step, :] = dots
 
 
 def kernel_call(body, outs, scratch, flops, operands):
@@ -181,10 +206,9 @@
 def first_product(part, row_points, before, rhs, amplitude):
     columns = part.shape[0] // (rhs + SPARE) * LANES
     pieces = row_points.shape[0] // SPARE
-    tiles = pieces * LANES // TILE
-    shape = (tiles, columns, TILE)
+    shape = (pieces * LANES // TILE, columns, TILE)
     outs = [
-        jax.ShapeDtypeStruct((pieces * (rhs + SPARE), LANES), jnp.float32),
+        jax.ShapeDtypeStruct((pieces * rhs, LANES), jnp.float32),
         jax.ShapeDtypeStruct(shape, jnp.bfloat16),
         jax.ShapeDtypeStruct(shape, jnp.bfloat16),
     ]
@@ -193,28 +217,22 @@
         pltpu.VMEM((columns, LANES), jnp.float32),
         pltpu.VMEM((columns, LANES), jnp.float32),
     ]
-    body = functools.partial(first_body, rhs, amplitude)
-    operands = [part, row_points]
-    if before is None:
-        body = functools.partial(no_before, body, 2)
-    else:
-        operands.append(before)
+    operands = [part, row_points] + ([] if before is None else [before])
+    body = functools.partial(first_body, rhs, amplitude, before is not None)
     return kernel_call(body, outs, scratch, 3 << 30, operands)
 
 
-def next_product(part, high, low, before, rhs, amplitude):
-    tiles, columns, _ = high.shape
-    outs = [
-        jax.ShapeDtypeStruct((tiles * (TILE // LANES) * (rhs + SPARE), LANES), jnp.float32)
-    ]
-    scratch = [pltpu.VMEM((2 * rhs, columns), jnp.bfloat16)]
-    body = functools.partial(next_body, rhs, amplitude)
-    operands = [part, high, low]
-    if before is None:
-        body = functools.partial(no_before, body, 3)
-    else:
-        operands.append(before)
-    return kernel_call(body, outs, scratch, 1 << 30, operands)[0]
+def next_product(vectors, rights, last, scalars, before, kernels, rhs, amplitude):
+    tiles, columns, _ = kernels[0][0].shape
+    rows = tiles * (TILE // LANES) * (rhs + SPARE)
+    outs = [jax.ShapeDtypeStruct((rows, LANES), jnp.float32)]
+    scratch = [pltpu.VMEM((2 * rhs, 2 * columns), jnp.bfloat16)]
+    operands = [vectors, *rights]
+    operands += [] if last is None else [last, scalars]
+    operands += [] if before is None else [before]
+    operands += [half for kernel in kernels for half in kernel]
+    body = functools.partial(next_body, rhs, amplitude, last is not None, before is not None)
+    return kernel_call(body, outs, scratch, 1 << 31, operands)[0]
 
 
 def dot(a, b):
@@ -230,46 +248,69 @@
     return square.T[:SPARE, :]
 
 
-def pack(rhs, right_ref, points_ref, noise_ref, out_ref, places_ref):
-    spare = jnp.concatenate(
-        [points_ref[...], noise_ref[...], jnp.zeros((SPARE - 3, LANES), jnp.float32)], axis=0
-    )
-    out_ref[:rhs, :] = right_ref[...]
+def pack(rhs, right_ref, points_ref, noise_ref, out_ref, places_ref, spare_ref, semaphores):
+    spare_ref[...] = jnp.zeros_like(spare_ref)
+    copies = [
+        pltpu.make_async_copy(right_ref, out_ref.at[pl.ds(0, rhs), :], semaphores.at[0]),
+        pltpu.make_async_copy(points_ref, spare_ref.at[pl.ds(0, 2), :], semaphores.at[1]),
+        pltpu.make_async_copy(noise_ref, spare_ref.at[pl.ds(2, 1), :], semaphores.at[2]),
+    ]
+    for copy in copies:
+        copy.start()
+    for copy in copies:
+        copy.wait()
+    spare = spare_ref[...]
     out_ref[rhs:, :] = spare
-    for copy in range(places_ref.shape[0] // SPARE):
-        places_ref[copy * SPARE : (copy + 1) * SPARE, :] = spare
-
-
-def summed(dealt_ref, rhs):
-    step = rhs + SPARE
+    for at in range(0, places_ref.shape[0], SPARE):
+        places_ref[at : at + SPARE, :] = spare
+
+
+def packed_inputs(right_side, points, noise):
+    rhs, own = right_side.shape
+    anywhere, whole = pl.BlockSpec(memory_space=pl.ANY), pl.BlockSpec(memory_space=pltpu.VMEM)
+    return pl.pallas_call(
+        functools.partial(pack, rhs),
+        in_specs=[anywhere] * 3,
+        out_specs=[whole] * 2,
+        out_shape=[
+            jax.ShapeDtypeStruct((rhs + SPARE, own), jnp.float32),
+            jax.ShapeDtypeStruct((SPARE * len(PLANES[0]), own), jnp.float32),
+        ],
+        scratch_shapes=[pltpu.VMEM((SPARE, own), jnp.float32), pltpu.SemaphoreType.DMA((3,))],
+        compiler_params=pltpu.CompilerParams(vmem_limit_bytes=60 * 1024 * 1024),
+    )(right_side, points, noise)
+
+
+def summed(dealt_ref, step):
     blocks = [dealt_ref[at : at + step, :] for at in range(0, dealt_ref.shape[0], step)]
     while len(blocks) > 1:
         blocks = [a + b for a, b in zip(blocks[::2], blocks[1::2])]
-    return blocks[0][:rhs, :], blocks[0][rhs:, :]
+    return blocks[0]
 
 
 def right_and_noise(packed_ref, rhs):
     return packed_ref[:rhs, :], packed_ref[rhs + 2 : rhs + 3, :]
 
 
-def update_one(rhs, dealt_ref, packed_ref, out_ref):
+def copy_out(copies_ref, vectors):
+    rows = vectors.shape[0]
+    for at in range(0, copies_ref.shape[0], rows):
+        copies_ref[at : at + rows, :] = vectors
+
+
+def update_one(rhs, dealt_ref, packed_ref, copies_ref):
     right, noise = right_and_noise(packed_ref, rhs)
-    image, _ = summed(dealt_ref, rhs)
-    image = image + noise * right
-    out_ref[:rhs, :] = image
-    out_ref[rhs:, :] = to_rows([dot(right, right), dot(right, image)], rhs)
-
-
-def update_two(rhs, dealt_ref, packed_ref, first_ref, out_ref, second_ref, scalars_ref):
+    copy_out(copies_ref, summed(dealt_ref, rhs) + noise * right)
+
+
+def update_two(rhs, dealt_ref, packed_ref, first_ref, copies_ref, second_ref, scalars_ref):
     right, noise = right_and_noise(packed_ref, rhs)
     w0 = first_ref[:rhs, :]
-    image, dots = summed(dealt_ref, rhs)
-    n0 = image + noise * w0
+    image = summed(dealt_ref, rhs + SPARE)
+    dots = image[rhs:, :]
+    n0 = image[:rhs, :] + noise * w0
     alpha = as_columns(dots[0:1, :] / dots[1:2, :], rhs)
-    r1 = right - alpha * w0
-    w1 = w0 - alpha * n0
-    out_ref[:rhs, :] = w1
-    out_ref[rhs:, :] = to_rows([dot(r1, r1), dot(r1, w1)], rhs)
+    copy_out(copies_ref, w0 - alpha * n0)
     second_ref[...] = n0
     scalars_ref[...] = dots
 
@@ -279,8 +320,9 @@
     w0 = first_ref[:rhs, :]
     n0 = second_ref[...]
     w1 = third_ref[:rhs, :]
-    image, dots = summed(dealt_ref, rhs)
-    n1 = image + noise * w1
+    image = summed(dealt_ref, rhs + SPARE)
+    dots = image[rhs:, :]
+    n1 = image[:rhs, :] + noise * w1
     norm0, curve0 = scalars_ref[0:1, :], scalars_ref[1:2, :]
     norm1, curve1 = dots[0:1, :], dots[1:2, :]
     alpha0_row = norm0 / curve0
@@ -327,37 +369,37 @@
 def on_device(total_stars, right_side, points, star_noise):
     rhs, own = right_side.shape
     amplitude = KERNEL_WEIGHT / total_stars
-    vector, augmented, spare = (rhs, own), (rhs + SPARE, own), (SPARE, own)
-
-    packed, places = small(
-        pack,
-        rhs,
-        [augmented, (SPARE * len(PLANES[0]), own)],
-        right_side,
-        points,
-        star_noise[None, :],
+    vector, spare, copies = (rhs, own), (SPARE, own), (rhs * len(BLOCKS), own)
+
+    packed, places = packed_inputs(right_side, points, star_noise[None, :])
+    row_points = deal(places, PLANES)
+    rights = parts_of(packed)
+    pieces, kernels = None, []
+    for part in rights:
+        pieces, high, low = first_product(part, row_points, pieces, rhs, amplitude)
+        kernels.append((high, low))
+    (first,) = small(update_one, rhs, [copies], deal(pieces, PLANES), packed)
+
+    def product(vectors, lasts, scalars):
+        mine = deal(vectors, LINES)
+        other = exchange(mine, "core", 1)
+        pieces = None
+        for n, part in enumerate((mine, other)):
+            pieces = next_product(
+                part, rights[n::2], lasts[n], scalars, pieces, kernels[n::2], rhs, amplitude
+            )
+        return deal(pieces, PLANES), (mine, other)
+
+    dealt, gathered = product(first, (None, None), None)
+    third, second, scalars = small(
+        update_two, rhs, [copies, vector, spare], dealt, packed, first
     )
-    row_points = deal(places, PLANES)
-    pieces, kernel = None, []
-    for part in parts_of(packed):
-        pieces, high, low = first_product(part, row_points, pieces, rhs, amplitude)
-        kernel.append((high, low))
-    (first,) = small(update_one, rhs, [augmented], deal(pieces, PLANES), packed)
-
-    def product(block):
-        pieces = None
-        for part, (high, low) in zip(parts_of(block), kernel):
-            pieces = next_product(part, high, low, pieces, rhs, amplitude)
-        return deal(pieces, PLANES)
-
-    third, second, scalars = small(
-        update_two, rhs, [augmented, vector, spare], product(first), packed, first
-    )
+    dealt, _ = product(third, gathered, scalars)
     dots, carry, kept = small(
         update_three,
         rhs,
         [spare, (5, rhs, own), spare],
-        product(third),
+        dealt,
         packed,
         first,
         second,

time: 150 us -> 146 us (0.973)
  blocking collectives: 72.4 us -> 95.7 us
  starting transfers between devices: 41.6 us -> 25.4 us
  waiting for transfers between devices: 14.7 us -> 4.71 us
    all_to_all x3 -> x5, blocking collectives: 48.7 us -> 71.7 us  [deal(): lax.all_to_all(blocks.reshape(count, rows, LANES), AXES, 0, 0, axis_index...]
    ppermute x18 -> x8, starting transfers between devices: 34.9 us -> 18.6 us  [exchange(): return lax.ppermute(value, AXES, pairs)]
    ppermute x18 -> x8, waiting for transfers between devices: 14.6 us -> 4.71 us  [exchange(): return lax.ppermute(value, AXES, pairs)]
    pallas_call x12 -> x8, Pallas kernels: 16.2 us -> 15.8 us  [kernel_call(): pl.pallas_call(body, in_specs=[whole] * len(operands), out_specs=[whole]...]
  transfers between devices with their start and end apart: 19 -> 9, of which waited for: 7 -> 1; matrix products, arithmetic and copies ran while one was open for 0% -> 1% of each run, Pallas kernels for 8% -> 7%
where the time goes in v4:
time: 146 us
  blocking collectives  95.7 us (66%)
  starting transfers between devices  25.4 us (17%)
  Pallas kernels  18.4 us (13%)
  waiting for transfers between devices  4.71 us (3%)
    all_to_all x5, blocking collectives, deal(): lax.all_to_all(blocks.reshape(count, rows, LANES), AXES, 0, 0, axis_index...  71.7 us
    all_to_all x2, blocking collectives, all_sum(): dealt = lax.all_to_all(copies, AXES, 0, 0, axis_index_groups=groups)  24.1 us
    ppermute x8, starting transfers between devices, exchange(): return lax.ppermute(value, AXES, pairs)  18.6 us
    pallas_call x8, Pallas kernels, kernel_call(): pl.pallas_call(body, in_specs=[whole] * len(operands), out_specs=[whole]...  15.8 us
    all_to_all x1, starting transfers between devices, deal(): lax.all_to_all(blocks.reshape(count, rows, LANES), AXES, 0, 0, axis_index...  6.76 us
    ppermute x8, waiting for transfers between devices, exchange(): return lax.ppermute(value, AXES, pairs)  4.71 us
  transfers between devices with their start and end apart: 9, of which 1 were waited for; matrix products, arithmetic and copies ran while one was open for 1% of the time, Pallas kernels for 7%

profile of v4, /device:TPU:1, one launch (start us, length us, event | category | flops | bytes accessed | tf_op | source)
XLA Modules:
  0.0 145.8 jit_solution(17556139468726788389)
XLA Ops:
  0.6 1.4 shard_map.50
  2.1 2.6 %collective-permute-start.2 = (f32[72,128]{1,0:T(8,128)}, f32[72,128]{1,0:T(8,128)S(1)}, u32[]{:S(2)}, u32[]{:S(2)}) collective-permute-start(f32[72,128]{1,0:T(8,128)} %get-tuple-element.22.packed_ref), channel_id=1, source_target_pairs={{0,16},{1,17},{2,18},{3,19},{4,20},{5,21},{6,22},{7,23},{8,24},{9,... | collective-permute-start | bytes 110600 | tf_op jit(solution)/shard_map/ppermute | solution.py:65
  4.6 3.0 %collective-permute-start.1 = (f32[72,128]{1,0:T(8,128)}, f32[72,128]{1,0:T(8,128)S(1)}, u32[]{:S(2)}, u32[]{:S(2)}) collective-permute-start(f32[72,128]{1,0:T(8,128)} %get-tuple-element.22.packed_ref), channel_id=1, source_target_pairs={{0,32},{1,33},{2,34},{3,35},{4,36},{5,37},{6,38},{7,39},{8,40},{9,... | collective-permute-start | bytes 110600 | tf_op jit(solution)/shard_map/ppermute | solution.py:65
  7.6 6.8 %all-to-all-start = ((f32[16,8,128]{2,1,0:T(8,128)}), f32[16,8,128]{2,1,0:T(8,128)S(1)}, u32[]{:S(2)}, u32[]{:S(2)}) async-start(f32[16,8,128]{2,1,0:T(8,128)} %bitcast.30), calls=%async_computation | async-start | bytes 131072 | tf_op jit(solution)/shard_map/all_to_all | solution.py:77
  15.2 1.6 %collective-permute-start.5 = (f32[288,128]{1,0:T(8,128)S(1)}, f32[288,128]{1,0:T(8,128)S(1)}, u32[]{:S(2)}, u32[]{:S(2)}) collective-permute-start(f32[288,128]{1,0:T(8,128)S(1)} %constant_dynamic-update-slice_fusion.v_ref.right_near_ref), channel_id=1, source_target_pairs={{0,1},{1,0},{2,3},{3,2},{4,5},{5,4},{6,7},{7,6},{8,9},{9,8},{10,11... | collective-permute-start | bytes 442376 | tf_op jit(solution)/shard_map/ppermute | solution.py:65
  16.8 4.8 %collective-permute-start.3 = (f32[288,128]{1,0:T(8,128)S(1)}, f32[288,128]{1,0:T(8,128)S(1)}, u32[]{:S(2)}, u32[]{:S(2)}) collective-permute-start(f32[288,128]{1,0:T(8,128)S(1)} %constant_dynamic-update-slice_fusion.v_ref.right_near_ref), channel_id=1, source_target_pairs={{0,50},{1,51},{2,48},{3,49},{4,54},{5,55},{6,52},{7,53},{8,58},{9,... | collective-permute-start | bytes 442376 | tf_op jit(solution)/shard_map/ppermute | solution.py:65
  21.6 2.4 %shard_map.51 = (f32[1024,128]{1,0:T(8,128)S(1)}, bf16[8,512,256]{2,1,0:T(8,128)(2,1)S(1)}, bf16[8,512,256]{2,1,0:T(8,128)(2,1)S(1)}) custom-call(f32[288,128]{1,0:T(8,128)S(1)} %constant_dynamic-update-slice_fusion.v_ref.right_near_ref, f32[128,128]{1,0:T(8,128)S(1)} %bitcast.26), custom_call_target="tpu_custom_call" | custom-call | flops 3221225472 | tf_op jit(solution)/shard_map/pallas_call | solution.py:195
  24.0 4.7 %collective-permute-done.3.v_ref.right_far_ref = f32[288,128]{1,0:T(8,128)S(1)} collective-permute-done((f32[288,128]{1,0:T(8,128)S(1)}, f32[288,128]{1,0:T(8,128)S(1)}, u32[]{:S(2)}, u32[]{:S(2)}) %collective-permute-start.3) | collective-permute-done | bytes 147488 | tf_op jit(solution)/shard_map/ppermute | solution.py:65
  29.1 2.4 %shard_map.52 = (f32[1024,128]{1,0:T(8,128)S(1)}, bf16[8,512,256]{2,1,0:T(8,128)(2,1)S(1)}, bf16[8,512,256]{2,1,0:T(8,128)(2,1)S(1)}) custom-call(f32[288,128]{1,0:T(8,128)S(1)} %collective-permute-done.5.v_ref.right_near_ref, f32[128,128]{1,0:T(8,128)S(1)} %bitcast.27, f32[1024,128]{1,0:T(8,128)S(1)} %get-tuple-element.24.refs_0_), custom_call_target="tpu_custom_call" | custom-call | flops 3221225472 | tf_op jit(solution)/shard_map/pallas_call | solution.py:195
  31.5 2.4 %shard_map.53 = (f32[1024,128]{1,0:T(8,128)S(1)}, bf16[8,512,256]{2,1,0:T(8,128)(2,1)S(1)}, bf16[8,512,256]{2,1,0:T(8,128)(2,1)S(1)}) custom-call(f32[288,128]{1,0:T(8,128)S(1)} %collective-permute-done.3.v_ref.right_far_ref, f32[128,128]{1,0:T(8,128)S(1)} %bitcast.28, f32[1024,128]{1,0:T(8,128)S(1)} %get-tuple-element.25.refs_0_), custom_call_target="tpu_custom_call" | custom-call | flops 3221225472 | tf_op jit(solution)/shard_map/pallas_call | solution.py:195
  33.9 2.4 %shard_map.54 = (f32[1024,128]{1,0:T(8,128)S(1)}, bf16[8,512,256]{2,1,0:T(8,128)(2,1)S(1)}, bf16[8,512,256]{2,1,0:T(8,128)(2,1)S(1)}) custom-call(f32[288,128]{1,0:T(8,128)S(1)} %collective-permute-done.4.v_ref.right_far_ref, f32[128,128]{1,0:T(8,128)S(1)} %bitcast.29, f32[1024,128]{1,0:T(8,128)S(1)} %get-tuple-element.26.refs_0_), custom_call_target="tpu_custom_call" | custom-call | flops 3221225472 | tf_op jit(solution)/shard_map/pallas_call | solution.py:195
  36.3 17.8 %all_to_all.40 = f32[16,64,128]{2,1,0:T(8,128)S(1)} all-to-all(f32[16,64,128]{2,1,0:T(8,128)S(1)} %bitcast.25), channel_id=1, replica_groups={{0,4,8,12,64,68,72,76,128,132,136,140,192,196,200,204},{1,5,9,13,65,69,..., dimensions={0} | all-to-all | bytes 1048576 | tf_op jit(solution)/shard_map/all_to_all | solution.py:77
  54.1 12.7 %all_to_all.41 = f32[8,64,128]{2,1,0:T(8,128)S(1)} all-to-all(f32[8,64,128]{2,1,0:T(8,128)S(1)} %bitcast.13), channel_id=1, replica_groups={{0,2,16,18,32,34,48,50},{1,3,17,19,33,35,49,51},{4,6,20,22,36,38,52,54}..., dimensions={0} | all-to-all | bytes 524288 | tf_op jit(solution)/shard_map/all_to_all | solution.py:77
  66.9 3.2 %collective-permute-start.6 = (f32[512,128]{1,0:T(8,128)S(1)}, f32[512,128]{1,0:T(8,128)S(1)}, u32[]{:S(2)}, u32[]{:S(2)}) collective-permute-start(f32[512,128]{1,0:T(8,128)S(1)} %bitcast.16), channel_id=1, source_target_pairs={{0,1},{1,0},{2,3},{3,2},{4,5},{5,4},{6,7},{7,6},{8,9},{9,8},{10,11... | collective-permute-start | bytes 786440 | tf_op jit(solution)/shard_map/ppermute | solution.py:65
  70.0 1.5 %shard_map.56.refs_0_ = f32[1152,128]{1,0:T(8,128)S(1)} custom-call(f32[512,128]{1,0:T(8,128)S(1)} %bitcast.17, f32[288,128]{1,0:T(8,128)S(1)} %constant_dynamic-update-slice_fusion.v_ref.right_near_ref, f32[288,128]{1,0:T(8,128)S(1)} %collective-permute-done.3.v_ref.right_far_ref, bf16[8,512,256]{2,1,0:T(8,128)(2,1)S(1)} %get-tuple-element.28.refs_0_.refs_2_, ...), custom_call_target="tpu_custom_call" | custom-call | flops 2147483648 | tf_op jit(solution)/shard_map/pallas_call | solution.py:195
  71.6 1.6 %shard_map.57 = f32[1152,128]{1,0:T(8,128)S(1)} custom-call(f32[512,128]{1,0:T(8,128)S(1)} %collective-permute-done.6.v_ref.refs_0_, f32[288,128]{1,0:T(8,128)S(1)} %collective-permute-done.5.v_ref.right_near_ref, f32[288,128]{1,0:T(8,128)S(1)} %collective-permute-done.4.v_ref.right_far_ref, f32[1152,128]{1,0:T(8,128)S(1)} %shard_map.56.refs_0_, ...), custom_call_target="tpu_custom_call" | custom-call | flops 2147483648 | tf_op jit(solution)/shard_map/pallas_call | solution.py:195
  73.2 15.0 %all_to_all.42 = f32[16,72,128]{2,1,0:T(8,128)S(1)} all-to-all(f32[16,72,128]{2,1,0:T(8,128)S(1)} %bitcast.15), channel_id=1, replica_groups={{0,4,8,12,64,68,72,76,128,132,136,140,192,196,200,204},{1,5,9,13,65,69,..., dimensions={0} | all-to-all | bytes 1179648 | tf_op jit(solution)/shard_map/all_to_all | solution.py:77
  88.3 11.2 %all_to_all.43 = f32[8,64,128]{2,1,0:T(8,128)S(1)} all-to-all(f32[8,64,128]{2,1,0:T(8,128)S(1)} %bitcast.24), channel_id=1, replica_groups={{0,2,16,18,32,34,48,50},{1,3,17,19,33,35,49,51},{4,6,20,22,36,38,52,54}..., dimensions={0} | all-to-all | bytes 524288 | tf_op jit(solution)/shard_map/all_to_all | solution.py:77
  99.5 3.1 %collective-permute-start.7 = (f32[512,128]{1,0:T(8,128)S(1)}, f32[512,128]{1,0:T(8,128)S(1)}, u32[]{:S(2)}, u32[]{:S(2)}) collective-permute-start(f32[512,128]{1,0:T(8,128)S(1)} %bitcast.22), channel_id=1, source_target_pairs={{0,1},{1,0},{2,3},{3,2},{4,5},{5,4},{6,7},{7,6},{8,9},{9,8},{10,11... | collective-permute-start | bytes 786440 | tf_op jit(solution)/shard_map/ppermute | solution.py:65
  102.6 1.6 %shard_map.59.refs_2_ = f32[1152,128]{1,0:T(8,128)S(1)} custom-call(f32[512,128]{1,0:T(8,128)S(1)} %bitcast.23, f32[288,128]{1,0:T(8,128)S(1)} %constant_dynamic-update-slice_fusion.v_ref.right_near_ref, f32[288,128]{1,0:T(8,128)S(1)} %collective-permute-done.3.v_ref.right_far_ref, f32[512,128]{1,0:T(8,128)S(1)} %bitcast.18, ...), custom_call_target="tpu_custom_call" | custom-call | flops 2147483648 | tf_op jit(solution)/shard_map/pallas_call | solution.py:195
  104.2 1.6 %shard_map.60 = f32[1152,128]{1,0:T(8,128)S(1)} custom-call(f32[512,128]{1,0:T(8,128)S(1)} %collective-permute-done.7.v_ref, f32[288,128]{1,0:T(8,128)S(1)} %collective-permute-done.5.v_ref.right_near_ref, f32[288,128]{1,0:T(8,128)S(1)} %collective-permute-done.4.v_ref.right_far_ref, f32[512,128]{1,0:T(8,128)S(1)} %collective-permute-done.6.v_ref.refs_0_, ...), custom_call_target="tpu_custom_call" | custom-call | flops 2147483648 | tf_op jit(solution)/shard_map/pallas_call | solution.py:195
  105.8 14.9 %all_to_all.44 = f32[16,72,128]{2,1,0:T(8,128)S(1)} all-to-all(f32[16,72,128]{2,1,0:T(8,128)S(1)} %bitcast.14), channel_id=1, replica_groups={{0,4,8,12,64,68,72,76,128,132,136,140,192,196,200,204},{1,5,9,13,65,69,..., dimensions={0} | all-to-all | bytes 1179648 | tf_op jit(solution)/shard_map/all_to_all | solution.py:77
  121.0 9.4 %all_to_all.45 = f32[16,8,128]{2,1,0:T(8,128)S(1)} all-to-all(f32[16,8,128]{2,1,0:T(8,128)S(1)} %broadcast_in_dim.7), channel_id=1, replica_groups={{0,4,8,12,64,68,72,76,128,132,136,140,192,196,200,204},{1,5,9,13,65,69,..., dimensions={0} | all-to-all | bytes 131072 | tf_op jit(solution)/shard_map/all_to_all | solution.py:86
  130.4 14.6 %all_to_all.46 = f32[16,8,128]{2,1,0:T(8,128)S(1)} all-to-all(f32[16,8,128]{2,1,0:T(8,128)S(1)} %broadcast_in_dim.8), channel_id=1, replica_groups={{0,1,2,3,16,17,18,19,32,33,34,35,48,49,50,51},{4,5,6,7,20,21,22,23,36,3..., dimensions={0} | all-to-all | bytes 131072 | tf_op jit(solution)/shard_map/all_to_all | solution.py:86
  (24 shorter events, 2.4 us)
Async XLA Ops:
  2.1 13.1 %collective-permute-start.2 = (f32[72,128]{1,0:T(8,128)}, f32[72,128]{1,0:T(8,128)S(1)}, u32[]{:S(2)}, u32[]{:S(2)}) collective-permute-start(f32[72,128]{1,0:T(8,128)} %get-tuple-element.22.packed_ref), channel_id=1, source_target_pairs={{0,16},{1,17},{2,18},{3,19},{4,20},{5,21},{6,22},{7,23},{8,24},{9,... | collective-permute-start | bytes 110600 | tf_op jit(solution)/shard_map/ppermute | solution.py:65
  4.6 10.5 %collective-permute-start.1 = (f32[72,128]{1,0:T(8,128)}, f32[72,128]{1,0:T(8,128)S(1)}, u32[]{:S(2)}, u32[]{:S(2)}) collective-permute-start(f32[72,128]{1,0:T(8,128)} %get-tuple-element.22.packed_ref), channel_id=1, source_target_pairs={{0,32},{1,33},{2,34},{3,35},{4,36},{5,37},{6,38},{7,39},{8,40},{9,... | collective-permute-start | bytes 110600 | tf_op jit(solution)/shard_map/ppermute | solution.py:65
  7.6 7.5 %collective-permute-start = (f32[72,128]{1,0:T(8,128)}, f32[72,128]{1,0:T(8,128)S(1)}, u32[]{:S(2)}, u32[]{:S(2)}) collective-permute-start(f32[72,128]{1,0:T(8,128)} %get-tuple-element.22.packed_ref), channel_id=1, source_target_pairs={{0,48},{1,49},{2,50},{3,51},{4,52},{5,53},{6,54},{7,55},{8,56},{9,... | collective-permute-start | bytes 110600 | tf_op jit(solution)/shard_map/ppermute | solution.py:65
  7.6 14.0 %all-to-all-start = ((f32[16,8,128]{2,1,0:T(8,128)}), f32[16,8,128]{2,1,0:T(8,128)S(1)}, u32[]{:S(2)}, u32[]{:S(2)}) async-start(f32[16,8,128]{2,1,0:T(8,128)} %bitcast.30), calls=%async_computation | async-start | bytes 131072 | tf_op jit(solution)/shard_map/all_to_all | solution.py:77
  15.2 13.9 %collective-permute-start.5 = (f32[288,128]{1,0:T(8,128)S(1)}, f32[288,128]{1,0:T(8,128)S(1)}, u32[]{:S(2)}, u32[]{:S(2)}) collective-permute-start(f32[288,128]{1,0:T(8,128)S(1)} %constant_dynamic-update-slice_fusion.v_ref.right_near_ref), channel_id=1, source_target_pairs={{0,1},{1,0},{2,3},{3,2},{4,5},{5,4},{6,7},{7,6},{8,9},{9,8},{10,11... | collective-permute-start | bytes 442376 | tf_op jit(solution)/shard_map/ppermute | solution.py:65
  16.8 11.9 %collective-permute-start.3 = (f32[288,128]{1,0:T(8,128)S(1)}, f32[288,128]{1,0:T(8,128)S(1)}, u32[]{:S(2)}, u32[]{:S(2)}) collective-permute-start(f32[288,128]{1,0:T(8,128)S(1)} %constant_dynamic-update-slice_fusion.v_ref.right_near_ref), channel_id=1, source_target_pairs={{0,50},{1,51},{2,48},{3,49},{4,54},{5,55},{6,52},{7,53},{8,58},{9,... | collective-permute-start | bytes 442376 | tf_op jit(solution)/shard_map/ppermute | solution.py:65
  28.7 5.2 %collective-permute-start.4 = (f32[288,128]{1,0:T(8,128)S(1)}, f32[288,128]{1,0:T(8,128)S(1)}, u32[]{:S(2)}, u32[]{:S(2)}) collective-permute-start(f32[288,128]{1,0:T(8,128)S(1)} %collective-permute-done.3.v_ref.right_far_ref), channel_id=1, source_target_pairs={{0,1},{1,0},{2,3},{3,2},{4,5},{5,4},{6,7},{7,6},{8,9},{9,8},{10,11... | collective-permute-start | bytes 442376 | tf_op jit(solution)/shard_map/ppermute | solution.py:65
  33.9 20.2 %copy-start = (f32[72,128]{1,0:T(8,128)S(1)}, f32[72,128]{1,0:T(8,128)}, u32[]{:S(2)}) copy-start(f32[72,128]{1,0:T(8,128)} %get-tuple-element.22.packed_ref) | copy-start | bytes 110596
  66.9 4.7 %collective-permute-start.6 = (f32[512,128]{1,0:T(8,128)S(1)}, f32[512,128]{1,0:T(8,128)S(1)}, u32[]{:S(2)}, u32[]{:S(2)}) collective-permute-start(f32[512,128]{1,0:T(8,128)S(1)} %bitcast.16), channel_id=1, source_target_pairs={{0,1},{1,0},{2,3},{3,2},{4,5},{5,4},{6,7},{7,6},{8,9},{9,8},{10,11... | collective-permute-start | bytes 786440 | tf_op jit(solution)/shard_map/ppermute | solution.py:65
  99.5 4.7 %collective-permute-start.7 = (f32[512,128]{1,0:T(8,128)S(1)}, f32[512,128]{1,0:T(8,128)S(1)}, u32[]{:S(2)}, u32[]{:S(2)}) collective-permute-start(f32[512,128]{1,0:T(8,128)S(1)} %bitcast.22), channel_id=1, source_target_pairs={{0,1},{1,0},{2,3},{3,2},{4,5},{5,4},{6,7},{7,6},{8,9},{9,8},{10,11... | collective-permute-start | bytes 786440 | tf_op jit(solution)/shard_map/ppermute | solution.py:65

commit v5 on v4

--- a/solution.py
+++ b/solution.py
@@ -65,10 +65,9 @@
     return lax.ppermute(value, AXES, pairs)
 
 
-def parts_of(block):
+def near_and_far(block):
     near = jnp.concatenate([block] + [exchange(block, "z", m) for m in NEAR], axis=0)
-    far = exchange(near, "z", 7)
-    return [near, exchange(near, "core", 1), far, exchange(far, "core", 1)]
+    return near, exchange(near, "z", 7)
 
 
 def deal(blocks, groups):
@@ -104,11 +103,17 @@
     pair_ref[rhs:, b * LANES : (b + 1) * LANES] = low
 
 
+def four_terms(pair, kernel, rhs):
+    terms = jnp.dot(pair, kernel, preferred_element_type=jnp.float32)
+    high, low = terms[:, :TILE], terms[:, TILE:]
+    return high[:rhs] + ((high[rhs:] + low[:rhs]) + low[rhs:])
+
+
 def first_body(rhs, amplitude, has_before, v_ref, rows_ref, *refs):
     before_ref, refs = (refs[0], refs[1:]) if has_before else (None, refs)
-    out_ref, high_ref, low_ref, pair_ref, p_ref, q_ref = refs
+    out_ref, kernel_ref, pair_ref, p_ref, q_ref = refs
     step = rhs + SPARE
-    tiles, stars, _ = high_ref.shape
+    tiles, stars, _ = kernel_ref.shape
     for b in range(stars // LANES):
         at = b * step + rhs
         put_pair(pair_ref, b, v_ref[at - rhs : at, :], rhs)
@@ -131,11 +136,9 @@
                 pieces.append(split(jnp.exp2(-distance)))
             high = jnp.concatenate([h for h, _ in pieces], axis=1)
             low = jnp.concatenate([l for _, l in pieces], axis=1)
-            high_ref[tile, j : j + TILE, :] = high
-            low_ref[tile, j : j + TILE, :] = low
-            both = jnp.dot(pair_ref[:, j : j + TILE], high, preferred_element_type=jnp.float32)
-            rest = jnp.dot(pair_ref[:rhs, j : j + TILE], low, preferred_element_type=jnp.float32)
-            product = product + (both[:rhs] + (both[rhs:] + rest))
+            both = jnp.concatenate([high, low], axis=1)
+            kernel_ref[tile, j : j + TILE, :] = both
+            product = product + four_terms(pair_ref[:, j : j + TILE], both, rhs)
         for piece in range(TILE // LANES):
             at = (tile * (TILE // LANES) + piece) * rhs
             part = product[:, piece * LANES : (piece + 1) * LANES] * amplitude
@@ -147,7 +150,7 @@
 def next_body(rhs, amplitude, has_last, has_before, v_ref, right_near_ref, right_far_ref, *refs):
     last_ref, scalars_ref, refs = (refs[0], refs[1], refs[2:]) if has_last else (None, None, refs)
     before_ref, refs = (refs[0], refs[1:]) if has_before else (None, refs)
-    kernel, out_ref, pair_ref = refs[:4], refs[4], refs[5]
+    kernel_refs, out_ref, pair_ref = refs[:2], refs[2], refs[3]
     step = rhs + SPARE
     z_lo = lax.rem(lax.axis_index("row"), 4)
     z_hi = lax.rem(lax.div(lax.axis_index("col"), 2), 2)
@@ -173,14 +176,12 @@
         dots = dots + before_ref[rhs:step, :]
 
     columns = half * LANES
-    for tile in range(kernel[0].shape[0]):
-        product = jnp.zeros((rhs, TILE), jnp.float32)
-        for part in range(2):
-            cut = slice(part * columns, (part + 1) * columns)
-            high, low = kernel[2 * part][tile], kernel[2 * part + 1][tile]
-            both = jnp.dot(pair_ref[:, cut], high, preferred_element_type=jnp.float32)
-            rest = jnp.dot(pair_ref[:rhs, cut], low, preferred_element_type=jnp.float32)
-            product = product + (both[:rhs] + (both[rhs:] + rest))
+    for tile in range(kernel_refs[0].shape[0]):
+        near, far = (
+            four_terms(pair_ref[:, n * columns : (n + 1) * columns], kernel_refs[n][tile], rhs)
+            for n in range(2)
+        )
+        product = near + far
         for piece in range(TILE // LANES):
             at = (tile * (TILE // LANES) + piece) * step
             part = product[:, piece * LANES : (piece + 1) * LANES] * amplitude
@@ -206,11 +207,9 @@
 def first_product(part, row_points, before, rhs, amplitude):
     columns = part.shape[0] // (rhs + SPARE) * LANES
     pieces = row_points.shape[0] // SPARE
-    shape = (pieces * LANES // TILE, columns, TILE)
     outs = [
         jax.ShapeDtypeStruct((pieces * rhs, LANES), jnp.float32),
-        jax.ShapeDtypeStruct(shape, jnp.bfloat16),
-        jax.ShapeDtypeStruct(shape, jnp.bfloat16),
+        jax.ShapeDtypeStruct((pieces * LANES // TILE, columns, 2 * TILE), jnp.bfloat16),
     ]
     scratch = [
         pltpu.VMEM((2 * rhs, columns), jnp.bfloat16),
@@ -223,14 +222,14 @@
 
 
 def next_product(vectors, rights, last, scalars, before, kernels, rhs, amplitude):
-    tiles, columns, _ = kernels[0][0].shape
+    tiles, columns, _ = kernels[0].shape
     rows = tiles * (TILE // LANES) * (rhs + SPARE)
     outs = [jax.ShapeDtypeStruct((rows, LANES), jnp.float32)]
     scratch = [pltpu.VMEM((2 * rhs, 2 * columns), jnp.bfloat16)]
     operands = [vectors, *rights]
     operands += [] if last is None else [last, scalars]
     operands += [] if before is None else [before]
-    operands += [half for kernel in kernels for half in kernel]
+    operands += kernels
     body = functools.partial(next_body, rhs, amplitude, last is not None, before is not None)
     return kernel_call(body, outs, scratch, 1 << 31, operands)[0]
 
@@ -373,11 +372,15 @@
 
     packed, places = packed_inputs(right_side, points, star_noise[None, :])
     row_points = deal(places, PLANES)
-    rights = parts_of(packed)
-    pieces, kernels = None, []
-    for part in rights:
-        pieces, high, low = first_product(part, row_points, pieces, rhs, amplitude)
-        kernels.append((high, low))
+    rights, kernels, pieces = [], [], None
+    near, far = near_and_far(packed)
+    for n, half in enumerate((near, far)):
+        if n == 1:
+            half, pieces = lax.optimization_barrier((half, pieces))
+        for part in (half, exchange(half, "core", 1)):
+            pieces, kernel = first_product(part, row_points, pieces, rhs, amplitude)
+            kernels.append(kernel)
+            rights.append(part)
     (first,) = small(update_one, rhs, [copies], deal(pieces, PLANES), packed)
 
     def product(vectors, lasts, scalars):

time: 146 us -> 143 us (0.979)
  waiting for transfers between devices: 4.71 us -> 2.19 us
    ppermute x8, waiting for transfers between devices: 4.71 us -> 2.19 us  [exchange(): return lax.ppermute(value, AXES, pairs)]
where the time goes in v5:
time: 143 us; the launch traced here: 142 us
  blocking collectives  95.4 us (67%)
  starting transfers between devices  25.4 us (18%)
  Pallas kernels  17.6 us (12%)
  waiting for transfers between devices  2.19 us (2%)
    all_to_all x5, blocking collectives, deal(): lax.all_to_all(blocks.reshape(count, rows, LANES), AXES, 0, 0, axis_index...  70.8 us
    all_to_all x2, blocking collectives, all_sum(): dealt = lax.all_to_all(copies, AXES, 0, 0, axis_index_groups=groups)  24.5 us
    ppermute x8, starting transfers between devices, exchange(): return lax.ppermute(value, AXES, pairs)  18.7 us
    pallas_call x8, Pallas kernels, kernel_call(): pl.pallas_call(body, in_specs=[whole] * len(operands), out_specs=[whole]...  15 us
    all_to_all x1, starting transfers between devices, deal(): lax.all_to_all(blocks.reshape(count, rows, LANES), AXES, 0, 0, axis_index...  6.76 us
  transfers between devices with their start and end apart: 9, of which 1 were waited for; matrix products, arithmetic and copies ran while one was open for 1% of the time, Pallas kernels for 7%

profile of v5, /device:TPU:1, one launch (start us, length us, event | category | flops | bytes accessed | tf_op | source)
XLA Modules:
  0.0 142.2 jit_solution(12793367232489436695)
XLA Ops:
  0.6 1.4 %shard_map.50 = (f32[72,128]{1,0:T(8,128)}, f32[128,128]{1,0:T(8,128)}) custom-call(f32[64,128]{1,0:T(8,128)} %right_ref.1, f32[2,128]{1,0:T(2,128)} %points_ref.1, f32[1,128]{1,0:T(1,128)} %bitcast.31), custom_call_target="tpu_custom_call" | custom-call | tf_op jit(solution)/shard_map/pallas_call | solution.py:270
  2.1 2.6 %collective-permute-start.2 = (f32[72,128]{1,0:T(8,128)}, f32[72,128]{1,0:T(8,128)S(1)}, u32[]{:S(2)}, u32[]{:S(2)}) collective-permute-start(f32[72,128]{1,0:T(8,128)} %get-tuple-element.20.packed_ref), channel_id=1, source_target_pairs={{0,16},{1,17},{2,18},{3,19},{4,20},{5,21},{6,22},{7,23},{8,24},{9,... | collective-permute-start | bytes 110600 | tf_op jit(solution)/shard_map/ppermute | solution.py:65
  4.6 3.0 %collective-permute-start.1 = (f32[72,128]{1,0:T(8,128)}, f32[72,128]{1,0:T(8,128)S(1)}, u32[]{:S(2)}, u32[]{:S(2)}) collective-permute-start(f32[72,128]{1,0:T(8,128)} %get-tuple-element.20.packed_ref), channel_id=1, source_target_pairs={{0,32},{1,33},{2,34},{3,35},{4,36},{5,37},{6,38},{7,39},{8,40},{9,... | collective-permute-start | bytes 110600 | tf_op jit(solution)/shard_map/ppermute | solution.py:65
  7.6 6.8 %all-to-all-start = ((f32[16,8,128]{2,1,0:T(8,128)}), f32[16,8,128]{2,1,0:T(8,128)S(1)}, u32[]{:S(2)}, u32[]{:S(2)}) async-start(f32[16,8,128]{2,1,0:T(8,128)} %bitcast.30), calls=%async_computation | async-start | bytes 131072 | tf_op jit(solution)/shard_map/all_to_all | solution.py:76
  15.2 1.6 %collective-permute-start.4 = (f32[288,128]{1,0:T(8,128)S(1)}, f32[288,128]{1,0:T(8,128)S(1)}, u32[]{:S(2)}, u32[]{:S(2)}) collective-permute-start(f32[288,128]{1,0:T(8,128)S(1)} %constant_dynamic-update-slice_fusion.v_ref.right_near_ref), channel_id=1, source_target_pairs={{0,1},{1,0},{2,3},{3,2},{4,5},{5,4},{6,7},{7,6},{8,9},{9,8},{10,11... | collective-permute-start | bytes 442376 | tf_op jit(solution)/shard_map/ppermute | solution.py:65
  16.8 4.8 %collective-permute-start.3 = (f32[288,128]{1,0:T(8,128)S(1)}, f32[288,128]{1,0:T(8,128)S(1)}, u32[]{:S(2)}, u32[]{:S(2)}) collective-permute-start(f32[288,128]{1,0:T(8,128)S(1)} %constant_dynamic-update-slice_fusion.v_ref.right_near_ref), channel_id=1, source_target_pairs={{0,50},{1,51},{2,48},{3,49},{4,54},{5,55},{6,52},{7,53},{8,58},{9,... | collective-permute-start | bytes 442376 | tf_op jit(solution)/shard_map/ppermute | solution.py:65
  21.6 2.4 %shard_map.51 = (f32[1024,128]{1,0:T(8,128)S(1)}, bf16[8,512,512]{2,1,0:T(8,128)(2,1)S(1)}) custom-call(f32[288,128]{1,0:T(8,128)S(1)} %constant_dynamic-update-slice_fusion.v_ref.right_near_ref, f32[128,128]{1,0:T(8,128)S(1)} %bitcast.26), custom_call_target="tpu_custom_call" | custom-call | flops 3221225472 | tf_op jit(solution)/shard_map/pallas_call | solution.py:196
  24.0 2.4 %shard_map.52 = (f32[1024,128]{1,0:T(8,128)S(1)}, bf16[8,512,512]{2,1,0:T(8,128)(2,1)S(1)}) custom-call(f32[288,128]{1,0:T(8,128)S(1)} %collective-permute-done.4.v_ref.right_near_ref, f32[128,128]{1,0:T(8,128)S(1)} %bitcast.27, f32[1024,128]{1,0:T(8,128)S(1)} %get-tuple-element.22.refs_0_), custom_call_target="tpu_custom_call" | custom-call | flops 3221225472 | tf_op jit(solution)/shard_map/pallas_call | solution.py:196
  26.5 2.2 %collective-permute-done.3.v_ref.right_far_ref = f32[288,128]{1,0:T(8,128)S(1)} collective-permute-done((f32[288,128]{1,0:T(8,128)S(1)}, f32[288,128]{1,0:T(8,128)S(1)}, u32[]{:S(2)}, u32[]{:S(2)}) %collective-permute-start.3) | collective-permute-done | bytes 147488 | tf_op jit(solution)/shard_map/ppermute | solution.py:65
  29.1 2.5 %shard_map.53 = (f32[1024,128]{1,0:T(8,128)S(1)}, bf16[8,512,512]{2,1,0:T(8,128)(2,1)S(1)}) custom-call(f32[288,128]{1,0:T(8,128)S(1)} %collective-permute-done.3.v_ref.right_far_ref, f32[128,128]{1,0:T(8,128)S(1)} %bitcast.28, f32[1024,128]{1,0:T(8,128)S(1)} %get-tuple-element.25.refs_0_), custom_call_target="tpu_custom_call" | custom-call | flops 3221225472 | tf_op jit(solution)/shard_map/pallas_call | solution.py:196
  31.6 2.5 %shard_map.54 = (f32[1024,128]{1,0:T(8,128)S(1)}, bf16[8,512,512]{2,1,0:T(8,128)(2,1)S(1)}) custom-call(f32[288,128]{1,0:T(8,128)S(1)} %collective-permute-done.5.v_ref.right_far_ref, f32[128,128]{1,0:T(8,128)S(1)} %bitcast.29, f32[1024,128]{1,0:T(8,128)S(1)} %get-tuple-element.26.refs_0_), custom_call_target="tpu_custom_call" | custom-call | flops 3221225472 | tf_op jit(solution)/shard_map/pallas_call | solution.py:196
  34.0 17.8 %all_to_all.40 = f32[16,64,128]{2,1,0:T(8,128)S(1)} all-to-all(f32[16,64,128]{2,1,0:T(8,128)S(1)} %bitcast.25), channel_id=1, replica_groups={{0,4,8,12,64,68,72,76,128,132,136,140,192,196,200,204},{1,5,9,13,65,69,..., dimensions={0} | all-to-all | bytes 1048576 | tf_op jit(solution)/shard_map/all_to_all | solution.py:76
  51.9 12.8 %all_to_all.41 = f32[8,64,128]{2,1,0:T(8,128)S(1)} all-to-all(f32[8,64,128]{2,1,0:T(8,128)S(1)} %bitcast.13), channel_id=1, replica_groups={{0,2,16,18,32,34,48,50},{1,3,17,19,33,35,49,51},{4,6,20,22,36,38,52,54}..., dimensions={0} | all-to-all | bytes 524288 | tf_op jit(solution)/shard_map/all_to_all | solution.py:76
  64.6 3.2 %collective-permute-start.6 = (f32[512,128]{1,0:T(8,128)S(1)}, f32[512,128]{1,0:T(8,128)S(1)}, u32[]{:S(2)}, u32[]{:S(2)}) collective-permute-start(f32[512,128]{1,0:T(8,128)S(1)} %bitcast.16), channel_id=1, source_target_pairs={{0,1},{1,0},{2,3},{3,2},{4,5},{5,4},{6,7},{7,6},{8,9},{9,8},{10,11... | collective-permute-start | bytes 786440 | tf_op jit(solution)/shard_map/ppermute | solution.py:65
  67.8 1.3 shard_map.56.refs_0_
  69.1 1.3 shard_map.57
  70.4 14.4 %all_to_all.42 = f32[16,72,128]{2,1,0:T(8,128)S(1)} all-to-all(f32[16,72,128]{2,1,0:T(8,128)S(1)} %bitcast.15), channel_id=1, replica_groups={{0,4,8,12,64,68,72,76,128,132,136,140,192,196,200,204},{1,5,9,13,65,69,..., dimensions={0} | all-to-all | bytes 1179648 | tf_op jit(solution)/shard_map/all_to_all | solution.py:76
  84.9 11.2 %all_to_all.43 = f32[8,64,128]{2,1,0:T(8,128)S(1)} all-to-all(f32[8,64,128]{2,1,0:T(8,128)S(1)} %bitcast.24), channel_id=1, replica_groups={{0,2,16,18,32,34,48,50},{1,3,17,19,33,35,49,51},{4,6,20,22,36,38,52,54}..., dimensions={0} | all-to-all | bytes 524288 | tf_op jit(solution)/shard_map/all_to_all | solution.py:76
  96.1 3.1 %collective-permute-start.7 = (f32[512,128]{1,0:T(8,128)S(1)}, f32[512,128]{1,0:T(8,128)S(1)}, u32[]{:S(2)}, u32[]{:S(2)}) collective-permute-start(f32[512,128]{1,0:T(8,128)S(1)} %bitcast.22), channel_id=1, source_target_pairs={{0,1},{1,0},{2,3},{3,2},{4,5},{5,4},{6,7},{7,6},{8,9},{9,8},{10,11... | collective-permute-start | bytes 786440 | tf_op jit(solution)/shard_map/ppermute | solution.py:65
  99.3 1.3 shard_map.59.refs_2_
  100.6 1.3 shard_map.60
  101.9 14.7 %all_to_all.44 = f32[16,72,128]{2,1,0:T(8,128)S(1)} all-to-all(f32[16,72,128]{2,1,0:T(8,128)S(1)} %bitcast.14), channel_id=1, replica_groups={{0,4,8,12,64,68,72,76,128,132,136,140,192,196,200,204},{1,5,9,13,65,69,..., dimensions={0} | all-to-all | bytes 1179648 | tf_op jit(solution)/shard_map/all_to_all | solution.py:76
  116.9 9.6 %all_to_all.45 = f32[16,8,128]{2,1,0:T(8,128)S(1)} all-to-all(f32[16,8,128]{2,1,0:T(8,128)S(1)} %broadcast_in_dim.7), channel_id=1, replica_groups={{0,4,8,12,64,68,72,76,128,132,136,140,192,196,200,204},{1,5,9,13,65,69,..., dimensions={0} | all-to-all | bytes 131072 | tf_op jit(solution)/shard_map/all_to_all | solution.py:85
  126.5 14.9 %all_to_all.46 = f32[16,8,128]{2,1,0:T(8,128)S(1)} all-to-all(f32[16,8,128]{2,1,0:T(8,128)S(1)} %broadcast_in_dim.8), channel_id=1, replica_groups={{0,1,2,3,16,17,18,19,32,33,34,35,48,49,50,51},{4,5,6,7,20,21,22,23,36,3..., dimensions={0} | all-to-all | bytes 131072 | tf_op jit(solution)/shard_map/all_to_all | solution.py:85
  (24 shorter events, 2.4 us)
Async XLA Ops:
  2.1 13.1 %collective-permute-start.2 = (f32[72,128]{1,0:T(8,128)}, f32[72,128]{1,0:T(8,128)S(1)}, u32[]{:S(2)}, u32[]{:S(2)}) collective-permute-start(f32[72,128]{1,0:T(8,128)} %get-tuple-element.20.packed_ref), channel_id=1, source_target_pairs={{0,16},{1,17},{2,18},{3,19},{4,20},{5,21},{6,22},{7,23},{8,24},{9,... | collective-permute-start | bytes 110600 | tf_op jit(solution)/shard_map/ppermute | solution.py:65
  4.6 10.5 %collective-permute-start.1 = (f32[72,128]{1,0:T(8,128)}, f32[72,128]{1,0:T(8,128)S(1)}, u32[]{:S(2)}, u32[]{:S(2)}) collective-permute-start(f32[72,128]{1,0:T(8,128)} %get-tuple-element.20.packed_ref), channel_id=1, source_target_pairs={{0,32},{1,33},{2,34},{3,35},{4,36},{5,37},{6,38},{7,39},{8,40},{9,... | collective-permute-start | bytes 110600 | tf_op jit(solution)/shard_map/ppermute | solution.py:65
  7.6 7.5 %collective-permute-start = (f32[72,128]{1,0:T(8,128)}, f32[72,128]{1,0:T(8,128)S(1)}, u32[]{:S(2)}, u32[]{:S(2)}) collective-permute-start(f32[72,128]{1,0:T(8,128)} %get-tuple-element.20.packed_ref), channel_id=1, source_target_pairs={{0,48},{1,49},{2,50},{3,51},{4,52},{5,53},{6,54},{7,55},{8,56},{9,... | collective-permute-start | bytes 110600 | tf_op jit(solution)/shard_map/ppermute | solution.py:65
  7.6 14.0 %all-to-all-start = ((f32[16,8,128]{2,1,0:T(8,128)}), f32[16,8,128]{2,1,0:T(8,128)S(1)}, u32[]{:S(2)}, u32[]{:S(2)}) async-start(f32[16,8,128]{2,1,0:T(8,128)} %bitcast.30), calls=%async_computation | async-start | bytes 131072 | tf_op jit(solution)/shard_map/all_to_all | solution.py:76
  15.2 8.8 %collective-permute-start.4 = (f32[288,128]{1,0:T(8,128)S(1)}, f32[288,128]{1,0:T(8,128)S(1)}, u32[]{:S(2)}, u32[]{:S(2)}) collective-permute-start(f32[288,128]{1,0:T(8,128)S(1)} %constant_dynamic-update-slice_fusion.v_ref.right_near_ref), channel_id=1, source_target_pairs={{0,1},{1,0},{2,3},{3,2},{4,5},{5,4},{6,7},{7,6},{8,9},{9,8},{10,11... | collective-permute-start | bytes 442376 | tf_op jit(solution)/shard_map/ppermute | solution.py:65
  16.8 11.9 %collective-permute-start.3 = (f32[288,128]{1,0:T(8,128)S(1)}, f32[288,128]{1,0:T(8,128)S(1)}, u32[]{:S(2)}, u32[]{:S(2)}) collective-permute-start(f32[288,128]{1,0:T(8,128)S(1)} %constant_dynamic-update-slice_fusion.v_ref.right_near_ref), channel_id=1, source_target_pairs={{0,50},{1,51},{2,48},{3,49},{4,54},{5,55},{6,52},{7,53},{8,58},{9,... | collective-permute-start | bytes 442376 | tf_op jit(solution)/shard_map/ppermute | solution.py:65
  28.7 2.9 %collective-permute-start.5 = (f32[288,128]{1,0:T(8,128)S(1)}, f32[288,128]{1,0:T(8,128)S(1)}, u32[]{:S(2)}, u32[]{:S(2)}) collective-permute-start(f32[288,128]{1,0:T(8,128)S(1)} %collective-permute-done.3.v_ref.right_far_ref), channel_id=1, source_target_pairs={{0,1},{1,0},{2,3},{3,2},{4,5},{5,4},{6,7},{7,6},{8,9},{9,8},{10,11... | collective-permute-start | bytes 442376 | tf_op jit(solution)/shard_map/ppermute | solution.py:65
  31.6 20.2 %copy-start = (f32[72,128]{1,0:T(8,128)S(1)}, f32[72,128]{1,0:T(8,128)}, u32[]{:S(2)}) copy-start(f32[72,128]{1,0:T(8,128)} %get-tuple-element.20.packed_ref) | copy-start | bytes 110596
  64.6 4.5 %collective-permute-start.6 = (f32[512,128]{1,0:T(8,128)S(1)}, f32[512,128]{1,0:T(8,128)S(1)}, u32[]{:S(2)}, u32[]{:S(2)}) collective-permute-start(f32[512,128]{1,0:T(8,128)S(1)} %bitcast.16), channel_id=1, source_target_pairs={{0,1},{1,0},{2,3},{3,2},{4,5},{5,4},{6,7},{7,6},{8,9},{9,8},{10,11... | collective-permute-start | bytes 786440 | tf_op jit(solution)/shard_map/ppermute | solution.py:65
  96.1 4.5 %collective-permute-start.7 = (f32[512,128]{1,0:T(8,128)S(1)}, f32[512,128]{1,0:T(8,128)S(1)}, u32[]{:S(2)}, u32[]{:S(2)}) collective-permute-start(f32[512,128]{1,0:T(8,128)S(1)} %bitcast.22), channel_id=1, source_target_pairs={{0,1},{1,0},{2,3},{3,2},{4,5},{5,4},{6,7},{7,6},{8,9},{9,8},{10,11... | collective-permute-start | bytes 786440 | tf_op jit(solution)/shard_map/ppermute | solution.py:65

commit v6 on v5

--- a/solution.py
+++ b/solution.py
@@ -52,8 +52,8 @@
 PLANES = groups_along("x", "y")
 LINES = groups_along("z")
 COLUMNS = groups_along("z", "core")
-NEAR = (3, 2, 1)
-BLOCKS = (0,) + NEAR + tuple(7 ^ m for m in (0,) + NEAR)
+NEAR, FAR = (2, 5, 7), 1
+BLOCKS = (0,) + NEAR + tuple(FAR ^ m for m in (0,) + NEAR)
 
 
 def exchange(value, axis, mask):
@@ -67,7 +67,7 @@
 
 def near_and_far(block):
     near = jnp.concatenate([block] + [exchange(block, "z", m) for m in NEAR], axis=0)
-    return near, exchange(near, "z", 7)
+    return near, exchange(near, "z", FAR)
 
 
 def deal(blocks, groups):

time: 143 us -> 142 us (level)
  blocking collectives: 95.4 us -> 91.6 us
  starting transfers between devices: 25.4 us -> 27 us
    all_to_all x5, blocking collectives: 70.8 us -> 67.1 us  [deal(): lax.all_to_all(blocks.reshape(count, rows, LANES), AXES, 0, 0, axis_index...]
    all_to_all x1, waiting for transfers between devices: 0.01 us -> 3.34 us  [deal(): lax.all_to_all(blocks.reshape(count, rows, LANES), AXES, 0, 0, axis_index...]
    ppermute x8, waiting for transfers between devices: 2.19 us -> 0.02 us  [exchange(): return lax.ppermute(value, AXES, pairs)]
    ppermute x8, starting transfers between devices: 18.7 us -> 20.3 us  [exchange(): return lax.ppermute(value, AXES, pairs)]
where the time goes in v6:
time: 142 us; the launch traced here: 141 us
  blocking collectives  91.6 us (65%)
  starting transfers between devices  27 us (19%)
  Pallas kernels  17.6 us (12%)
  waiting for transfers between devices  3.36 us (2%)
    all_to_all x5, blocking collectives, deal(): lax.all_to_all(blocks.reshape(count, rows, LANES), AXES, 0, 0, axis_index...  67.1 us
    all_to_all x2, blocking collectives, all_sum(): dealt = lax.all_to_all(copies, AXES, 0, 0, axis_index_groups=groups)  24.5 us
    ppermute x8, starting transfers between devices, exchange(): return lax.ppermute(value, AXES, pairs)  20.3 us
    pallas_call x8, Pallas kernels, kernel_call(): pl.pallas_call(body, in_specs=[whole] * len(operands), out_specs=[whole]...  15 us
    all_to_all x1, starting transfers between devices, deal(): lax.all_to_all(blocks.reshape(count, rows, LANES), AXES, 0, 0, axis_index...  6.75 us
    all_to_all x1, waiting for transfers between devices, deal(): lax.all_to_all(blocks.reshape(count, rows, LANES), AXES, 0, 0, axis_index...  3.34 us
  transfers between devices with their start and end apart: 9, of which 1 were waited for; matrix products, arithmetic and copies ran while one was open for 1% of the time, Pallas kernels for 7%

profile of v6, /device:TPU:1, one launch (start us, length us, event | category | flops | bytes accessed | tf_op | source)
XLA Modules:
  0.0 141.2 jit_solution(16111965715271233272)
XLA Ops:
  0.6 1.4 %shard_map.50 = (f32[72,128]{1,0:T(8,128)}, f32[128,128]{1,0:T(8,128)}) custom-call(f32[64,128]{1,0:T(8,128)} %right_ref.1, f32[2,128]{1,0:T(2,128)} %points_ref.1, f32[1,128]{1,0:T(1,128)} %bitcast.31), custom_call_target="tpu_custom_call" | custom-call | tf_op jit(solution)/shard_map/pallas_call | solution.py:270
  2.1 6.5 %collective-permute-start.2 = (f32[72,128]{1,0:T(8,128)}, f32[72,128]{1,0:T(8,128)S(1)}, u32[]{:S(2)}, u32[]{:S(2)}) collective-permute-start(f32[72,128]{1,0:T(8,128)} %get-tuple-element.20.packed_ref), channel_id=1, source_target_pairs={{0,50},{1,51},{2,48},{3,49},{4,54},{5,55},{6,52},{7,53},{8,58},{9,... | collective-permute-start | bytes 110600 | tf_op jit(solution)/shard_map/ppermute | solution.py:65
  9.5 1.2 collective-permute-start
  10.7 6.8 %all-to-all-start = ((f32[16,8,128]{2,1,0:T(8,128)}), f32[16,8,128]{2,1,0:T(8,128)S(1)}, u32[]{:S(2)}, u32[]{:S(2)}) async-start(f32[16,8,128]{2,1,0:T(8,128)} %bitcast.30), calls=%async_computation | async-start | bytes 131072 | tf_op jit(solution)/shard_map/all_to_all | solution.py:76
  18.3 1.6 %collective-permute-start.4 = (f32[288,128]{1,0:T(8,128)S(1)}, f32[288,128]{1,0:T(8,128)S(1)}, u32[]{:S(2)}, u32[]{:S(2)}) collective-permute-start(f32[288,128]{1,0:T(8,128)S(1)} %constant_dynamic-update-slice_fusion.v_ref.right_near_ref), channel_id=1, source_target_pairs={{0,1},{1,0},{2,3},{3,2},{4,5},{5,4},{6,7},{7,6},{8,9},{9,8},{10,11... | collective-permute-start | bytes 442376 | tf_op jit(solution)/shard_map/ppermute | solution.py:65
  20.7 3.3 %all-to-all-done = f32[16,8,128]{2,1,0:T(8,128)S(1)} async-done(((f32[16,8,128]{2,1,0:T(8,128)}), f32[16,8,128]{2,1,0:T(8,128)S(1)}, u32[]{:S(2)}, u32[]{:S(2)}) %all-to-all-start) | async-done | bytes 65568 | tf_op jit(solution)/shard_map/all_to_all | solution.py:76
  24.0 2.4 %shard_map.51 = (f32[1024,128]{1,0:T(8,128)S(1)}, bf16[8,512,512]{2,1,0:T(8,128)(2,1)S(1)}) custom-call(f32[288,128]{1,0:T(8,128)S(1)} %constant_dynamic-update-slice_fusion.v_ref.right_near_ref, f32[128,128]{1,0:T(8,128)S(1)} %bitcast.26), custom_call_target="tpu_custom_call" | custom-call | flops 3221225472 | tf_op jit(solution)/shard_map/pallas_call | solution.py:196
  26.5 2.4 %shard_map.52 = (f32[1024,128]{1,0:T(8,128)S(1)}, bf16[8,512,512]{2,1,0:T(8,128)(2,1)S(1)}) custom-call(f32[288,128]{1,0:T(8,128)S(1)} %collective-permute-done.4.v_ref.right_near_ref, f32[128,128]{1,0:T(8,128)S(1)} %bitcast.27, f32[1024,128]{1,0:T(8,128)S(1)} %get-tuple-element.22.refs_0_), custom_call_target="tpu_custom_call" | custom-call | flops 3221225472 | tf_op jit(solution)/shard_map/pallas_call | solution.py:196
  28.9 2.9 %collective-permute-start.5 = (f32[288,128]{1,0:T(8,128)S(1)}, f32[288,128]{1,0:T(8,128)S(1)}, u32[]{:S(2)}, u32[]{:S(2)}) collective-permute-start(f32[288,128]{1,0:T(8,128)S(1)} %collective-permute-done.3.v_ref.right_far_ref), channel_id=1, source_target_pairs={{0,1},{1,0},{2,3},{3,2},{4,5},{5,4},{6,7},{7,6},{8,9},{9,8},{10,11... | collective-permute-start | bytes 442376 | tf_op jit(solution)/shard_map/ppermute | solution.py:65
  31.8 2.5 %shard_map.53 = (f32[1024,128]{1,0:T(8,128)S(1)}, bf16[8,512,512]{2,1,0:T(8,128)(2,1)S(1)}) custom-call(f32[288,128]{1,0:T(8,128)S(1)} %collective-permute-done.3.v_ref.right_far_ref, f32[128,128]{1,0:T(8,128)S(1)} %bitcast.28, f32[1024,128]{1,0:T(8,128)S(1)} %get-tuple-element.25.refs_0_), custom_call_target="tpu_custom_call" | custom-call | flops 3221225472 | tf_op jit(solution)/shard_map/pallas_call | solution.py:196
  34.3 2.5 %shard_map.54 = (f32[1024,128]{1,0:T(8,128)S(1)}, bf16[8,512,512]{2,1,0:T(8,128)(2,1)S(1)}) custom-call(f32[288,128]{1,0:T(8,128)S(1)} %collective-permute-done.5.v_ref.right_far_ref, f32[128,128]{1,0:T(8,128)S(1)} %bitcast.29, f32[1024,128]{1,0:T(8,128)S(1)} %get-tuple-element.26.refs_0_), custom_call_target="tpu_custom_call" | custom-call | flops 3221225472 | tf_op jit(solution)/shard_map/pallas_call | solution.py:196
  36.8 13.9 %all_to_all.40 = f32[16,64,128]{2,1,0:T(8,128)S(1)} all-to-all(f32[16,64,128]{2,1,0:T(8,128)S(1)} %bitcast.25), channel_id=1, replica_groups={{0,4,8,12,64,68,72,76,128,132,136,140,192,196,200,204},{1,5,9,13,65,69,..., dimensions={0} | all-to-all | bytes 1048576 | tf_op jit(solution)/shard_map/all_to_all | solution.py:76
  50.8 12.8 %all_to_all.41 = f32[8,64,128]{2,1,0:T(8,128)S(1)} all-to-all(f32[8,64,128]{2,1,0:T(8,128)S(1)} %bitcast.13), channel_id=1, replica_groups={{0,2,16,18,32,34,48,50},{1,3,17,19,33,35,49,51},{4,6,20,22,36,38,52,54}..., dimensions={0} | all-to-all | bytes 524288 | tf_op jit(solution)/shard_map/all_to_all | solution.py:76
  63.6 3.2 %collective-permute-start.6 = (f32[512,128]{1,0:T(8,128)S(1)}, f32[512,128]{1,0:T(8,128)S(1)}, u32[]{:S(2)}, u32[]{:S(2)}) collective-permute-start(f32[512,128]{1,0:T(8,128)S(1)} %bitcast.16), channel_id=1, source_target_pairs={{0,1},{1,0},{2,3},{3,2},{4,5},{5,4},{6,7},{7,6},{8,9},{9,8},{10,11... | collective-permute-start | bytes 786440 | tf_op jit(solution)/shard_map/ppermute | solution.py:65
  66.8 1.3 shard_map.56.refs_0_
  68.1 1.3 shard_map.57
  69.4 14.4 %all_to_all.42 = f32[16,72,128]{2,1,0:T(8,128)S(1)} all-to-all(f32[16,72,128]{2,1,0:T(8,128)S(1)} %bitcast.15), channel_id=1, replica_groups={{0,4,8,12,64,68,72,76,128,132,136,140,192,196,200,204},{1,5,9,13,65,69,..., dimensions={0} | all-to-all | bytes 1179648 | tf_op jit(solution)/shard_map/all_to_all | solution.py:76
  84.0 11.2 %all_to_all.43 = f32[8,64,128]{2,1,0:T(8,128)S(1)} all-to-all(f32[8,64,128]{2,1,0:T(8,128)S(1)} %bitcast.24), channel_id=1, replica_groups={{0,2,16,18,32,34,48,50},{1,3,17,19,33,35,49,51},{4,6,20,22,36,38,52,54}..., dimensions={0} | all-to-all | bytes 524288 | tf_op jit(solution)/shard_map/all_to_all | solution.py:76
  95.1 3.2 %collective-permute-start.7 = (f32[512,128]{1,0:T(8,128)S(1)}, f32[512,128]{1,0:T(8,128)S(1)}, u32[]{:S(2)}, u32[]{:S(2)}) collective-permute-start(f32[512,128]{1,0:T(8,128)S(1)} %bitcast.22), channel_id=1, source_target_pairs={{0,1},{1,0},{2,3},{3,2},{4,5},{5,4},{6,7},{7,6},{8,9},{9,8},{10,11... | collective-permute-start | bytes 786440 | tf_op jit(solution)/shard_map/ppermute | solution.py:65
  98.3 1.3 shard_map.59.refs_2_
  99.6 1.3 shard_map.60
  101.0 14.7 %all_to_all.44 = f32[16,72,128]{2,1,0:T(8,128)S(1)} all-to-all(f32[16,72,128]{2,1,0:T(8,128)S(1)} %bitcast.14), channel_id=1, replica_groups={{0,4,8,12,64,68,72,76,128,132,136,140,192,196,200,204},{1,5,9,13,65,69,..., dimensions={0} | all-to-all | bytes 1179648 | tf_op jit(solution)/shard_map/all_to_all | solution.py:76
  116.0 9.6 %all_to_all.45 = f32[16,8,128]{2,1,0:T(8,128)S(1)} all-to-all(f32[16,8,128]{2,1,0:T(8,128)S(1)} %broadcast_in_dim.7), channel_id=1, replica_groups={{0,4,8,12,64,68,72,76,128,132,136,140,192,196,200,204},{1,5,9,13,65,69,..., dimensions={0} | all-to-all | bytes 131072 | tf_op jit(solution)/shard_map/all_to_all | solution.py:85
  125.6 14.9 %all_to_all.46 = f32[16,8,128]{2,1,0:T(8,128)S(1)} all-to-all(f32[16,8,128]{2,1,0:T(8,128)S(1)} %broadcast_in_dim.8), channel_id=1, replica_groups={{0,1,2,3,16,17,18,19,32,33,34,35,48,49,50,51},{4,5,6,7,20,21,22,23,36,3..., dimensions={0} | all-to-all | bytes 131072 | tf_op jit(solution)/shard_map/all_to_all | solution.py:85
  (24 shorter events, 3.7 us)
Async XLA Ops:
  2.1 16.2 %collective-permute-start.2 = (f32[72,128]{1,0:T(8,128)}, f32[72,128]{1,0:T(8,128)S(1)}, u32[]{:S(2)}, u32[]{:S(2)}) collective-permute-start(f32[72,128]{1,0:T(8,128)} %get-tuple-element.20.packed_ref), channel_id=1, source_target_pairs={{0,50},{1,51},{2,48},{3,49},{4,54},{5,55},{6,52},{7,53},{8,58},{9,... | collective-permute-start | bytes 110600 | tf_op jit(solution)/shard_map/ppermute | solution.py:65
  8.6 9.7 %collective-permute-start.1 = (f32[72,128]{1,0:T(8,128)}, f32[72,128]{1,0:T(8,128)S(1)}, u32[]{:S(2)}, u32[]{:S(2)}) collective-permute-start(f32[72,128]{1,0:T(8,128)} %get-tuple-element.20.packed_ref), channel_id=1, source_target_pairs={{0,18},{1,19},{2,16},{3,17},{4,22},{5,23},{6,20},{7,21},{8,26},{9,... | collective-permute-start | bytes 110600 | tf_op jit(solution)/shard_map/ppermute | solution.py:65
  9.5 8.7 %collective-permute-start = (f32[72,128]{1,0:T(8,128)}, f32[72,128]{1,0:T(8,128)S(1)}, u32[]{:S(2)}, u32[]{:S(2)}) collective-permute-start(f32[72,128]{1,0:T(8,128)} %get-tuple-element.20.packed_ref), channel_id=1, source_target_pairs={{0,32},{1,33},{2,34},{3,35},{4,36},{5,37},{6,38},{7,39},{8,40},{9,... | collective-permute-start | bytes 110600 | tf_op jit(solution)/shard_map/ppermute | solution.py:65
  10.7 13.3 %all-to-all-start = ((f32[16,8,128]{2,1,0:T(8,128)}), f32[16,8,128]{2,1,0:T(8,128)S(1)}, u32[]{:S(2)}, u32[]{:S(2)}) async-start(f32[16,8,128]{2,1,0:T(8,128)} %bitcast.30), calls=%async_computation | async-start | bytes 131072 | tf_op jit(solution)/shard_map/all_to_all | solution.py:76
  18.3 8.1 %collective-permute-start.4 = (f32[288,128]{1,0:T(8,128)S(1)}, f32[288,128]{1,0:T(8,128)S(1)}, u32[]{:S(2)}, u32[]{:S(2)}) collective-permute-start(f32[288,128]{1,0:T(8,128)S(1)} %constant_dynamic-update-slice_fusion.v_ref.right_near_ref), channel_id=1, source_target_pairs={{0,1},{1,0},{2,3},{3,2},{4,5},{5,4},{6,7},{7,6},{8,9},{9,8},{10,11... | collective-permute-start | bytes 442376 | tf_op jit(solution)/shard_map/ppermute | solution.py:65
  19.9 9.0 %collective-permute-start.3 = (f32[288,128]{1,0:T(8,128)S(1)}, f32[288,128]{1,0:T(8,128)S(1)}, u32[]{:S(2)}, u32[]{:S(2)}) collective-permute-start(f32[288,128]{1,0:T(8,128)S(1)} %constant_dynamic-update-slice_fusion.v_ref.right_near_ref), channel_id=1, source_target_pairs={{0,16},{1,17},{2,18},{3,19},{4,20},{5,21},{6,22},{7,23},{8,24},{9,... | collective-permute-start | bytes 442376 | tf_op jit(solution)/shard_map/ppermute | solution.py:65
  28.9 5.4 %collective-permute-start.5 = (f32[288,128]{1,0:T(8,128)S(1)}, f32[288,128]{1,0:T(8,128)S(1)}, u32[]{:S(2)}, u32[]{:S(2)}) collective-permute-start(f32[288,128]{1,0:T(8,128)S(1)} %collective-permute-done.3.v_ref.right_far_ref), channel_id=1, source_target_pairs={{0,1},{1,0},{2,3},{3,2},{4,5},{5,4},{6,7},{7,6},{8,9},{9,8},{10,11... | collective-permute-start | bytes 442376 | tf_op jit(solution)/shard_map/ppermute | solution.py:65
  34.3 16.4 %copy-start = (f32[72,128]{1,0:T(8,128)S(1)}, f32[72,128]{1,0:T(8,128)}, u32[]{:S(2)}) copy-start(f32[72,128]{1,0:T(8,128)} %get-tuple-element.20.packed_ref) | copy-start | bytes 110596
  63.6 4.5 %collective-permute-start.6 = (f32[512,128]{1,0:T(8,128)S(1)}, f32[512,128]{1,0:T(8,128)S(1)}, u32[]{:S(2)}, u32[]{:S(2)}) collective-permute-start(f32[512,128]{1,0:T(8,128)S(1)} %bitcast.16), channel_id=1, source_target_pairs={{0,1},{1,0},{2,3},{3,2},{4,5},{5,4},{6,7},{7,6},{8,9},{9,8},{10,11... | collective-permute-start | bytes 786440 | tf_op jit(solution)/shard_map/ppermute | solution.py:65
  95.1 4.5 %collective-permute-start.7 = (f32[512,128]{1,0:T(8,128)S(1)}, f32[512,128]{1,0:T(8,128)S(1)}, u32[]{:S(2)}, u32[]{:S(2)}) collective-permute-start(f32[512,128]{1,0:T(8,128)S(1)} %bitcast.22), channel_id=1, source_target_pairs={{0,1},{1,0},{2,3},{3,2},{4,5},{5,4},{6,7},{7,6},{8,9},{9,8},{10,11... | collective-permute-start | bytes 786440 | tf_op jit(solution)/shard_map/ppermute | solution.py:65

commit v7 on v6

--- a/solution.py
+++ b/solution.py
@@ -41,18 +41,21 @@
     return row * 16 + at["x"] * 4 + (at["z"] // 4) * 2 + at["core"]
 
 
-def groups_along(*axes):
+def bit_reversed(value, bits):
+    return sum(((value >> b) & 1) << (bits - 1 - b) for b in range(bits))
+
+
+def groups_along(*axes, key=None):
     groups = {}
     for index in range(DEVICES):
         rest = tuple(v for k, v in place(index).items() if k not in axes)
         groups.setdefault(rest, []).append(index)
-    return list(groups.values())
+    return [sorted(g, key=None if key is None else lambda i: key(place(i))) for g in groups.values()]
 
 
 PLANES = groups_along("x", "y")
-LINES = groups_along("z")
-COLUMNS = groups_along("z", "core")
-NEAR, FAR = (2, 5, 7), 1
+LINES = groups_along("z", key=lambda at: bit_reversed(at["z"], 3))
+NEAR, FAR = (7, 2, 5), 1
 BLOCKS = (0,) + NEAR + tuple(FAR ^ m for m in (0,) + NEAR)
 
 
@@ -80,7 +83,8 @@
 
 
 def all_sum(block):
-    for groups in (PLANES, COLUMNS):
+    block = block + exchange(block, "core", 1)
+    for groups in (PLANES, LINES):
         copies = jnp.broadcast_to(block[None], (len(groups[0]),) + block.shape)
         dealt = lax.all_to_all(copies, AXES, 0, 0, axis_index_groups=groups)
         block = jnp.sum(dealt, axis=0)
@@ -161,7 +165,8 @@
     half = len(BLOCKS) // 2
     for b, mask in enumerate(BLOCKS):
         lo, hi = lax.bitwise_xor(z_lo, mask % 4), lax.bitwise_xor(z_hi, mask // 4)
-        at = pl.multiple_of((lo * 2 + hi) * rhs, rhs)
+        place_in_line = lax.rem(lo, 2) * 4 + lax.div(lo, 2) * 2 + hi
+        at = pl.multiple_of(place_in_line * rhs, rhs)
         block = v_ref[pl.ds(at, rhs), :]
         put_pair(pair_ref, b, block, rhs)
         right_ref = right_near_ref if b < half else right_far_ref

time: 142 us -> 140 us (0.986)
  blocking collectives: 91.6 us -> 86.8 us
  starting transfers between devices: 27 us -> 28.9 us
    all_to_all x2, blocking collectives: 24.5 us -> 19.8 us  [all_sum(): dealt = lax.all_to_all(copies, AXES, 0, 0, axis_index_groups=groups)]
    ppermute x8 -> x9, starting transfers between devices: 20.3 us -> 22.1 us  [exchange(): return lax.ppermute(value, AXES, pairs)]
  transfers between devices with their start and end apart: 9 -> 10, of which waited for: 1 -> 2; matrix products, arithmetic and copies ran while one was open for 1% -> 1% of each run, Pallas kernels for 7% -> 7%
where the time goes in v7:
time: 140 us; the launch traced here: 139 us
  blocking collectives  86.8 us (62%)
  starting transfers between devices  28.9 us (21%)
  Pallas kernels  17.6 us (13%)
  waiting for transfers between devices  4.09 us (3%)
    all_to_all x5, blocking collectives, deal(): lax.all_to_all(blocks.reshape(count, rows, LANES), AXES, 0, 0, axis_index...  67 us
    ppermute x9, starting transfers between devices, exchange(): return lax.ppermute(value, AXES, pairs)  22.1 us
    all_to_all x2, blocking collectives, all_sum(): dealt = lax.all_to_all(copies, AXES, 0, 0, axis_index_groups=groups)  19.8 us
    pallas_call x8, Pallas kernels, kernel_call(): pl.pallas_call(body, in_specs=[whole] * len(operands), out_specs=[whole]...  15 us
    all_to_all x1, starting transfers between devices, deal(): lax.all_to_all(blocks.reshape(count, rows, LANES), AXES, 0, 0, axis_index...  6.76 us
    all_to_all x1, waiting for transfers between devices, deal(): lax.all_to_all(blocks.reshape(count, rows, LANES), AXES, 0, 0, axis_index...  3.25 us
  transfers between devices with their start and end apart: 10, of which 2 were waited for; matrix products, arithmetic and copies ran while one was open for 1% of the time, Pallas kernels for 7%

profile of v7, /device:TPU:1, one launch (start us, length us, event | category | flops | bytes accessed | tf_op | source)
XLA Modules:
  0.0 139.0 jit_solution(6740485856464584198)
XLA Ops:
  0.6 1.4 %shard_map.50 = (f32[72,128]{1,0:T(8,128)}, f32[128,128]{1,0:T(8,128)}) custom-call(f32[64,128]{1,0:T(8,128)} %right_ref.1, f32[2,128]{1,0:T(2,128)} %points_ref.1, f32[1,128]{1,0:T(1,128)} %bitcast.31), custom_call_target="tpu_custom_call" | custom-call | tf_op jit(solution)/shard_map/pallas_call | solution.py:275
  2.1 7.4 %collective-permute-start.2 = (f32[72,128]{1,0:T(8,128)}, f32[72,128]{1,0:T(8,128)S(1)}, u32[]{:S(2)}, u32[]{:S(2)}) collective-permute-start(f32[72,128]{1,0:T(8,128)} %get-tuple-element.20.packed_ref), channel_id=1, source_target_pairs={{0,18},{1,19},{2,16},{3,17},{4,22},{5,23},{6,20},{7,21},{8,26},{9,... | collective-permute-start | bytes 110600 | tf_op jit(solution)/shard_map/ppermute | solution.py:68
  10.6 6.8 %all-to-all-start = ((f32[16,8,128]{2,1,0:T(8,128)}), f32[16,8,128]{2,1,0:T(8,128)S(1)}, u32[]{:S(2)}, u32[]{:S(2)}) async-start(f32[16,8,128]{2,1,0:T(8,128)} %bitcast.30), calls=%async_computation | async-start | bytes 131072 | tf_op jit(solution)/shard_map/all_to_all | solution.py:79
  18.2 1.6 %collective-permute-start.4 = (f32[288,128]{1,0:T(8,128)S(1)}, f32[288,128]{1,0:T(8,128)S(1)}, u32[]{:S(2)}, u32[]{:S(2)}) collective-permute-start(f32[288,128]{1,0:T(8,128)S(1)} %constant_dynamic-update-slice_fusion.v_ref.right_near_ref), channel_id=1, source_target_pairs={{0,1},{1,0},{2,3},{3,2},{4,5},{5,4},{6,7},{7,6},{8,9},{9,8},{10,11... | collective-permute-start | bytes 442376 | tf_op jit(solution)/shard_map/ppermute | solution.py:68
  20.7 3.2 %all-to-all-done = f32[16,8,128]{2,1,0:T(8,128)S(1)} async-done(((f32[16,8,128]{2,1,0:T(8,128)}), f32[16,8,128]{2,1,0:T(8,128)S(1)}, u32[]{:S(2)}, u32[]{:S(2)}) %all-to-all-start) | async-done | bytes 65568 | tf_op jit(solution)/shard_map/all_to_all | solution.py:79
  23.9 2.4 %shard_map.51 = (f32[1024,128]{1,0:T(8,128)S(1)}, bf16[8,512,512]{2,1,0:T(8,128)(2,1)S(1)}) custom-call(f32[288,128]{1,0:T(8,128)S(1)} %constant_dynamic-update-slice_fusion.v_ref.right_near_ref, f32[128,128]{1,0:T(8,128)S(1)} %bitcast.26), custom_call_target="tpu_custom_call" | custom-call | flops 3221225472 | tf_op jit(solution)/shard_map/pallas_call | solution.py:201
  26.4 2.4 %shard_map.52 = (f32[1024,128]{1,0:T(8,128)S(1)}, bf16[8,512,512]{2,1,0:T(8,128)(2,1)S(1)}) custom-call(f32[288,128]{1,0:T(8,128)S(1)} %collective-permute-done.4.v_ref.right_near_ref, f32[128,128]{1,0:T(8,128)S(1)} %bitcast.27, f32[1024,128]{1,0:T(8,128)S(1)} %get-tuple-element.22.refs_0_), custom_call_target="tpu_custom_call" | custom-call | flops 3221225472 | tf_op jit(solution)/shard_map/pallas_call | solution.py:201
  28.8 2.9 %collective-permute-start.5 = (f32[288,128]{1,0:T(8,128)S(1)}, f32[288,128]{1,0:T(8,128)S(1)}, u32[]{:S(2)}, u32[]{:S(2)}) collective-permute-start(f32[288,128]{1,0:T(8,128)S(1)} %collective-permute-done.3.v_ref.right_far_ref), channel_id=1, source_target_pairs={{0,1},{1,0},{2,3},{3,2},{4,5},{5,4},{6,7},{7,6},{8,9},{9,8},{10,11... | collective-permute-start | bytes 442376 | tf_op jit(solution)/shard_map/ppermute | solution.py:68
  31.7 2.5 %shard_map.53 = (f32[1024,128]{1,0:T(8,128)S(1)}, bf16[8,512,512]{2,1,0:T(8,128)(2,1)S(1)}) custom-call(f32[288,128]{1,0:T(8,128)S(1)} %collective-permute-done.3.v_ref.right_far_ref, f32[128,128]{1,0:T(8,128)S(1)} %bitcast.28, f32[1024,128]{1,0:T(8,128)S(1)} %get-tuple-element.25.refs_0_), custom_call_target="tpu_custom_call" | custom-call | flops 3221225472 | tf_op jit(solution)/shard_map/pallas_call | solution.py:201
  34.2 2.5 %shard_map.54 = (f32[1024,128]{1,0:T(8,128)S(1)}, bf16[8,512,512]{2,1,0:T(8,128)(2,1)S(1)}) custom-call(f32[288,128]{1,0:T(8,128)S(1)} %collective-permute-done.5.v_ref.right_far_ref, f32[128,128]{1,0:T(8,128)S(1)} %bitcast.29, f32[1024,128]{1,0:T(8,128)S(1)} %get-tuple-element.26.refs_0_), custom_call_target="tpu_custom_call" | custom-call | flops 3221225472 | tf_op jit(solution)/shard_map/pallas_call | solution.py:201
  36.7 13.9 %all_to_all.40 = f32[16,64,128]{2,1,0:T(8,128)S(1)} all-to-all(f32[16,64,128]{2,1,0:T(8,128)S(1)} %bitcast.25), channel_id=1, replica_groups={{0,4,8,12,64,68,72,76,128,132,136,140,192,196,200,204},{1,5,9,13,65,69,..., dimensions={0} | all-to-all | bytes 1048576 | tf_op jit(solution)/shard_map/all_to_all | solution.py:79
  50.7 12.9 %all_to_all.41 = f32[8,64,128]{2,1,0:T(8,128)S(1)} all-to-all(f32[8,64,128]{2,1,0:T(8,128)S(1)} %bitcast.13), channel_id=1, replica_groups={{0,2,32,34,16,18,48,50},{1,3,33,35,17,19,49,51},{4,6,36,38,20,22,52,54}..., dimensions={0} | all-to-all | bytes 524288 | tf_op jit(solution)/shard_map/all_to_all | solution.py:79
  63.6 3.2 %collective-permute-start.6 = (f32[512,128]{1,0:T(8,128)S(1)}, f32[512,128]{1,0:T(8,128)S(1)}, u32[]{:S(2)}, u32[]{:S(2)}) collective-permute-start(f32[512,128]{1,0:T(8,128)S(1)} %bitcast.16), channel_id=1, source_target_pairs={{0,1},{1,0},{2,3},{3,2},{4,5},{5,4},{6,7},{7,6},{8,9},{9,8},{10,11... | collective-permute-start | bytes 786440 | tf_op jit(solution)/shard_map/ppermute | solution.py:68
  66.8 1.3 shard_map.56.refs_0_
  68.1 1.3 shard_map.57
  69.4 14.3 %all_to_all.42 = f32[16,72,128]{2,1,0:T(8,128)S(1)} all-to-all(f32[16,72,128]{2,1,0:T(8,128)S(1)} %bitcast.15), channel_id=1, replica_groups={{0,4,8,12,64,68,72,76,128,132,136,140,192,196,200,204},{1,5,9,13,65,69,..., dimensions={0} | all-to-all | bytes 1179648 | tf_op jit(solution)/shard_map/all_to_all | solution.py:79
  83.8 11.3 %all_to_all.43 = f32[8,64,128]{2,1,0:T(8,128)S(1)} all-to-all(f32[8,64,128]{2,1,0:T(8,128)S(1)} %bitcast.24), channel_id=1, replica_groups={{0,2,32,34,16,18,48,50},{1,3,33,35,17,19,49,51},{4,6,36,38,20,22,52,54}..., dimensions={0} | all-to-all | bytes 524288 | tf_op jit(solution)/shard_map/all_to_all | solution.py:79
  95.1 3.3 %collective-permute-start.7 = (f32[512,128]{1,0:T(8,128)S(1)}, f32[512,128]{1,0:T(8,128)S(1)}, u32[]{:S(2)}, u32[]{:S(2)}) collective-permute-start(f32[512,128]{1,0:T(8,128)S(1)} %bitcast.22), channel_id=1, source_target_pairs={{0,1},{1,0},{2,3},{3,2},{4,5},{5,4},{6,7},{7,6},{8,9},{9,8},{10,11... | collective-permute-start | bytes 786440 | tf_op jit(solution)/shard_map/ppermute | solution.py:68
  98.4 1.3 shard_map.59.refs_2_
  99.7 1.3 shard_map.60
  101.1 14.6 %all_to_all.44 = f32[16,72,128]{2,1,0:T(8,128)S(1)} all-to-all(f32[16,72,128]{2,1,0:T(8,128)S(1)} %bitcast.14), channel_id=1, replica_groups={{0,4,8,12,64,68,72,76,128,132,136,140,192,196,200,204},{1,5,9,13,65,69,..., dimensions={0} | all-to-all | bytes 1179648 | tf_op jit(solution)/shard_map/all_to_all | solution.py:79
  115.9 1.7 %collective-permute-start.8 = (f32[8,128]{1,0:T(8,128)S(1)}, f32[8,128]{1,0:T(8,128)S(1)}, u32[]{:S(2)}, u32[]{:S(2)}) collective-permute-start(f32[8,128]{1,0:T(8,128)S(1)} %get-tuple-element.35), channel_id=1, source_target_pairs={{0,1},{1,0},{2,3},{3,2},{4,5},{5,4},{6,7},{7,6},{8,9},{9,8},{10,11... | collective-permute-start | bytes 12296 | tf_op jit(solution)/shard_map/ppermute | solution.py:68
  118.4 9.4 %all_to_all.45 = f32[16,8,128]{2,1,0:T(8,128)S(1)} all-to-all(f32[16,8,128]{2,1,0:T(8,128)S(1)} %broadcast_in_dim.7), channel_id=1, replica_groups={{0,4,8,12,64,68,72,76,128,132,136,140,192,196,200,204},{1,5,9,13,65,69,..., dimensions={0} | all-to-all | bytes 131072 | tf_op jit(solution)/shard_map/all_to_all | solution.py:89
  127.8 10.5 %all_to_all.46 = f32[8,8,128]{2,1,0:T(8,128)S(1)} all-to-all(f32[8,8,128]{2,1,0:T(8,128)S(1)} %broadcast_in_dim.8), channel_id=1, replica_groups={{0,2,32,34,16,18,48,50},{1,3,33,35,17,19,49,51},{4,6,36,38,20,22,52,54}..., dimensions={0} | all-to-all | bytes 65536 | tf_op jit(solution)/shard_map/all_to_all | solution.py:89
  (27 shorter events, 4.8 us)
Async XLA Ops:
  2.1 16.1 %collective-permute-start.2 = (f32[72,128]{1,0:T(8,128)}, f32[72,128]{1,0:T(8,128)S(1)}, u32[]{:S(2)}, u32[]{:S(2)}) collective-permute-start(f32[72,128]{1,0:T(8,128)} %get-tuple-element.20.packed_ref), channel_id=1, source_target_pairs={{0,18},{1,19},{2,16},{3,17},{4,22},{5,23},{6,20},{7,21},{8,26},{9,... | collective-permute-start | bytes 110600 | tf_op jit(solution)/shard_map/ppermute | solution.py:68
  9.4 8.7 %collective-permute-start.1 = (f32[72,128]{1,0:T(8,128)}, f32[72,128]{1,0:T(8,128)S(1)}, u32[]{:S(2)}, u32[]{:S(2)}) collective-permute-start(f32[72,128]{1,0:T(8,128)} %get-tuple-element.20.packed_ref), channel_id=1, source_target_pairs={{0,32},{1,33},{2,34},{3,35},{4,36},{5,37},{6,38},{7,39},{8,40},{9,... | collective-permute-start | bytes 110600 | tf_op jit(solution)/shard_map/ppermute | solution.py:68
  10.6 7.5 %collective-permute-start = (f32[72,128]{1,0:T(8,128)}, f32[72,128]{1,0:T(8,128)S(1)}, u32[]{:S(2)}, u32[]{:S(2)}) collective-permute-start(f32[72,128]{1,0:T(8,128)} %get-tuple-element.20.packed_ref), channel_id=1, source_target_pairs={{0,50},{1,51},{2,48},{3,49},{4,54},{5,55},{6,52},{7,53},{8,58},{9,... | collective-permute-start | bytes 110600 | tf_op jit(solution)/shard_map/ppermute | solution.py:68
  10.6 13.3 %all-to-all-start = ((f32[16,8,128]{2,1,0:T(8,128)}), f32[16,8,128]{2,1,0:T(8,128)S(1)}, u32[]{:S(2)}, u32[]{:S(2)}) async-start(f32[16,8,128]{2,1,0:T(8,128)} %bitcast.30), calls=%async_computation | async-start | bytes 131072 | tf_op jit(solution)/shard_map/all_to_all | solution.py:79
  18.2 8.1 %collective-permute-start.4 = (f32[288,128]{1,0:T(8,128)S(1)}, f32[288,128]{1,0:T(8,128)S(1)}, u32[]{:S(2)}, u32[]{:S(2)}) collective-permute-start(f32[288,128]{1,0:T(8,128)S(1)} %constant_dynamic-update-slice_fusion.v_ref.right_near_ref), channel_id=1, source_target_pairs={{0,1},{1,0},{2,3},{3,2},{4,5},{5,4},{6,7},{7,6},{8,9},{9,8},{10,11... | collective-permute-start | bytes 442376 | tf_op jit(solution)/shard_map/ppermute | solution.py:68
  19.8 9.0 %collective-permute-start.3 = (f32[288,128]{1,0:T(8,128)S(1)}, f32[288,128]{1,0:T(8,128)S(1)}, u32[]{:S(2)}, u32[]{:S(2)}) collective-permute-start(f32[288,128]{1,0:T(8,128)S(1)} %constant_dynamic-update-slice_fusion.v_ref.right_near_ref), channel_id=1, source_target_pairs={{0,16},{1,17},{2,18},{3,19},{4,20},{5,21},{6,22},{7,23},{8,24},{9,... | collective-permute-start | bytes 442376 | tf_op jit(solution)/shard_map/ppermute | solution.py:68
  28.8 5.4 %collective-permute-start.5 = (f32[288,128]{1,0:T(8,128)S(1)}, f32[288,128]{1,0:T(8,128)S(1)}, u32[]{:S(2)}, u32[]{:S(2)}) collective-permute-start(f32[288,128]{1,0:T(8,128)S(1)} %collective-permute-done.3.v_ref.right_far_ref), channel_id=1, source_target_pairs={{0,1},{1,0},{2,3},{3,2},{4,5},{5,4},{6,7},{7,6},{8,9},{9,8},{10,11... | collective-permute-start | bytes 442376 | tf_op jit(solution)/shard_map/ppermute | solution.py:68
  34.2 16.4 %copy-start = (f32[72,128]{1,0:T(8,128)S(1)}, f32[72,128]{1,0:T(8,128)}, u32[]{:S(2)}) copy-start(f32[72,128]{1,0:T(8,128)} %get-tuple-element.20.packed_ref) | copy-start | bytes 110596
  63.6 4.5 %collective-permute-start.6 = (f32[512,128]{1,0:T(8,128)S(1)}, f32[512,128]{1,0:T(8,128)S(1)}, u32[]{:S(2)}, u32[]{:S(2)}) collective-permute-start(f32[512,128]{1,0:T(8,128)S(1)} %bitcast.16), channel_id=1, source_target_pairs={{0,1},{1,0},{2,3},{3,2},{4,5},{5,4},{6,7},{7,6},{8,9},{9,8},{10,11... | collective-permute-start | bytes 786440 | tf_op jit(solution)/shard_map/ppermute | solution.py:68
  95.1 4.6 %collective-permute-start.7 = (f32[512,128]{1,0:T(8,128)S(1)}, f32[512,128]{1,0:T(8,128)S(1)}, u32[]{:S(2)}, u32[]{:S(2)}) collective-permute-start(f32[512,128]{1,0:T(8,128)S(1)} %bitcast.22), channel_id=1, source_target_pairs={{0,1},{1,0},{2,3},{3,2},{4,5},{5,4},{6,7},{7,6},{8,9},{9,8},{10,11... | collective-permute-start | bytes 786440 | tf_op jit(solution)/shard_map/ppermute | solution.py:68
  115.9 2.5 %collective-permute-start.8 = (f32[8,128]{1,0:T(8,128)S(1)}, f32[8,128]{1,0:T(8,128)S(1)}, u32[]{:S(2)}, u32[]{:S(2)}) collective-permute-start(f32[8,128]{1,0:T(8,128)S(1)} %get-tuple-element.35), channel_id=1, source_target_pairs={{0,1},{1,0},{2,3},{3,2},{4,5},{5,4},{6,7},{7,6},{8,9},{9,8},{10,11... | collective-permute-start | bytes 12296 | tf_op jit(solution)/shard_map/ppermute | solution.py:68

commit v8 on v7

--- a/solution.py
+++ b/solution.py
@@ -84,7 +84,7 @@
 
 def all_sum(block):
     block = block + exchange(block, "core", 1)
-    for groups in (PLANES, LINES):
+    for groups in (LINES, PLANES):
         copies = jnp.broadcast_to(block[None], (len(groups[0]),) + block.shape)
         dealt = lax.all_to_all(copies, AXES, 0, 0, axis_index_groups=groups)
         block = jnp.sum(dealt, axis=0)

time: 140 us -> 140 us (level)
  no operation moved by 1% of the time
where the time goes in v8:
time: 140 us; the launch traced here: 139 us
  blocking collectives  86.8 us (62%)
  starting transfers between devices  28.9 us (21%)
  Pallas kernels  17.6 us (13%)
  waiting for transfers between devices  4.09 us (3%)
    all_to_all x5, blocking collectives, deal(): lax.all_to_all(blocks.reshape(count, rows, LANES), AXES, 0, 0, axis_index...  67 us
    ppermute x9, starting transfers between devices, exchange(): return lax.ppermute(value, AXES, pairs)  22.1 us
    all_to_all x2, blocking collectives, all_sum(): dealt = lax.all_to_all(copies, AXES, 0, 0, axis_index_groups=groups)  19.8 us
    pallas_call x8, Pallas kernels, kernel_call(): pl.pallas_call(body, in_specs=[whole] * len(operands), out_specs=[whole]...  15 us
    all_to_all x1, starting transfers between devices, deal(): lax.all_to_all(blocks.reshape(count, rows, LANES), AXES, 0, 0, axis_index...  6.76 us
    all_to_all x1, waiting for transfers between devices, deal(): lax.all_to_all(blocks.reshape(count, rows, LANES), AXES, 0, 0, axis_index...  3.25 us
  transfers between devices with their start and end apart: 10, of which 2 were waited for; matrix products, arithmetic and copies ran while one was open for 1% of the time, Pallas kernels for 7%

profile of v8, /device:TPU:1, one launch (start us, length us, event | category | flops | bytes accessed | tf_op | source)
XLA Modules:
  0.0 139.0 jit_solution(13016002991973674474)
XLA Ops:
  0.6 1.4 %shard_map.50 = (f32[72,128]{1,0:T(8,128)}, f32[128,128]{1,0:T(8,128)}) custom-call(f32[64,128]{1,0:T(8,128)} %right_ref.1, f32[2,128]{1,0:T(2,128)} %points_ref.1, f32[1,128]{1,0:T(1,128)} %bitcast.31), custom_call_target="tpu_custom_call" | custom-call | tf_op jit(solution)/shard_map/pallas_call | solution.py:275
  2.1 7.4 %collective-permute-start.2 = (f32[72,128]{1,0:T(8,128)}, f32[72,128]{1,0:T(8,128)S(1)}, u32[]{:S(2)}, u32[]{:S(2)}) collective-permute-start(f32[72,128]{1,0:T(8,128)} %get-tuple-element.20.packed_ref), channel_id=1, source_target_pairs={{0,18},{1,19},{2,16},{3,17},{4,22},{5,23},{6,20},{7,21},{8,26},{9,... | collective-permute-start | bytes 110600 | tf_op jit(solution)/shard_map/ppermute | solution.py:68
  10.6 6.8 %all-to-all-start = ((f32[16,8,128]{2,1,0:T(8,128)}), f32[16,8,128]{2,1,0:T(8,128)S(1)}, u32[]{:S(2)}, u32[]{:S(2)}) async-start(f32[16,8,128]{2,1,0:T(8,128)} %bitcast.30), calls=%async_computation | async-start | bytes 131072 | tf_op jit(solution)/shard_map/all_to_all | solution.py:79
  18.2 1.6 %collective-permute-start.4 = (f32[288,128]{1,0:T(8,128)S(1)}, f32[288,128]{1,0:T(8,128)S(1)}, u32[]{:S(2)}, u32[]{:S(2)}) collective-permute-start(f32[288,128]{1,0:T(8,128)S(1)} %constant_dynamic-update-slice_fusion.v_ref.right_near_ref), channel_id=1, source_target_pairs={{0,1},{1,0},{2,3},{3,2},{4,5},{5,4},{6,7},{7,6},{8,9},{9,8},{10,11... | collective-permute-start | bytes 442376 | tf_op jit(solution)/shard_map/ppermute | solution.py:68
  20.7 3.2 %all-to-all-done = f32[16,8,128]{2,1,0:T(8,128)S(1)} async-done(((f32[16,8,128]{2,1,0:T(8,128)}), f32[16,8,128]{2,1,0:T(8,128)S(1)}, u32[]{:S(2)}, u32[]{:S(2)}) %all-to-all-start) | async-done | bytes 65568 | tf_op jit(solution)/shard_map/all_to_all | solution.py:79
  23.9 2.4 %shard_map.51 = (f32[1024,128]{1,0:T(8,128)S(1)}, bf16[8,512,512]{2,1,0:T(8,128)(2,1)S(1)}) custom-call(f32[288,128]{1,0:T(8,128)S(1)} %constant_dynamic-update-slice_fusion.v_ref.right_near_ref, f32[128,128]{1,0:T(8,128)S(1)} %bitcast.26), custom_call_target="tpu_custom_call" | custom-call | flops 3221225472 | tf_op jit(solution)/shard_map/pallas_call | solution.py:201
  26.4 2.4 %shard_map.52 = (f32[1024,128]{1,0:T(8,128)S(1)}, bf16[8,512,512]{2,1,0:T(8,128)(2,1)S(1)}) custom-call(f32[288,128]{1,0:T(8,128)S(1)} %collective-permute-done.4.v_ref.right_near_ref, f32[128,128]{1,0:T(8,128)S(1)} %bitcast.27, f32[1024,128]{1,0:T(8,128)S(1)} %get-tuple-element.22.refs_0_), custom_call_target="tpu_custom_call" | custom-call | flops 3221225472 | tf_op jit(solution)/shard_map/pallas_call | solution.py:201
  28.8 2.9 %collective-permute-start.5 = (f32[288,128]{1,0:T(8,128)S(1)}, f32[288,128]{1,0:T(8,128)S(1)}, u32[]{:S(2)}, u32[]{:S(2)}) collective-permute-start(f32[288,128]{1,0:T(8,128)S(1)} %collective-permute-done.3.v_ref.right_far_ref), channel_id=1, source_target_pairs={{0,1},{1,0},{2,3},{3,2},{4,5},{5,4},{6,7},{7,6},{8,9},{9,8},{10,11... | collective-permute-start | bytes 442376 | tf_op jit(solution)/shard_map/ppermute | solution.py:68
  31.7 2.5 %shard_map.53 = (f32[1024,128]{1,0:T(8,128)S(1)}, bf16[8,512,512]{2,1,0:T(8,128)(2,1)S(1)}) custom-call(f32[288,128]{1,0:T(8,128)S(1)} %collective-permute-done.3.v_ref.right_far_ref, f32[128,128]{1,0:T(8,128)S(1)} %bitcast.28, f32[1024,128]{1,0:T(8,128)S(1)} %get-tuple-element.25.refs_0_), custom_call_target="tpu_custom_call" | custom-call | flops 3221225472 | tf_op jit(solution)/shard_map/pallas_call | solution.py:201
  34.2 2.5 %shard_map.54 = (f32[1024,128]{1,0:T(8,128)S(1)}, bf16[8,512,512]{2,1,0:T(8,128)(2,1)S(1)}) custom-call(f32[288,128]{1,0:T(8,128)S(1)} %collective-permute-done.5.v_ref.right_far_ref, f32[128,128]{1,0:T(8,128)S(1)} %bitcast.29, f32[1024,128]{1,0:T(8,128)S(1)} %get-tuple-element.26.refs_0_), custom_call_target="tpu_custom_call" | custom-call | flops 3221225472 | tf_op jit(solution)/shard_map/pallas_call | solution.py:201
  36.7 13.9 %all_to_all.40 = f32[16,64,128]{2,1,0:T(8,128)S(1)} all-to-all(f32[16,64,128]{2,1,0:T(8,128)S(1)} %bitcast.25), channel_id=1, replica_groups={{0,4,8,12,64,68,72,76,128,132,136,140,192,196,200,204},{1,5,9,13,65,69,..., dimensions={0} | all-to-all | bytes 1048576 | tf_op jit(solution)/shard_map/all_to_all | solution.py:79
  50.7 12.9 %all_to_all.41 = f32[8,64,128]{2,1,0:T(8,128)S(1)} all-to-all(f32[8,64,128]{2,1,0:T(8,128)S(1)} %bitcast.13), channel_id=1, replica_groups={{0,2,32,34,16,18,48,50},{1,3,33,35,17,19,49,51},{4,6,36,38,20,22,52,54}..., dimensions={0} | all-to-all | bytes 524288 | tf_op jit(solution)/shard_map/all_to_all | solution.py:79
  63.6 3.2 %collective-permute-start.6 = (f32[512,128]{1,0:T(8,128)S(1)}, f32[512,128]{1,0:T(8,128)S(1)}, u32[]{:S(2)}, u32[]{:S(2)}) collective-permute-start(f32[512,128]{1,0:T(8,128)S(1)} %bitcast.16), channel_id=1, source_target_pairs={{0,1},{1,0},{2,3},{3,2},{4,5},{5,4},{6,7},{7,6},{8,9},{9,8},{10,11... | collective-permute-start | bytes 786440 | tf_op jit(solution)/shard_map/ppermute | solution.py:68
  66.8 1.3 shard_map.56.refs_0_
  68.1 1.3 shard_map.57
  69.4 14.3 %all_to_all.42 = f32[16,72,128]{2,1,0:T(8,128)S(1)} all-to-all(f32[16,72,128]{2,1,0:T(8,128)S(1)} %bitcast.15), channel_id=1, replica_groups={{0,4,8,12,64,68,72,76,128,132,136,140,192,196,200,204},{1,5,9,13,65,69,..., dimensions={0} | all-to-all | bytes 1179648 | tf_op jit(solution)/shard_map/all_to_all | solution.py:79
  83.8 11.3 %all_to_all.43 = f32[8,64,128]{2,1,0:T(8,128)S(1)} all-to-all(f32[8,64,128]{2,1,0:T(8,128)S(1)} %bitcast.24), channel_id=1, replica_groups={{0,2,32,34,16,18,48,50},{1,3,33,35,17,19,49,51},{4,6,36,38,20,22,52,54}..., dimensions={0} | all-to-all | bytes 524288 | tf_op jit(solution)/shard_map/all_to_all | solution.py:79
  95.1 3.3 %collective-permute-start.7 = (f32[512,128]{1,0:T(8,128)S(1)}, f32[512,128]{1,0:T(8,128)S(1)}, u32[]{:S(2)}, u32[]{:S(2)}) collective-permute-start(f32[512,128]{1,0:T(8,128)S(1)} %bitcast.22), channel_id=1, source_target_pairs={{0,1},{1,0},{2,3},{3,2},{4,5},{5,4},{6,7},{7,6},{8,9},{9,8},{10,11... | collective-permute-start | bytes 786440 | tf_op jit(solution)/shard_map/ppermute | solution.py:68
  98.4 1.3 shard_map.59.refs_2_
  99.7 1.3 shard_map.60
  101.1 14.6 %all_to_all.44 = f32[16,72,128]{2,1,0:T(8,128)S(1)} all-to-all(f32[16,72,128]{2,1,0:T(8,128)S(1)} %bitcast.14), channel_id=1, replica_groups={{0,4,8,12,64,68,72,76,128,132,136,140,192,196,200,204},{1,5,9,13,65,69,..., dimensions={0} | all-to-all | bytes 1179648 | tf_op jit(solution)/shard_map/all_to_all | solution.py:79
  115.9 1.7 %collective-permute-start.8 = (f32[8,128]{1,0:T(8,128)S(1)}, f32[8,128]{1,0:T(8,128)S(1)}, u32[]{:S(2)}, u32[]{:S(2)}) collective-permute-start(f32[8,128]{1,0:T(8,128)S(1)} %get-tuple-element.35), channel_id=1, source_target_pairs={{0,1},{1,0},{2,3},{3,2},{4,5},{5,4},{6,7},{7,6},{8,9},{9,8},{10,11... | collective-permute-start | bytes 12296 | tf_op jit(solution)/shard_map/ppermute | solution.py:68
  118.4 10.5 %all_to_all.45 = f32[8,8,128]{2,1,0:T(8,128)S(1)} all-to-all(f32[8,8,128]{2,1,0:T(8,128)S(1)} %broadcast_in_dim.7), channel_id=1, replica_groups={{0,2,32,34,16,18,48,50},{1,3,33,35,17,19,49,51},{4,6,36,38,20,22,52,54}..., dimensions={0} | all-to-all | bytes 65536 | tf_op jit(solution)/shard_map/all_to_all | solution.py:89
  128.9 9.4 %all_to_all.46 = f32[16,8,128]{2,1,0:T(8,128)S(1)} all-to-all(f32[16,8,128]{2,1,0:T(8,128)S(1)} %broadcast_in_dim.8), channel_id=1, replica_groups={{0,4,8,12,64,68,72,76,128,132,136,140,192,196,200,204},{1,5,9,13,65,69,..., dimensions={0} | all-to-all | bytes 131072 | tf_op jit(solution)/shard_map/all_to_all | solution.py:89
  (27 shorter events, 4.8 us)
Async XLA Ops:
  2.1 16.1 %collective-permute-start.2 = (f32[72,128]{1,0:T(8,128)}, f32[72,128]{1,0:T(8,128)S(1)}, u32[]{:S(2)}, u32[]{:S(2)}) collective-permute-start(f32[72,128]{1,0:T(8,128)} %get-tuple-element.20.packed_ref), channel_id=1, source_target_pairs={{0,18},{1,19},{2,16},{3,17},{4,22},{5,23},{6,20},{7,21},{8,26},{9,... | collective-permute-start | bytes 110600 | tf_op jit(solution)/shard_map/ppermute | solution.py:68
  9.4 8.7 %collective-permute-start.1 = (f32[72,128]{1,0:T(8,128)}, f32[72,128]{1,0:T(8,128)S(1)}, u32[]{:S(2)}, u32[]{:S(2)}) collective-permute-start(f32[72,128]{1,0:T(8,128)} %get-tuple-element.20.packed_ref), channel_id=1, source_target_pairs={{0,32},{1,33},{2,34},{3,35},{4,36},{5,37},{6,38},{7,39},{8,40},{9,... | collective-permute-start | bytes 110600 | tf_op jit(solution)/shard_map/ppermute | solution.py:68
  10.6 7.5 %collective-permute-start = (f32[72,128]{1,0:T(8,128)}, f32[72,128]{1,0:T(8,128)S(1)}, u32[]{:S(2)}, u32[]{:S(2)}) collective-permute-start(f32[72,128]{1,0:T(8,128)} %get-tuple-element.20.packed_ref), channel_id=1, source_target_pairs={{0,50},{1,51},{2,48},{3,49},{4,54},{5,55},{6,52},{7,53},{8,58},{9,... | collective-permute-start | bytes 110600 | tf_op jit(solution)/shard_map/ppermute | solution.py:68
  10.6 13.3 %all-to-all-start = ((f32[16,8,128]{2,1,0:T(8,128)}), f32[16,8,128]{2,1,0:T(8,128)S(1)}, u32[]{:S(2)}, u32[]{:S(2)}) async-start(f32[16,8,128]{2,1,0:T(8,128)} %bitcast.30), calls=%async_computation | async-start | bytes 131072 | tf_op jit(solution)/shard_map/all_to_all | solution.py:79
  18.2 8.1 %collective-permute-start.4 = (f32[288,128]{1,0:T(8,128)S(1)}, f32[288,128]{1,0:T(8,128)S(1)}, u32[]{:S(2)}, u32[]{:S(2)}) collective-permute-start(f32[288,128]{1,0:T(8,128)S(1)} %constant_dynamic-update-slice_fusion.v_ref.right_near_ref), channel_id=1, source_target_pairs={{0,1},{1,0},{2,3},{3,2},{4,5},{5,4},{6,7},{7,6},{8,9},{9,8},{10,11... | collective-permute-start | bytes 442376 | tf_op jit(solution)/shard_map/ppermute | solution.py:68
  19.8 9.0 %collective-permute-start.3 = (f32[288,128]{1,0:T(8,128)S(1)}, f32[288,128]{1,0:T(8,128)S(1)}, u32[]{:S(2)}, u32[]{:S(2)}) collective-permute-start(f32[288,128]{1,0:T(8,128)S(1)} %constant_dynamic-update-slice_fusion.v_ref.right_near_ref), channel_id=1, source_target_pairs={{0,16},{1,17},{2,18},{3,19},{4,20},{5,21},{6,22},{7,23},{8,24},{9,... | collective-permute-start | bytes 442376 | tf_op jit(solution)/shard_map/ppermute | solution.py:68
  28.8 5.4 %collective-permute-start.5 = (f32[288,128]{1,0:T(8,128)S(1)}, f32[288,128]{1,0:T(8,128)S(1)}, u32[]{:S(2)}, u32[]{:S(2)}) collective-permute-start(f32[288,128]{1,0:T(8,128)S(1)} %collective-permute-done.3.v_ref.right_far_ref), channel_id=1, source_target_pairs={{0,1},{1,0},{2,3},{3,2},{4,5},{5,4},{6,7},{7,6},{8,9},{9,8},{10,11... | collective-permute-start | bytes 442376 | tf_op jit(solution)/shard_map/ppermute | solution.py:68
  34.2 16.4 %copy-start = (f32[72,128]{1,0:T(8,128)S(1)}, f32[72,128]{1,0:T(8,128)}, u32[]{:S(2)}) copy-start(f32[72,128]{1,0:T(8,128)} %get-tuple-element.20.packed_ref) | copy-start | bytes 110596
  63.6 4.5 %collective-permute-start.6 = (f32[512,128]{1,0:T(8,128)S(1)}, f32[512,128]{1,0:T(8,128)S(1)}, u32[]{:S(2)}, u32[]{:S(2)}) collective-permute-start(f32[512,128]{1,0:T(8,128)S(1)} %bitcast.16), channel_id=1, source_target_pairs={{0,1},{1,0},{2,3},{3,2},{4,5},{5,4},{6,7},{7,6},{8,9},{9,8},{10,11... | collective-permute-start | bytes 786440 | tf_op jit(solution)/shard_map/ppermute | solution.py:68
  95.1 4.6 %collective-permute-start.7 = (f32[512,128]{1,0:T(8,128)S(1)}, f32[512,128]{1,0:T(8,128)S(1)}, u32[]{:S(2)}, u32[]{:S(2)}) collective-permute-start(f32[512,128]{1,0:T(8,128)S(1)} %bitcast.22), channel_id=1, source_target_pairs={{0,1},{1,0},{2,3},{3,2},{4,5},{5,4},{6,7},{7,6},{8,9},{9,8},{10,11... | collective-permute-start | bytes 786440 | tf_op jit(solution)/shard_map/ppermute | solution.py:68
  115.9 2.5 %collective-permute-start.8 = (f32[8,128]{1,0:T(8,128)S(1)}, f32[8,128]{1,0:T(8,128)S(1)}, u32[]{:S(2)}, u32[]{:S(2)}) collective-permute-start(f32[8,128]{1,0:T(8,128)S(1)} %get-tuple-element.35), channel_id=1, source_target_pairs={{0,1},{1,0},{2,3},{3,2},{4,5},{5,4},{6,7},{7,6},{8,9},{9,8},{10,11... | collective-permute-start | bytes 12296 | tf_op jit(solution)/shard_map/ppermute | solution.py:68

commit v9 on v7

--- a/solution.py
+++ b/solution.py
@@ -250,39 +250,6 @@
         tile = jnp.where(lane == i, column, tile)
     square = jnp.concatenate([tile, jnp.zeros((LANES - rhs, LANES), jnp.float32)], axis=0)
     return square.T[:SPARE, :]
-
-
-def pack(rhs, right_ref, points_ref, noise_ref, out_ref, places_ref, spare_ref, semaphores):
-    spare_ref[...] = jnp.zeros_like(spare_ref)
-    copies = [
-        pltpu.make_async_copy(right_ref, out_ref.at[pl.ds(0, rhs), :], semaphores.at[0]),
-        pltpu.make_async_copy(points_ref, spare_ref.at[pl.ds(0, 2), :], semaphores.at[1]),
-        pltpu.make_async_copy(noise_ref, spare_ref.at[pl.ds(2, 1), :], semaphores.at[2]),
-    ]
-    for copy in copies:
-        copy.start()
-    for copy in copies:
-        copy.wait()
-    spare = spare_ref[...]
-    out_ref[rhs:, :] = spare
-    for at in range(0, places_ref.shape[0], SPARE):
-        places_ref[at : at + SPARE, :] = spare
-
-
-def packed_inputs(right_side, points, noise):
-    rhs, own = right_side.shape
-    anywhere, whole = pl.BlockSpec(memory_space=pl.ANY), pl.BlockSpec(memory_space=pltpu.VMEM)
-    return pl.pallas_call(
-        functools.partial(pack, rhs),
-        in_specs=[anywhere] * 3,
-        out_specs=[whole] * 2,
-        out_shape=[
-            jax.ShapeDtypeStruct((rhs + SPARE, own), jnp.float32),
-            jax.ShapeDtypeStruct((SPARE * len(PLANES[0]), own), jnp.float32),
-        ],
-        scratch_shapes=[pltpu.VMEM((SPARE, own), jnp.float32), pltpu.SemaphoreType.DMA((3,))],
-        compiler_params=pltpu.CompilerParams(vmem_limit_bytes=60 * 1024 * 1024),
-    )(right_side, points, noise)
 
 
 def summed(dealt_ref, step):
@@ -375,8 +342,10 @@
     amplitude = KERNEL_WEIGHT / total_stars
     vector, spare, copies = (rhs, own), (SPARE, own), (rhs * len(BLOCKS), own)
 
-    packed, places = packed_inputs(right_side, points, star_noise[None, :])
-    row_points = deal(places, PLANES)
+    empty = jnp.zeros((SPARE - 3, own), jnp.float32)
+    packed = jnp.concatenate([right_side, points, star_noise[None, :], empty], axis=0)
+    packed = lax.optimization_barrier(packed)
+    row_points = deal(jnp.tile(packed[rhs:], (len(PLANES[0]), 1)), PLANES)
     rights, kernels, pieces = [], [], None
     near, far = near_and_far(packed)
     for n, half in enumerate((near, far)):

time: 140 us -> 140 us (level)
  Pallas kernels: 17.6 us -> 16.1 us
    pallas_call x1 -> x0, Pallas kernels: 1.42 us -> none  [packed_inputs(): pl.pallas_call(functools.partial(pack, rhs), in_specs=[anywhere] * 3, out...]
  transfers between devices with their start and end apart: 10 -> 10, of which waited for: 2 -> 2; matrix products, arithmetic and copies ran while one was open for 1% -> 0% of each run, Pallas kernels for 7% -> 7%
where the time goes in v9:
time: 140 us; the launch traced here: 139 us
  blocking collectives  86.8 us (62%)
  starting transfers between devices  28.9 us (21%)
  Pallas kernels  16.1 us (12%)
  waiting for transfers between devices  4.87 us (3%)
    all_to_all x5, blocking collectives, deal(): lax.all_to_all(blocks.reshape(count, rows, LANES), AXES, 0, 0, axis_index...  67 us
    ppermute x9, starting transfers between devices, exchange(): return lax.ppermute(value, AXES, pairs)  22.2 us
    all_to_all x2, blocking collectives, all_sum(): dealt = lax.all_to_all(copies, AXES, 0, 0, axis_index_groups=groups)  19.8 us
    pallas_call x8, Pallas kernels, kernel_call(): pl.pallas_call(body, in_specs=[whole] * len(operands), out_specs=[whole]...  15 us
    all_to_all x1, starting transfers between devices, deal(): lax.all_to_all(blocks.reshape(count, rows, LANES), AXES, 0, 0, axis_index...  6.75 us
    all_to_all x1, waiting for transfers between devices, deal(): lax.all_to_all(blocks.reshape(count, rows, LANES), AXES, 0, 0, axis_index...  4.03 us
  transfers between devices with their start and end apart: 10, of which 2 were waited for; matrix products, arithmetic and copies ran while one was open for 0% of the time, Pallas kernels for 7%

profile of v9, /device:TPU:1, one launch (start us, length us, event | category | flops | bytes accessed | tf_op | source)
XLA Modules:
  0.0 139.2 jit_solution(16694217354827415217)
XLA Ops:
  1.6 7.4 %collective-permute-start.2 = (f32[72,128]{1,0:T(8,128)S(1)}, f32[72,128]{1,0:T(8,128)S(1)}, u32[]{:S(2)}, u32[]{:S(2)}) collective-permute-start(f32[72,128]{1,0:T(8,128)S(1)} %maximum_maximum_fusion.packed_ref), channel_id=1, source_target_pairs={{0,18},{1,19},{2,16},{3,17},{4,22},{5,23},{6,20},{7,21},{8,26},{9,... | collective-permute-start | bytes 110600 | tf_op jit(solution)/shard_map/ppermute | solution.py:68
  8.9 1.2 collective-permute-start.1
  10.8 6.8 %all-to-all-start = ((f32[16,8,128]{2,1,0:T(8,128)}), f32[16,8,128]{2,1,0:T(8,128)S(1)}, u32[]{:S(2)}, u32[]{:S(2)}) async-start(f32[16,8,128]{2,1,0:T(8,128)} %reshape_tile.3), calls=%async_computation | async-start | bytes 131072 | tf_op jit(solution)/shard_map/all_to_all | solution.py:79
  17.6 1.6 %collective-permute-start.4 = (f32[288,128]{1,0:T(8,128)S(1)}, f32[288,128]{1,0:T(8,128)S(1)}, u32[]{:S(2)}, u32[]{:S(2)}) collective-permute-start(f32[288,128]{1,0:T(8,128)S(1)} %pad_maximum_fusion.v_ref.right_near_ref), channel_id=1, source_target_pairs={{0,1},{1,0},{2,3},{3,2},{4,5},{5,4},{6,7},{7,6},{8,9},{9,8},{10,11... | collective-permute-start | bytes 442376 | tf_op jit(solution)/shard_map/ppermute | solution.py:68
  20.0 4.0 %all-to-all-done = f32[16,8,128]{2,1,0:T(8,128)S(1)} async-done(((f32[16,8,128]{2,1,0:T(8,128)}), f32[16,8,128]{2,1,0:T(8,128)S(1)}, u32[]{:S(2)}, u32[]{:S(2)}) %all-to-all-start) | async-done | bytes 65568 | tf_op jit(solution)/shard_map/all_to_all | solution.py:79
  24.0 2.4 %shard_map.50 = (f32[1024,128]{1,0:T(8,128)S(1)}, bf16[8,512,512]{2,1,0:T(8,128)(2,1)S(1)}) custom-call(f32[288,128]{1,0:T(8,128)S(1)} %pad_maximum_fusion.v_ref.right_near_ref, f32[128,128]{1,0:T(8,128)S(1)} %bitcast.25), custom_call_target="tpu_custom_call" | custom-call | flops 3221225472 | tf_op jit(solution)/shard_map/pallas_call | solution.py:201
  26.5 2.4 %shard_map.51 = (f32[1024,128]{1,0:T(8,128)S(1)}, bf16[8,512,512]{2,1,0:T(8,128)(2,1)S(1)}) custom-call(f32[288,128]{1,0:T(8,128)S(1)} %collective-permute-done.4.v_ref.right_near_ref, f32[128,128]{1,0:T(8,128)S(1)} %bitcast.26, f32[1024,128]{1,0:T(8,128)S(1)} %get-tuple-element.18.refs_0_), custom_call_target="tpu_custom_call" | custom-call | flops 3221225472 | tf_op jit(solution)/shard_map/pallas_call | solution.py:201
  29.0 2.9 %collective-permute-start.5 = (f32[288,128]{1,0:T(8,128)S(1)}, f32[288,128]{1,0:T(8,128)S(1)}, u32[]{:S(2)}, u32[]{:S(2)}) collective-permute-start(f32[288,128]{1,0:T(8,128)S(1)} %collective-permute-done.3.v_ref.right_far_ref), channel_id=1, source_target_pairs={{0,1},{1,0},{2,3},{3,2},{4,5},{5,4},{6,7},{7,6},{8,9},{9,8},{10,11... | collective-permute-start | bytes 442376 | tf_op jit(solution)/shard_map/ppermute | solution.py:68
  31.9 2.4 %shard_map.52 = (f32[1024,128]{1,0:T(8,128)S(1)}, bf16[8,512,512]{2,1,0:T(8,128)(2,1)S(1)}) custom-call(f32[288,128]{1,0:T(8,128)S(1)} %collective-permute-done.3.v_ref.right_far_ref, f32[128,128]{1,0:T(8,128)S(1)} %bitcast.27, f32[1024,128]{1,0:T(8,128)S(1)} %get-tuple-element.21.refs_0_), custom_call_target="tpu_custom_call" | custom-call | flops 3221225472 | tf_op jit(solution)/shard_map/pallas_call | solution.py:201
  34.4 2.5 %shard_map.53 = (f32[1024,128]{1,0:T(8,128)S(1)}, bf16[8,512,512]{2,1,0:T(8,128)(2,1)S(1)}) custom-call(f32[288,128]{1,0:T(8,128)S(1)} %collective-permute-done.5.v_ref.right_far_ref, f32[128,128]{1,0:T(8,128)S(1)} %bitcast.28, f32[1024,128]{1,0:T(8,128)S(1)} %get-tuple-element.22.refs_0_), custom_call_target="tpu_custom_call" | custom-call | flops 3221225472 | tf_op jit(solution)/shard_map/pallas_call | solution.py:201
  36.8 13.9 %all_to_all.40 = f32[16,64,128]{2,1,0:T(8,128)S(1)} all-to-all(f32[16,64,128]{2,1,0:T(8,128)S(1)} %bitcast.24), channel_id=1, replica_groups={{0,4,8,12,64,68,72,76,128,132,136,140,192,196,200,204},{1,5,9,13,65,69,..., dimensions={0} | all-to-all | bytes 1048576 | tf_op jit(solution)/shard_map/all_to_all | solution.py:79
  50.8 12.9 %all_to_all.41 = f32[8,64,128]{2,1,0:T(8,128)S(1)} all-to-all(f32[8,64,128]{2,1,0:T(8,128)S(1)} %bitcast.12), channel_id=1, replica_groups={{0,2,32,34,16,18,48,50},{1,3,33,35,17,19,49,51},{4,6,36,38,20,22,52,54}..., dimensions={0} | all-to-all | bytes 524288 | tf_op jit(solution)/shard_map/all_to_all | solution.py:79
  63.7 3.2 %collective-permute-start.6 = (f32[512,128]{1,0:T(8,128)S(1)}, f32[512,128]{1,0:T(8,128)S(1)}, u32[]{:S(2)}, u32[]{:S(2)}) collective-permute-start(f32[512,128]{1,0:T(8,128)S(1)} %bitcast.15), channel_id=1, source_target_pairs={{0,1},{1,0},{2,3},{3,2},{4,5},{5,4},{6,7},{7,6},{8,9},{9,8},{10,11... | collective-permute-start | bytes 786440 | tf_op jit(solution)/shard_map/ppermute | solution.py:68
  66.9 1.3 shard_map.55.refs_0_
  68.2 1.3 shard_map.56
  69.6 14.3 %all_to_all.42 = f32[16,72,128]{2,1,0:T(8,128)S(1)} all-to-all(f32[16,72,128]{2,1,0:T(8,128)S(1)} %bitcast.14), channel_id=1, replica_groups={{0,4,8,12,64,68,72,76,128,132,136,140,192,196,200,204},{1,5,9,13,65,69,..., dimensions={0} | all-to-all | bytes 1179648 | tf_op jit(solution)/shard_map/all_to_all | solution.py:79
  84.0 11.3 %all_to_all.43 = f32[8,64,128]{2,1,0:T(8,128)S(1)} all-to-all(f32[8,64,128]{2,1,0:T(8,128)S(1)} %bitcast.23), channel_id=1, replica_groups={{0,2,32,34,16,18,48,50},{1,3,33,35,17,19,49,51},{4,6,36,38,20,22,52,54}..., dimensions={0} | all-to-all | bytes 524288 | tf_op jit(solution)/shard_map/all_to_all | solution.py:79
  95.3 3.3 %collective-permute-start.7 = (f32[512,128]{1,0:T(8,128)S(1)}, f32[512,128]{1,0:T(8,128)S(1)}, u32[]{:S(2)}, u32[]{:S(2)}) collective-permute-start(f32[512,128]{1,0:T(8,128)S(1)} %bitcast.21), channel_id=1, source_target_pairs={{0,1},{1,0},{2,3},{3,2},{4,5},{5,4},{6,7},{7,6},{8,9},{9,8},{10,11... | collective-permute-start | bytes 786440 | tf_op jit(solution)/shard_map/ppermute | solution.py:68
  98.6 1.3 shard_map.58.refs_2_
  99.9 1.3 shard_map.59
  101.2 14.5 %all_to_all.44 = f32[16,72,128]{2,1,0:T(8,128)S(1)} all-to-all(f32[16,72,128]{2,1,0:T(8,128)S(1)} %bitcast.13), channel_id=1, replica_groups={{0,4,8,12,64,68,72,76,128,132,136,140,192,196,200,204},{1,5,9,13,65,69,..., dimensions={0} | all-to-all | bytes 1179648 | tf_op jit(solution)/shard_map/all_to_all | solution.py:79
  116.0 1.7 %collective-permute-start.8 = (f32[8,128]{1,0:T(8,128)S(1)}, f32[8,128]{1,0:T(8,128)S(1)}, u32[]{:S(2)}, u32[]{:S(2)}) collective-permute-start(f32[8,128]{1,0:T(8,128)S(1)} %get-tuple-element.31), channel_id=1, source_target_pairs={{0,1},{1,0},{2,3},{3,2},{4,5},{5,4},{6,7},{7,6},{8,9},{9,8},{10,11... | collective-permute-start | bytes 12296 | tf_op jit(solution)/shard_map/ppermute | solution.py:68
  118.6 9.4 %all_to_all.45 = f32[16,8,128]{2,1,0:T(8,128)S(1)} all-to-all(f32[16,8,128]{2,1,0:T(8,128)S(1)} %broadcast_in_dim.20), channel_id=1, replica_groups={{0,4,8,12,64,68,72,76,128,132,136,140,192,196,200,204},{1,5,9,13,65,69,..., dimensions={0} | all-to-all | bytes 131072 | tf_op jit(solution)/shard_map/all_to_all | solution.py:89
  128.0 10.5 %all_to_all.46 = f32[8,8,128]{2,1,0:T(8,128)S(1)} all-to-all(f32[8,8,128]{2,1,0:T(8,128)S(1)} %broadcast_in_dim.21), channel_id=1, replica_groups={{0,2,32,34,16,18,48,50},{1,3,33,35,17,19,49,51},{4,6,36,38,20,22,52,54}..., dimensions={0} | all-to-all | bytes 65536 | tf_op jit(solution)/shard_map/all_to_all | solution.py:89
  (26 shorter events, 4.4 us)
Async XLA Ops:
  1.6 15.9 %collective-permute-start.2 = (f32[72,128]{1,0:T(8,128)S(1)}, f32[72,128]{1,0:T(8,128)S(1)}, u32[]{:S(2)}, u32[]{:S(2)}) collective-permute-start(f32[72,128]{1,0:T(8,128)S(1)} %maximum_maximum_fusion.packed_ref), channel_id=1, source_target_pairs={{0,18},{1,19},{2,16},{3,17},{4,22},{5,23},{6,20},{7,21},{8,26},{9,... | collective-permute-start | bytes 110600 | tf_op jit(solution)/shard_map/ppermute | solution.py:68
  8.9 8.6 %collective-permute-start.1 = (f32[72,128]{1,0:T(8,128)S(1)}, f32[72,128]{1,0:T(8,128)S(1)}, u32[]{:S(2)}, u32[]{:S(2)}) collective-permute-start(f32[72,128]{1,0:T(8,128)S(1)} %maximum_maximum_fusion.packed_ref), channel_id=1, source_target_pairs={{0,32},{1,33},{2,34},{3,35},{4,36},{5,37},{6,38},{7,39},{8,40},{9,... | collective-permute-start | bytes 110600 | tf_op jit(solution)/shard_map/ppermute | solution.py:68
  10.1 7.4 %collective-permute-start = (f32[72,128]{1,0:T(8,128)S(1)}, f32[72,128]{1,0:T(8,128)S(1)}, u32[]{:S(2)}, u32[]{:S(2)}) collective-permute-start(f32[72,128]{1,0:T(8,128)S(1)} %maximum_maximum_fusion.packed_ref), channel_id=1, source_target_pairs={{0,50},{1,51},{2,48},{3,49},{4,54},{5,55},{6,52},{7,53},{8,58},{9,... | collective-permute-start | bytes 110600 | tf_op jit(solution)/shard_map/ppermute | solution.py:68
  10.8 13.3 %all-to-all-start = ((f32[16,8,128]{2,1,0:T(8,128)}), f32[16,8,128]{2,1,0:T(8,128)S(1)}, u32[]{:S(2)}, u32[]{:S(2)}) async-start(f32[16,8,128]{2,1,0:T(8,128)} %reshape_tile.3), calls=%async_computation | async-start | bytes 131072 | tf_op jit(solution)/shard_map/all_to_all | solution.py:79
  17.6 8.9 %collective-permute-start.4 = (f32[288,128]{1,0:T(8,128)S(1)}, f32[288,128]{1,0:T(8,128)S(1)}, u32[]{:S(2)}, u32[]{:S(2)}) collective-permute-start(f32[288,128]{1,0:T(8,128)S(1)} %pad_maximum_fusion.v_ref.right_near_ref), channel_id=1, source_target_pairs={{0,1},{1,0},{2,3},{3,2},{4,5},{5,4},{6,7},{7,6},{8,9},{9,8},{10,11... | collective-permute-start | bytes 442376 | tf_op jit(solution)/shard_map/ppermute | solution.py:68
  19.2 9.8 %collective-permute-start.3 = (f32[288,128]{1,0:T(8,128)S(1)}, f32[288,128]{1,0:T(8,128)S(1)}, u32[]{:S(2)}, u32[]{:S(2)}) collective-permute-start(f32[288,128]{1,0:T(8,128)S(1)} %pad_maximum_fusion.v_ref.right_near_ref), channel_id=1, source_target_pairs={{0,16},{1,17},{2,18},{3,19},{4,20},{5,21},{6,22},{7,23},{8,24},{9,... | collective-permute-start | bytes 442376 | tf_op jit(solution)/shard_map/ppermute | solution.py:68
  29.0 5.4 %collective-permute-start.5 = (f32[288,128]{1,0:T(8,128)S(1)}, f32[288,128]{1,0:T(8,128)S(1)}, u32[]{:S(2)}, u32[]{:S(2)}) collective-permute-start(f32[288,128]{1,0:T(8,128)S(1)} %collective-permute-done.3.v_ref.right_far_ref), channel_id=1, source_target_pairs={{0,1},{1,0},{2,3},{3,2},{4,5},{5,4},{6,7},{7,6},{8,9},{9,8},{10,11... | collective-permute-start | bytes 442376 | tf_op jit(solution)/shard_map/ppermute | solution.py:68
  63.7 4.5 %collective-permute-start.6 = (f32[512,128]{1,0:T(8,128)S(1)}, f32[512,128]{1,0:T(8,128)S(1)}, u32[]{:S(2)}, u32[]{:S(2)}) collective-permute-start(f32[512,128]{1,0:T(8,128)S(1)} %bitcast.15), channel_id=1, source_target_pairs={{0,1},{1,0},{2,3},{3,2},{4,5},{5,4},{6,7},{7,6},{8,9},{9,8},{10,11... | collective-permute-start | bytes 786440 | tf_op jit(solution)/shard_map/ppermute | solution.py:68
  95.3 4.6 %collective-permute-start.7 = (f32[512,128]{1,0:T(8,128)S(1)}, f32[512,128]{1,0:T(8,128)S(1)}, u32[]{:S(2)}, u32[]{:S(2)}) collective-permute-start(f32[512,128]{1,0:T(8,128)S(1)} %bitcast.21), channel_id=1, source_target_pairs={{0,1},{1,0},{2,3},{3,2},{4,5},{5,4},{6,7},{7,6},{8,9},{9,8},{10,11... | collective-permute-start | bytes 786440 | tf_op jit(solution)/shard_map/ppermute | solution.py:68
  116.0 2.5 %collective-permute-start.8 = (f32[8,128]{1,0:T(8,128)S(1)}, f32[8,128]{1,0:T(8,128)S(1)}, u32[]{:S(2)}, u32[]{:S(2)}) collective-permute-start(f32[8,128]{1,0:T(8,128)S(1)} %get-tuple-element.31), channel_id=1, source_target_pairs={{0,1},{1,0},{2,3},{3,2},{4,5},{5,4},{6,7},{7,6},{8,9},{9,8},{10,11... | collective-permute-start | bytes 12296 | tf_op jit(solution)/shard_map/ppermute | solution.py:68
